TPU v7x, 512 devices: a whole 4x8x8 slice. The times are simulated.
512 devices in a mesh: scene: 8 (over y), space: 64 (over x, z, core).
Axes of the slice: x: 4, y: 8, z: 8, core: 2. Of those that a mesh axis runs over, the one named last changes fastest.
Arguments:
- features: bfloat16 [8, 256, 64, 128], P('scene', 'space'), may hold values from -40 to 40, as said below
- active: int32 [8, 256], P('scene', 'space'), may hold values from 0 to 1, as said below
- neighbor_owner: int32 [8, 256, 26], P('scene', 'space'), may hold values from -1 to 63, as said below
- record_position: int32 [8, 256, 26], P('scene', 'space'), may hold values from 0 to 9, as said below
- send_list: int32 [8, 64, 64, 10], P('scene', 'space'), may hold values from -1 to 23, as said below
- conv_first: bfloat16 [27, 128, 128], replicated, may hold values from -0.109375 to 0.109375
- conv_second: bfloat16 [27, 128, 128], replicated, may hold values from -0.109375 to 0.109375
- gain_first: float32 [128], replicated, may hold values from 0.4 to 1.6
- bias_first: float32 [128], replicated, may hold values from -3 to 3
- gain_second: float32 [128], replicated, may hold values from 0.4 to 1.6
- bias_second: float32 [128], replicated, may hold values from -3 to 3
- grad_output: bfloat16 [8, 256, 64, 128], P('scene', 'space'), may hold values from -6 to 6, as said below
Outputs:
- block_output: bfloat16 [8, 256, 64, 128], P('scene', 'space')
- grad_input: bfloat16 [8, 256, 64, 128], P('scene', 'space')
- grad_conv_first: bfloat16 [3456, 128], P('space')
- grad_conv_second: bfloat16 [3456, 128], P('space')
Inputs may be any that keep to these rules, and one draw needn't show every extreme that they name: `features`: finite values. `grad_output`: finite values. Each device's active bricks fill its first slots; in every scene some device has all 4 slots active. `neighbor_owner`: -1 where a slot is inactive or its neighbour in that direction is absent; otherwise the neighbour is an active brick whose owner's index differs from the slot's own device by 0, 1, 3, 4 or 5 in either direction, and adjacency is mutual with the opposite direction. `record_position`: 0 where there is no neighbour; the records from one owner to one device are numbered from 0 without gaps. send_list[s, p, k] = slot * 6 + face of the plane that device s sends as record k to device p within a scene, -1 for unused entries; each list holds at most 10 records and some list holds exactly 10 in every scene.
All inputs are finite; a program needn't handle non-finite values.
Results may differ from a plain program's by a relative error of at most 0.0051.
Values may be sent and summed in bfloat16 or wider, within the bound.
No kernel may reach another device: no remote copies, remote signals or barrier semaphores. Data moves between devices by JAX's collectives and lax.ppermute only.
A program may use at most 128 MiB of HBM per device.

v0:
```python
import jax
import jax.numpy as jnp
from jax import lax
from jax.sharding import PartitionSpec as P

GROUPS = 32
EDGE = 4
ROW_SPAN = 4


directions = [
    (ordinal // 9 - 1, ordinal // 3 % 3 - 1, ordinal % 3 - 1)
    for ordinal in range(27)
    if ordinal != 13
]
norm_eps = 1e-05


def shifted_2(value, axis, steps):
    count = lax.axis_size(axis)
    leading, last = (max(0, -steps), min(count, count - steps))
    return lax.ppermute(value, axis, [(source, source + steps) for source in range(leading, last)])


def leading_axis(direction):
    for dimension in range(3):
        if direction[dimension] != 0:
            return dimension
    return 0


def end_planes(brick_field, brick_edge):
    slot_count, channels = (brick_field.shape[0], brick_field.shape[2])
    brick_cube = brick_field.reshape(slot_count, brick_edge, brick_edge, brick_edge, channels)
    layers = [
        brick_cube[:, 0],
        brick_cube[:, -1],
        brick_cube[:, :, 0],
        brick_cube[:, :, -1],
        brick_cube[:, :, :, 0],
        brick_cube[:, :, :, -1],
    ]
    return jnp.stack(layers, axis=1).reshape(slot_count * 6, brick_edge * brick_edge, channels)


def place_record(padded, record, direction, brick_edge):
    leading = leading_axis(direction)
    record = record.reshape(record.shape[0], brick_edge, brick_edge, record.shape[-1])
    source = [slice(None)]
    for dimension in range(3):
        if dimension == leading:
            continue
        if direction[dimension] == 0:
            source.append(slice(None))
        elif direction[dimension] > 0:
            source.append(slice(0, 1))
        else:
            source.append(slice(brick_edge - 1, brick_edge))
    source.append(slice(None))
    slab_piece = jnp.expand_dims(record[tuple(source)], leading + 1)
    target = [slice(None)]
    for dimension in range(3):
        if direction[dimension] == 0:
            target.append(slice(1, brick_edge + 1))
        elif direction[dimension] > 0:
            target.append(slice(brick_edge + 1, brick_edge + 2))
        else:
            target.append(slice(0, 1))
    target.append(slice(None))
    return padded.at[tuple(target)].set(slab_piece)


def surround(brick_field, records, owners, brick_edge):
    slot_count, channels = (brick_field.shape[0], brick_field.shape[2])
    wide_edge = brick_edge + 2
    padded = jnp.zeros((slot_count, wide_edge, wide_edge, wide_edge, channels), brick_field.dtype)
    inner = brick_field.reshape(slot_count, brick_edge, brick_edge, brick_edge, channels)
    padded = padded.at[:, 1 : brick_edge + 1, 1 : brick_edge + 1, 1 : brick_edge + 1].set(inner)
    for number, direction in enumerate(directions):
        picked = records[:, number]
        picked = jnp.where((owners[:, number] >= 0)[:, None, None], picked, jnp.zeros_like(picked))
        padded = place_record(padded, picked, direction, brick_edge)
    return padded


def unfold(padded, brick_edge, flipped):
    slot_count, channels = (padded.shape[0], padded.shape[-1])
    columns = []
    for ordinal in range(27):
        offset_x, offset_y, offset_z = (ordinal // 9, ordinal // 3 % 3, ordinal % 3)
        if flipped:
            offset_x, offset_y, offset_z = (2 - offset_x, 2 - offset_y, 2 - offset_z)
        window = padded[
            :,
            offset_x : offset_x + brick_edge,
            offset_y : offset_y + brick_edge,
            offset_z : offset_z + brick_edge,
        ]
        columns.append(window.reshape(slot_count * brick_edge**3, channels))
    return jnp.concatenate(columns, axis=1)


def group_sums(values):
    per_channel = jnp.sum(values, axis=(0, 1))
    return per_channel.reshape(GROUPS, -1).sum(axis=1)


def halo_cube(brick_field, owners, positions, sendlist):
    own_index = lax.axis_index("space")
    peer_count = lax.axis_size("space")
    capacity = sendlist.shape[-1]
    planes = end_planes(brick_field, EDGE)
    safe_list = jnp.maximum(sendlist, 0)
    offsets = [1, -1, ROW_SPAN - 1, 1 - ROW_SPAN, ROW_SPAN, -ROW_SPAN, ROW_SPAN + 1, -ROW_SPAN - 1]
    own_row = lax.dynamic_index_in_dim(safe_list, own_index, 0, keepdims=False)
    blocks = [planes[own_row]]
    distance = owners - own_index
    source_lane = jnp.zeros_like(owners)
    for number, offset in enumerate(offsets):
        target = jnp.clip(own_index + offset, 0, peer_count - 1)
        outgoing = planes[lax.dynamic_index_in_dim(safe_list, target, 0, keepdims=False)]
        blocks.append(shifted_2(outgoing, "space", offset))
        source_lane = jnp.where(distance == -offset, number + 1, source_lane)
    received_table = jnp.concatenate(blocks, axis=0)
    table_rows = source_lane * capacity + positions
    records = received_table[table_rows]
    return surround(brick_field, records, owners, EDGE)


def norm_forward(values, weight, gain_row, bias_row):
    per_group = values.shape[2] // GROUPS
    masked = values * weight[:, None, None]
    group_total, squares, count = lax.psum(
        (
            group_sums(masked),
            group_sums(masked * values),
            jnp.sum(weight) * (values.shape[1] * per_group),
        ),
        "space",
    )
    group_mean = group_total / count
    inverse_std = lax.rsqrt(squares / count - group_mean * group_mean + norm_eps)
    channel_inv = jnp.repeat(inverse_std, per_group)
    centred = (values - jnp.repeat(group_mean, per_group)) * channel_inv
    shifted = centred * gain_row + bias_row
    return (centred, shifted, channel_inv, count)


def norm_backward(grad_act, centred, shifted, channel_inv, gain_row, weight, count):
    per_group = centred.shape[2] // GROUPS
    sigmoid_value = jax.nn.sigmoid(shifted)
    grad_centred = (
        grad_act
        * weight[:, None, None]
        * sigmoid_value
        * (1.0 + shifted * (1.0 - sigmoid_value))
        * gain_row
    )
    sum_grad, sum_cross = lax.psum(
        (group_sums(grad_centred), group_sums(grad_centred * centred)), "space"
    )
    sum_grad = sum_grad / count
    sum_cross = sum_cross / count
    return (
        weight[:, None, None]
        * channel_inv
        * (
            grad_centred
            - jnp.repeat(sum_grad, per_group)
            - centred * jnp.repeat(sum_cross, per_group)
        )
    )


def per_device(
    features,
    active,
    neighbor_owner,
    record_position,
    send_list,
    conv_first,
    conv_second,
    gain_first,
    bias_first,
    gain_second,
    bias_second,
    grad_output,
):
    inputs = features[0]
    slot_count, voxels, channels = inputs.shape
    weight = active[0].astype(jnp.float32)
    owners = neighbor_owner[0]
    positions = record_position[0]
    sendlist = send_list[0, 0]
    weight_first = conv_first.reshape(27 * channels, channels)
    weight_second = conv_second.reshape(27 * channels, channels)
    back_first = jnp.transpose(conv_first, (0, 2, 1)).reshape(27 * channels, channels)
    back_second = jnp.transpose(conv_second, (0, 2, 1)).reshape(27 * channels, channels)
    input_wide = inputs.astype(jnp.float32)
    centred_a, shifted_a, inv_a, count_a = norm_forward(input_wide, weight, gain_first, bias_first)
    act_first = (jax.nn.silu(shifted_a) * weight[:, None, None]).astype(jnp.bfloat16)
    cols_first = unfold(halo_cube(act_first, owners, positions, sendlist), EDGE, False)
    middle = jnp.dot(cols_first, weight_first, preferred_element_type=jnp.float32).reshape(
        slot_count, voxels, channels
    )
    centred_b, shifted_b, inv_b, count_b = norm_forward(middle, weight, gain_second, bias_second)
    act_second = (jax.nn.silu(shifted_b) * weight[:, None, None]).astype(jnp.bfloat16)
    cols_second = unfold(halo_cube(act_second, owners, positions, sendlist), EDGE, False)
    conv_out = jnp.dot(cols_second, weight_second, preferred_element_type=jnp.float32).reshape(
        slot_count, voxels, channels
    )
    block_output = ((input_wide + conv_out) * weight[:, None, None]).astype(jnp.bfloat16)
    cotangent = grad_output[0]
    grad_top = jnp.where(weight[:, None, None] > 0.0, cotangent, jnp.zeros_like(cotangent))
    grad_flat = grad_top.reshape(slot_count * voxels, channels)
    grad_second_w = lax.dot_general(
        cols_second, grad_flat, (((0,), (0,)), ((), ())), preferred_element_type=jnp.float32
    )
    cols_grad = unfold(halo_cube(grad_top, owners, positions, sendlist), EDGE, True)
    grad_act_second = jnp.dot(cols_grad, back_second, preferred_element_type=jnp.float32).reshape(
        slot_count, voxels, channels
    )
    grad_middle = norm_backward(
        grad_act_second, centred_b, shifted_b, inv_b, gain_second, weight, count_b
    ).astype(jnp.bfloat16)
    grad_first_w = lax.dot_general(
        cols_first,
        grad_middle.reshape(slot_count * voxels, channels),
        (((0,), (0,)), ((), ())),
        preferred_element_type=jnp.float32,
    )
    cols_middle = unfold(halo_cube(grad_middle, owners, positions, sendlist), EDGE, True)
    grad_act_first = jnp.dot(cols_middle, back_first, preferred_element_type=jnp.float32).reshape(
        slot_count, voxels, channels
    )
    grad_input = (
        grad_top.astype(jnp.float32)
        + norm_backward(grad_act_first, centred_a, shifted_a, inv_a, gain_first, weight, count_a)
    ).astype(jnp.bfloat16)
    total_first, total_second = lax.psum((grad_first_w, grad_second_w), ("scene", "space"))
    rows_share = total_first.shape[0] // lax.axis_size("space")
    row_start = lax.axis_index("space") * rows_share
    rows_first = lax.dynamic_slice_in_dim(total_first, row_start, rows_share, 0)
    rows_second = lax.dynamic_slice_in_dim(total_second, row_start, rows_share, 0)
    return (
        block_output[None],
        grad_input[None],
        rows_first.astype(jnp.bfloat16),
        rows_second.astype(jnp.bfloat16),
    )


def solution(mesh):
    return jax.shard_map(
        per_device,
        mesh=mesh,
        in_specs=(
            P("scene", "space", None, None),
            P("scene", "space"),
            P("scene", "space", None),
            P("scene", "space", None),
            P("scene", "space", None, None),
            P(),
            P(),
            P(),
            P(),
            P(),
            P(),
            P("scene", "space", None, None),
        ),
        out_specs=(
            P("scene", "space", None, None),
            P("scene", "space", None, None),
            P("space", None),
            P("space", None),
        ),
        check_vma=False,
    )
```

profile of v0, /device:TPU:2, one launch (start us, length us, event | category | flops | bytes accessed | tf_op | source)
XLA Modules:
  0.0 961.7 jit_solution(7818189182278570854)
XLA Ops:
  3.1 1.8 dynamic-slice_reduce_fusion
  5.6 1.9 collective-permute-start.16
  8.1 10.4 %collective-permute-start.17 = (bf16[10,16,128]{2,1,0:T(8,128)(2,1)S(1)}, bf16[10,16,128]{2,1,0:T(8,128)(2,1)}, u32[]{:S(2)}, u32[]{:S(2)}) collective-permute-start(bf16[10,16,128]{2,1,0:T(8,128)(2,1)S(1)} %gather_fusion.22), channel_id=1, source_target_pairs={{1,0},{2,1},{3,2},{4,3},{5,4},{6,5},{7,6},{8,7},{9,8},{10,9},{11,1... | collective-permute-start | bytes 122888 | tf_op jit(solution)/shard_map/ppermute | solution.py:22
  19.1 2.1 collective-permute-start.18
  21.7 6.7 collective-permute-start.19
  29.0 1.9 collective-permute-start.20
  35.8 105.5 %all-reduce.8 = (f32[32]{0:T(128)S(1)}, f32[]{:T(128)}, f32[32]{0:T(128)S(1)}) all-reduce(f32[32]{0:T(128)S(1)} %reduce_sum.158, f32[]{:T(128)S(6)} %mul.245, f32[32]{0:T(128)S(1)} %reduce_sum.161), channel_id=1, replica_groups=mesh['scene'=8,'space'=64] {'space'}, use_global_device_ids=true, to_apply=%region_2.0 | all-reduce | flops 65 | bytes 520 | tf_op jit(solution)/shard_map/psum | solution.py:133
  161.2 1.7 copy.1119
  164.3 1.9 collective-permute-start.21
  167.6 3.7 collective-permute-start.22
  172.7 6.6 collective-permute-start.23
  180.7 1.9 collective-permute-start
  184.0 6.0 collective-permute-start.1
  191.5 1.9 collective-permute-start.2
  194.0 8.5 collective-permute-start.3
  203.1 1.9 collective-permute-start.4
  205.7 1.7 gather_fusion.29
  208.7 10.8 %collective-permute-start.5 = (bf16[10,16,128]{2,1,0:T(8,128)(2,1)S(1)}, bf16[10,16,128]{2,1,0:T(8,128)(2,1)S(1)}, u32[]{:S(2)}, u32[]{:S(2)}) collective-permute-start(bf16[10,16,128]{2,1,0:T(8,128)(2,1)S(1)} %copy-done.112), channel_id=1, source_target_pairs={{4,0},{5,1},{6,2},{7,3},{8,4},{9,5},{10,6},{11,7},{12,8},{13,9},{1... | collective-permute-start | bytes 122888 | tf_op jit(solution)/shard_map/ppermute | solution.py:22
  219.5 1.9 collective-permute-start.6
  221.5 7.5 collective-permute-start.7
  284.6 106.8 %all-reduce.7 = (f32[32]{0:T(128)S(1)}, f32[32]{0:T(128)S(1)}) all-reduce(f32[32]{0:T(128)S(1)} %reduce_sum.163, f32[32]{0:T(128)S(1)} %reduce_sum.165), channel_id=1, replica_groups=mesh['scene'=8,'space'=64] {'space'}, use_global_device_ids=true, to_apply=%region_10.11 | all-reduce | flops 64 | bytes 512 | tf_op jit(solution)/shard_map/psum | solution.py:133
  405.1 109.3 %all-reduce.6 = (f32[32]{0:T(128)S(1)}, f32[32]{0:T(128)S(1)}) all-reduce(f32[32]{0:T(128)S(1)} %reduce_sum.169, f32[32]{0:T(128)S(1)} %reduce_sum.167), channel_id=1, replica_groups=mesh['scene'=8,'space'=64] {'space'}, use_global_device_ids=true, to_apply=%region_19.20 | all-reduce | flops 64 | bytes 512 | tf_op jit(solution)/shard_map/psum | solution.py:159
  539.6 1.9 collective-permute-start.24
  541.5 7.0 collective-permute-start.25
  548.5 1.9 collective-permute-start.26
  550.4 7.6 collective-permute-start.27
  558.0 1.9 collective-permute-start.28
  561.6 12.5 %collective-permute-start.29 = (bf16[10,16,128]{2,1,0:T(8,128)(2,1)S(1)}, bf16[10,16,128]{2,1,0:T(8,128)(2,1)S(1)}, u32[]{:S(2)}, u32[]{:S(2)}) collective-permute-start(bf16[10,16,128]{2,1,0:T(8,128)(2,1)S(1)} %copy-done.111), channel_id=1, source_target_pairs={{4,0},{5,1},{6,2},{7,3},{8,4},{9,5},{10,6},{11,7},{12,8},{13,9},{1... | collective-permute-start | bytes 122888 | tf_op jit(solution)/shard_map/ppermute | solution.py:22
  574.1 1.9 collective-permute-start.30
  576.1 16.9 %collective-permute-start.31 = (bf16[10,16,128]{2,1,0:T(8,128)(2,1)S(1)}, bf16[10,16,128]{2,1,0:T(8,128)(2,1)S(1)}, u32[]{:S(2)}, u32[]{:S(2)}) collective-permute-start(bf16[10,16,128]{2,1,0:T(8,128)(2,1)S(1)} %copy-done.109), channel_id=1, source_target_pairs={{5,0},{6,1},{7,2},{8,3},{9,4},{10,5},{11,6},{12,7},{13,8},{14,9},{... | collective-permute-start | bytes 122888 | tf_op jit(solution)/shard_map/ppermute | solution.py:22
  593.0 1.9 collective-permute-start.8
  595.0 5.8 collective-permute-start.9
  600.7 1.9 collective-permute-start.10
  602.7 6.7 collective-permute-start.11
  609.4 1.9 collective-permute-start.12
  613.3 6.9 collective-permute-start.13
  621.1 1.9 collective-permute-start.14
  623.8 7.5 collective-permute-start.15
  685.5 105.4 %all-reduce.5 = (f32[32]{0:T(128)S(1)}, f32[32]{0:T(128)S(1)}) all-reduce(f32[32]{0:T(128)S(1)} %reduce_sum.173, f32[32]{0:T(128)S(1)} %reduce_sum.171), channel_id=1, replica_groups=mesh['scene'=8,'space'=64] {'space'}, use_global_device_ids=true, to_apply=%region_25.26 | all-reduce | flops 64 | bytes 512 | tf_op jit(solution)/shard_map/psum | solution.py:159
  795.9 131.4 %all-reduce.10 = (bf16[3456,128]{1,0:T(8,128)(2,1)}, bf16[3456,128]{1,0:T(8,128)(2,1)}) all-reduce(f32[3456,128]{1,0:T(8,128)S(1)} %fusion.153, f32[3456,128]{1,0:T(8,128)S(1)} %fusion.154), channel_id=1, replica_groups=mesh['scene'=8,'space'=64] {'scene','space'}, use_global_device_ids=true, to_apply=%region_26.27 | all-reduce | flops 884736 | bytes 5308416 | tf_op jit(solution)/shard_map/psum | solution.py:240
  927.5 1.5 dynamic-slice_convert_fusion.1
  930.3 1.5 constant_dynamic-update-slice_fusion.82
  931.8 1.5 constant_dynamic-update-slice_fusion.81
  937.7 1.5 constant_dynamic-update-slice_fusion.77
  939.2 1.5 constant_dynamic-update-slice_fusion.76
  942.2 1.5 constant_dynamic-update-slice_fusion.74
  945.1 1.5 constant_dynamic-update-slice_fusion.72
  958.2 2.7 fusion.8
  (1118 shorter events, 215.9 us)
Async XLA Ops:
  0.6 142.6 %copy-start.3 = (s32[1,4,26]{2,1,0:T(4,128)S(1)}, s32[1,4,26]{2,1,0:T(4,128)}, u32[]{:S(2)}) copy-start(s32[1,4,26]{2,1,0:T(4,128)} %param.230) | copy-start | bytes 1252
  0.6 145.8 %copy-start.191 = (s32[1,4,26]{2,1,0:T(4,128)S(1)}, s32[1,4,26]{2,1,0:T(4,128)}, u32[]{:S(2)}) copy-start(s32[1,4,26]{2,1,0:T(4,128)} %param.231) | copy-start | bytes 1252
  4.9 154.8 %copy-start.150 = (s32[1024]{0:T(1024)}, s32[1024]{0:T(1024)S(1)}, u32[]{:S(2)}) copy-start(s32[1024]{0:T(1024)S(1)} %pad_clamp_fusion.8) | copy-start | bytes 12292
  5.6 158.7 %collective-permute-start.16 = (bf16[10,16,128]{2,1,0:T(8,128)(2,1)S(1)}, bf16[10,16,128]{2,1,0:T(8,128)(2,1)}, u32[]{:S(2)}, u32[]{:S(2)}) collective-permute-start(bf16[10,16,128]{2,1,0:T(8,128)(2,1)S(1)} %gather_fusion.21), channel_id=1, source_target_pairs={{0,1},{1,2},{2,3},{3,4},{4,5},{5,6},{6,7},{7,8},{8,9},{9,10},{10,1... | collective-permute-start | bytes 122888 | tf_op jit(solution)/shard_map/ppermute | solution.py:22
  7.5 152.3 %copy-start.151 = (s32[1024]{0:T(1024)}, s32[1024]{0:T(1024)S(1)}, u32[]{:S(2)}) copy-start(s32[1024]{0:T(1024)S(1)} %pad_clamp_fusion.7) | copy-start | bytes 12292
  8.1 159.5 %collective-permute-start.17 = (bf16[10,16,128]{2,1,0:T(8,128)(2,1)S(1)}, bf16[10,16,128]{2,1,0:T(8,128)(2,1)}, u32[]{:S(2)}, u32[]{:S(2)}) collective-permute-start(bf16[10,16,128]{2,1,0:T(8,128)(2,1)S(1)} %gather_fusion.22), channel_id=1, source_target_pairs={{1,0},{2,1},{3,2},{4,3},{5,4},{6,5},{7,6},{8,7},{9,8},{10,9},{11,1... | collective-permute-start | bytes 122888 | tf_op jit(solution)/shard_map/ppermute | solution.py:22
  18.5 141.3 %copy-start.152 = (s32[1024]{0:T(1024)}, s32[1024]{0:T(1024)S(1)}, u32[]{:S(2)}) copy-start(s32[1024]{0:T(1024)S(1)} %pad_clamp_fusion.6) | copy-start | bytes 12292
  19.1 140.7 %copy-start.1 = (bf16[27,128,128]{2,1,0:T(8,128)(2,1)S(1)}, bf16[27,128,128]{2,1,0:T(8,128)(2,1)}, u32[]{:S(2)}) copy-start(bf16[27,128,128]{2,1,0:T(8,128)(2,1)} %param.234) | copy-start | bytes 2654212
  19.1 153.6 %collective-permute-start.18 = (bf16[10,16,128]{2,1,0:T(8,128)(2,1)S(1)}, bf16[10,16,128]{2,1,0:T(8,128)(2,1)}, u32[]{:S(2)}, u32[]{:S(2)}) collective-permute-start(bf16[10,16,128]{2,1,0:T(8,128)(2,1)S(1)} %gather_fusion.23), channel_id=1, source_target_pairs={{0,3},{1,4},{2,5},{3,6},{4,7},{5,8},{6,9},{7,10},{8,11},{9,12},{10... | collective-permute-start | bytes 122888 | tf_op jit(solution)/shard_map/ppermute | solution.py:22
  21.2 140.0 %copy-start.153 = (s32[1024]{0:T(1024)}, s32[1024]{0:T(1024)S(1)}, u32[]{:S(2)}) copy-start(s32[1024]{0:T(1024)S(1)} %pad_clamp_fusion.5) | copy-start | bytes 12292
  21.7 159.0 %collective-permute-start.19 = (bf16[10,16,128]{2,1,0:T(8,128)(2,1)S(1)}, bf16[10,16,128]{2,1,0:T(8,128)(2,1)}, u32[]{:S(2)}, u32[]{:S(2)}) collective-permute-start(bf16[10,16,128]{2,1,0:T(8,128)(2,1)S(1)} %gather_fusion.24), channel_id=1, source_target_pairs={{3,0},{4,1},{5,2},{6,3},{7,4},{8,5},{9,6},{10,7},{11,8},{12,9},{13... | collective-permute-start | bytes 122888 | tf_op jit(solution)/shard_map/ppermute | solution.py:22
  28.4 129.5 %copy-start.154 = (s32[1024]{0:T(1024)}, s32[1024]{0:T(1024)S(1)}, u32[]{:S(2)}) copy-start(s32[1024]{0:T(1024)S(1)} %pad_clamp_fusion.4) | copy-start | bytes 12292
  29.0 155.0 %collective-permute-start.20 = (bf16[10,16,128]{2,1,0:T(8,128)(2,1)S(1)}, bf16[10,16,128]{2,1,0:T(8,128)(2,1)}, u32[]{:S(2)}, u32[]{:S(2)}) collective-permute-start(bf16[10,16,128]{2,1,0:T(8,128)(2,1)S(1)} %gather_fusion.25), channel_id=1, source_target_pairs={{0,4},{1,5},{2,6},{3,7},{4,8},{5,9},{6,10},{7,11},{8,12},{9,13},{1... | collective-permute-start | bytes 122888 | tf_op jit(solution)/shard_map/ppermute | solution.py:22
  31.6 484.4 %copy-start.131 = (f32[4]{0:T(128)}, f32[4]{0:T(128)S(1)}, u32[]{:S(2)}) copy-start(f32[4]{0:T(128)S(1)} %convert_bitcast_fusion) | copy-start | bytes 52
  164.3 27.2 %collective-permute-start.21 = (bf16[10,16,128]{2,1,0:T(8,128)(2,1)S(1)}, bf16[10,16,128]{2,1,0:T(8,128)(2,1)S(1)}, u32[]{:S(2)}, u32[]{:S(2)}) collective-permute-start(bf16[10,16,128]{2,1,0:T(8,128)(2,1)S(1)} %copy-done.115), channel_id=1, source_target_pairs={{4,0},{5,1},{6,2},{7,3},{8,4},{9,5},{10,6},{11,7},{12,8},{13,9},{1... | collective-permute-start | bytes 122888 | tf_op jit(solution)/shard_map/ppermute | solution.py:22
  167.6 26.4 %collective-permute-start.22 = (bf16[10,16,128]{2,1,0:T(8,128)(2,1)S(1)}, bf16[10,16,128]{2,1,0:T(8,128)(2,1)S(1)}, u32[]{:S(2)}, u32[]{:S(2)}) collective-permute-start(bf16[10,16,128]{2,1,0:T(8,128)(2,1)S(1)} %copy-done.114), channel_id=1, source_target_pairs={{0,5},{1,6},{2,7},{3,8},{4,9},{5,10},{6,11},{7,12},{8,13},{9,14},{... | collective-permute-start | bytes 122888 | tf_op jit(solution)/shard_map/ppermute | solution.py:22
  172.7 30.4 %collective-permute-start.23 = (bf16[10,16,128]{2,1,0:T(8,128)(2,1)S(1)}, bf16[10,16,128]{2,1,0:T(8,128)(2,1)S(1)}, u32[]{:S(2)}, u32[]{:S(2)}) collective-permute-start(bf16[10,16,128]{2,1,0:T(8,128)(2,1)S(1)} %copy-done.113), channel_id=1, source_target_pairs={{5,0},{6,1},{7,2},{8,3},{9,4},{10,5},{11,6},{12,7},{13,8},{14,9},{... | collective-permute-start | bytes 122888 | tf_op jit(solution)/shard_map/ppermute | solution.py:22
  180.7 28.0 %collective-permute-start = (bf16[10,16,128]{2,1,0:T(8,128)(2,1)}, bf16[10,16,128]{2,1,0:T(8,128)(2,1)S(1)}, u32[]{:S(2)}, u32[]{:S(2)}) collective-permute-start(bf16[10,16,128]{2,1,0:T(8,128)(2,1)} %gather_fusion.1), channel_id=1, source_target_pairs={{0,1},{1,2},{2,3},{3,4},{4,5},{5,6},{6,7},{7,8},{8,9},{9,10},{10,1... | collective-permute-start | bytes 122888 | tf_op jit(solution)/shard_map/ppermute | solution.py:22
  184.0 35.5 %collective-permute-start.1 = (bf16[10,16,128]{2,1,0:T(8,128)(2,1)}, bf16[10,16,128]{2,1,0:T(8,128)(2,1)S(1)}, u32[]{:S(2)}, u32[]{:S(2)}) collective-permute-start(bf16[10,16,128]{2,1,0:T(8,128)(2,1)} %gather_fusion.2), channel_id=1, source_target_pairs={{1,0},{2,1},{3,2},{4,3},{5,4},{6,5},{7,6},{8,7},{9,8},{10,9},{11,1... | collective-permute-start | bytes 122888 | tf_op jit(solution)/shard_map/ppermute | solution.py:22
  191.5 30.0 %collective-permute-start.2 = (bf16[10,16,128]{2,1,0:T(8,128)(2,1)}, bf16[10,16,128]{2,1,0:T(8,128)(2,1)S(1)}, u32[]{:S(2)}, u32[]{:S(2)}) collective-permute-start(bf16[10,16,128]{2,1,0:T(8,128)(2,1)} %gather_fusion.3), channel_id=1, source_target_pairs={{0,3},{1,4},{2,5},{3,6},{4,7},{5,8},{6,9},{7,10},{8,11},{9,12},{10... | collective-permute-start | bytes 122888 | tf_op jit(solution)/shard_map/ppermute | solution.py:22
  194.0 35.1 %collective-permute-start.3 = (bf16[10,16,128]{2,1,0:T(8,128)(2,1)}, bf16[10,16,128]{2,1,0:T(8,128)(2,1)}, u32[]{:S(2)}, u32[]{:S(2)}) collective-permute-start(bf16[10,16,128]{2,1,0:T(8,128)(2,1)} %gather_fusion.4), channel_id=1, source_target_pairs={{3,0},{4,1},{5,2},{6,3},{7,4},{8,5},{9,6},{10,7},{11,8},{12,9},{13... | collective-permute-start | bytes 122888 | tf_op jit(solution)/shard_map/ppermute | solution.py:22
  203.1 26.7 %collective-permute-start.4 = (bf16[10,16,128]{2,1,0:T(8,128)(2,1)}, bf16[10,16,128]{2,1,0:T(8,128)(2,1)}, u32[]{:S(2)}, u32[]{:S(2)}) collective-permute-start(bf16[10,16,128]{2,1,0:T(8,128)(2,1)} %gather_fusion.5), channel_id=1, source_target_pairs={{0,4},{1,5},{2,6},{3,7},{4,8},{5,9},{6,10},{7,11},{8,12},{9,13},{1... | collective-permute-start | bytes 122888 | tf_op jit(solution)/shard_map/ppermute | solution.py:22
  208.7 22.0 %collective-permute-start.5 = (bf16[10,16,128]{2,1,0:T(8,128)(2,1)S(1)}, bf16[10,16,128]{2,1,0:T(8,128)(2,1)S(1)}, u32[]{:S(2)}, u32[]{:S(2)}) collective-permute-start(bf16[10,16,128]{2,1,0:T(8,128)(2,1)S(1)} %copy-done.112), channel_id=1, source_target_pairs={{4,0},{5,1},{6,2},{7,3},{8,4},{9,5},{10,6},{11,7},{12,8},{13,9},{1... | collective-permute-start | bytes 122888 | tf_op jit(solution)/shard_map/ppermute | solution.py:22
  219.5 11.2 %collective-permute-start.6 = (bf16[10,16,128]{2,1,0:T(8,128)(2,1)S(1)}, bf16[10,16,128]{2,1,0:T(8,128)(2,1)S(1)}, u32[]{:S(2)}, u32[]{:S(2)}) collective-permute-start(bf16[10,16,128]{2,1,0:T(8,128)(2,1)S(1)} %gather_fusion.7), channel_id=1, source_target_pairs={{0,5},{1,6},{2,7},{3,8},{4,9},{5,10},{6,11},{7,12},{8,13},{9,14},{... | collective-permute-start | bytes 122888 | tf_op jit(solution)/shard_map/ppermute | solution.py:22
  221.5 9.3 collective-permute-start.7
  539.6 21.9 %collective-permute-start.24 = (bf16[10,16,128]{2,1,0:T(8,128)(2,1)}, bf16[10,16,128]{2,1,0:T(8,128)(2,1)S(1)}, u32[]{:S(2)}, u32[]{:S(2)}) collective-permute-start(bf16[10,16,128]{2,1,0:T(8,128)(2,1)} %gather_fusion.31), channel_id=1, source_target_pairs={{0,1},{1,2},{2,3},{3,4},{4,5},{5,6},{6,7},{7,8},{8,9},{9,10},{10,1... | collective-permute-start | bytes 122888 | tf_op jit(solution)/shard_map/ppermute | solution.py:22
  541.5 32.6 %collective-permute-start.25 = (bf16[10,16,128]{2,1,0:T(8,128)(2,1)}, bf16[10,16,128]{2,1,0:T(8,128)(2,1)S(1)}, u32[]{:S(2)}, u32[]{:S(2)}) collective-permute-start(bf16[10,16,128]{2,1,0:T(8,128)(2,1)} %gather_fusion.32), channel_id=1, source_target_pairs={{1,0},{2,1},{3,2},{4,3},{5,4},{6,5},{7,6},{8,7},{9,8},{10,9},{11,1... | collective-permute-start | bytes 122888 | tf_op jit(solution)/shard_map/ppermute | solution.py:22
  548.5 27.5 %collective-permute-start.26 = (bf16[10,16,128]{2,1,0:T(8,128)(2,1)}, bf16[10,16,128]{2,1,0:T(8,128)(2,1)S(1)}, u32[]{:S(2)}, u32[]{:S(2)}) collective-permute-start(bf16[10,16,128]{2,1,0:T(8,128)(2,1)} %gather_fusion.33), channel_id=1, source_target_pairs={{0,3},{1,4},{2,5},{3,6},{4,7},{5,8},{6,9},{7,10},{8,11},{9,12},{10... | collective-permute-start | bytes 122888 | tf_op jit(solution)/shard_map/ppermute | solution.py:22
  550.4 42.6 %collective-permute-start.27 = (bf16[10,16,128]{2,1,0:T(8,128)(2,1)}, bf16[10,16,128]{2,1,0:T(8,128)(2,1)S(1)}, u32[]{:S(2)}, u32[]{:S(2)}) collective-permute-start(bf16[10,16,128]{2,1,0:T(8,128)(2,1)} %gather_fusion.34), channel_id=1, source_target_pairs={{3,0},{4,1},{5,2},{6,3},{7,4},{8,5},{9,6},{10,7},{11,8},{12,9},{13... | collective-permute-start | bytes 122888 | tf_op jit(solution)/shard_map/ppermute | solution.py:22
  558.0 36.9 %collective-permute-start.28 = (bf16[10,16,128]{2,1,0:T(8,128)(2,1)}, bf16[10,16,128]{2,1,0:T(8,128)(2,1)S(1)}, u32[]{:S(2)}, u32[]{:S(2)}) collective-permute-start(bf16[10,16,128]{2,1,0:T(8,128)(2,1)} %gather_fusion.35), channel_id=1, source_target_pairs={{0,4},{1,5},{2,6},{3,7},{4,8},{5,9},{6,10},{7,11},{8,12},{9,13},{1... | collective-permute-start | bytes 122888 | tf_op jit(solution)/shard_map/ppermute | solution.py:22
  561.6 39.2 %collective-permute-start.29 = (bf16[10,16,128]{2,1,0:T(8,128)(2,1)S(1)}, bf16[10,16,128]{2,1,0:T(8,128)(2,1)S(1)}, u32[]{:S(2)}, u32[]{:S(2)}) collective-permute-start(bf16[10,16,128]{2,1,0:T(8,128)(2,1)S(1)} %copy-done.111), channel_id=1, source_target_pairs={{4,0},{5,1},{6,2},{7,3},{8,4},{9,5},{10,6},{11,7},{12,8},{13,9},{1... | collective-permute-start | bytes 122888 | tf_op jit(solution)/shard_map/ppermute | solution.py:22
  574.1 28.6 %collective-permute-start.30 = (bf16[10,16,128]{2,1,0:T(8,128)(2,1)S(1)}, bf16[10,16,128]{2,1,0:T(8,128)(2,1)S(1)}, u32[]{:S(2)}, u32[]{:S(2)}) collective-permute-start(bf16[10,16,128]{2,1,0:T(8,128)(2,1)S(1)} %copy-done.110), channel_id=1, source_target_pairs={{0,5},{1,6},{2,7},{3,8},{4,9},{5,10},{6,11},{7,12},{8,13},{9,14},{... | collective-permute-start | bytes 122888 | tf_op jit(solution)/shard_map/ppermute | solution.py:22
  576.1 33.3 %collective-permute-start.31 = (bf16[10,16,128]{2,1,0:T(8,128)(2,1)S(1)}, bf16[10,16,128]{2,1,0:T(8,128)(2,1)S(1)}, u32[]{:S(2)}, u32[]{:S(2)}) collective-permute-start(bf16[10,16,128]{2,1,0:T(8,128)(2,1)S(1)} %copy-done.109), channel_id=1, source_target_pairs={{5,0},{6,1},{7,2},{8,3},{9,4},{10,5},{11,6},{12,7},{13,8},{14,9},{... | collective-permute-start | bytes 122888 | tf_op jit(solution)/shard_map/ppermute | solution.py:22
  593.0 20.3 %collective-permute-start.8 = (bf16[10,16,128]{2,1,0:T(8,128)(2,1)}, bf16[10,16,128]{2,1,0:T(8,128)(2,1)}, u32[]{:S(2)}, u32[]{:S(2)}) collective-permute-start(bf16[10,16,128]{2,1,0:T(8,128)(2,1)} %gather_fusion.11), channel_id=1, source_target_pairs={{0,1},{1,2},{2,3},{3,4},{4,5},{5,6},{6,7},{7,8},{8,9},{9,10},{10,1... | collective-permute-start | bytes 122888 | tf_op jit(solution)/shard_map/ppermute | solution.py:22
  595.0 26.1 %collective-permute-start.9 = (bf16[10,16,128]{2,1,0:T(8,128)(2,1)}, bf16[10,16,128]{2,1,0:T(8,128)(2,1)}, u32[]{:S(2)}, u32[]{:S(2)}) collective-permute-start(bf16[10,16,128]{2,1,0:T(8,128)(2,1)} %gather_fusion.12), channel_id=1, source_target_pairs={{1,0},{2,1},{3,2},{4,3},{5,4},{6,5},{7,6},{8,7},{9,8},{10,9},{11,1... | collective-permute-start | bytes 122888 | tf_op jit(solution)/shard_map/ppermute | solution.py:22
  600.7 23.0 %collective-permute-start.10 = (bf16[10,16,128]{2,1,0:T(8,128)(2,1)}, bf16[10,16,128]{2,1,0:T(8,128)(2,1)}, u32[]{:S(2)}, u32[]{:S(2)}) collective-permute-start(bf16[10,16,128]{2,1,0:T(8,128)(2,1)} %gather_fusion.13), channel_id=1, source_target_pairs={{0,3},{1,4},{2,5},{3,6},{4,7},{5,8},{6,9},{7,10},{8,11},{9,12},{10... | collective-permute-start | bytes 122888 | tf_op jit(solution)/shard_map/ppermute | solution.py:22
  602.7 29.4 %collective-permute-start.11 = (bf16[10,16,128]{2,1,0:T(8,128)(2,1)}, bf16[10,16,128]{2,1,0:T(8,128)(2,1)}, u32[]{:S(2)}, u32[]{:S(2)}) collective-permute-start(bf16[10,16,128]{2,1,0:T(8,128)(2,1)} %gather_fusion.14), channel_id=1, source_target_pairs={{3,0},{4,1},{5,2},{6,3},{7,4},{8,5},{9,6},{10,7},{11,8},{12,9},{13... | collective-permute-start | bytes 122888 | tf_op jit(solution)/shard_map/ppermute | solution.py:22
  609.4 23.5 %collective-permute-start.12 = (bf16[10,16,128]{2,1,0:T(8,128)(2,1)}, bf16[10,16,128]{2,1,0:T(8,128)(2,1)}, u32[]{:S(2)}, u32[]{:S(2)}) collective-permute-start(bf16[10,16,128]{2,1,0:T(8,128)(2,1)} %gather_fusion.15), channel_id=1, source_target_pairs={{0,4},{1,5},{2,6},{3,7},{4,8},{5,9},{6,10},{7,11},{8,12},{9,13},{1... | collective-permute-start | bytes 122888 | tf_op jit(solution)/shard_map/ppermute | solution.py:22
  613.3 20.4 %collective-permute-start.13 = (bf16[10,16,128]{2,1,0:T(8,128)(2,1)}, bf16[10,16,128]{2,1,0:T(8,128)(2,1)S(1)}, u32[]{:S(2)}, u32[]{:S(2)}) collective-permute-start(bf16[10,16,128]{2,1,0:T(8,128)(2,1)} %gather_fusion.16), channel_id=1, source_target_pairs={{4,0},{5,1},{6,2},{7,3},{8,4},{9,5},{10,6},{11,7},{12,8},{13,9},{1... | collective-permute-start | bytes 122888 | tf_op jit(solution)/shard_map/ppermute | solution.py:22
  621.1 12.7 %collective-permute-start.14 = (bf16[10,16,128]{2,1,0:T(8,128)(2,1)}, bf16[10,16,128]{2,1,0:T(8,128)(2,1)S(1)}, u32[]{:S(2)}, u32[]{:S(2)}) collective-permute-start(bf16[10,16,128]{2,1,0:T(8,128)(2,1)} %gather_fusion.17), channel_id=1, source_target_pairs={{0,5},{1,6},{2,7},{3,8},{4,9},{5,10},{6,11},{7,12},{8,13},{9,14},{... | collective-permute-start | bytes 122888 | tf_op jit(solution)/shard_map/ppermute | solution.py:22
  623.8 10.0 %collective-permute-start.15 = (bf16[10,16,128]{2,1,0:T(8,128)(2,1)}, bf16[10,16,128]{2,1,0:T(8,128)(2,1)S(1)}, u32[]{:S(2)}, u32[]{:S(2)}) collective-permute-start(bf16[10,16,128]{2,1,0:T(8,128)(2,1)} %gather_fusion.18), channel_id=1, source_target_pairs={{5,0},{6,1},{7,2},{8,3},{9,4},{10,5},{11,6},{12,7},{13,8},{14,9},{... | collective-permute-start | bytes 122888 | tf_op jit(solution)/shard_map/ppermute | solution.py:22
  672.8 122.0 %copy-start.20 = (bf16[4,4,4,4,128]{4,3,2,1,0:T(4,128)(2,1)}, bf16[4,4,4,4,128]{4,3,2,1,0:T(4,128)(2,1)S(1)}, u32[]{:S(2)}) copy-start(bf16[4,4,4,4,128]{4,3,2,1,0:T(4,128)(2,1)S(1)} %get-tuple-element.1523) | copy-start | bytes 196612
  672.8 122.1 %copy-start.18 = (bf16[4,4,4,4,128]{4,3,2,1,0:T(4,128)(2,1)}, bf16[4,4,4,4,128]{4,3,2,1,0:T(4,128)(2,1)S(1)}, u32[]{:S(2)}) copy-start(bf16[4,4,4,4,128]{4,3,2,1,0:T(4,128)(2,1)S(1)} %get-tuple-element.1522) | copy-start | bytes 196612
  672.8 122.1 %copy-start.16 = (bf16[4,4,4,4,128]{4,3,2,1,0:T(4,128)(2,1)}, bf16[4,4,4,4,128]{4,3,2,1,0:T(4,128)(2,1)S(1)}, u32[]{:S(2)}) copy-start(bf16[4,4,4,4,128]{4,3,2,1,0:T(4,128)(2,1)S(1)} %get-tuple-element.1521) | copy-start | bytes 196612
  672.8 122.1 %copy-start.14 = (bf16[4,4,4,4,128]{4,3,2,1,0:T(4,128)(2,1)}, bf16[4,4,4,4,128]{4,3,2,1,0:T(4,128)(2,1)S(1)}, u32[]{:S(2)}) copy-start(bf16[4,4,4,4,128]{4,3,2,1,0:T(4,128)(2,1)S(1)} %get-tuple-element.1520) | copy-start | bytes 196612
  672.9 122.1 %copy-start.12 = (bf16[4,4,4,4,128]{4,3,2,1,0:T(4,128)(2,1)}, bf16[4,4,4,4,128]{4,3,2,1,0:T(4,128)(2,1)S(1)}, u32[]{:S(2)}) copy-start(bf16[4,4,4,4,128]{4,3,2,1,0:T(4,128)(2,1)S(1)} %get-tuple-element.1519) | copy-start | bytes 196612
  672.9 122.2 %copy-start.10 = (bf16[4,4,4,4,128]{4,3,2,1,0:T(4,128)(2,1)}, bf16[4,4,4,4,128]{4,3,2,1,0:T(4,128)(2,1)S(1)}, u32[]{:S(2)}) copy-start(bf16[4,4,4,4,128]{4,3,2,1,0:T(4,128)(2,1)S(1)} %get-tuple-element.1518) | copy-start | bytes 196612
  672.9 122.2 %copy-start.8 = (bf16[4,4,4,4,128]{4,3,2,1,0:T(4,128)(2,1)}, bf16[4,4,4,4,128]{4,3,2,1,0:T(4,128)(2,1)S(1)}, u32[]{:S(2)}) copy-start(bf16[4,4,4,4,128]{4,3,2,1,0:T(4,128)(2,1)S(1)} %get-tuple-element.1517) | copy-start | bytes 196612
  (181 other events, 6049.0 us)
where the time goes:
time: 967 us; the launch traced here: 962 us
  blocking collectives  558 us (58%)
  local copies, waits for them, and re-layouts  162 us (17%)
  starting transfers between devices  162 us (17%)
  other arithmetic  65.6 us (7%)
    psum x2, blocking collectives, norm_backward(): lax.psum((group_sums(grad_centred), group_sums(grad_centred * centred)),...  215 us
    psum x2, blocking collectives, norm_forward(): lax.psum((group_sums(masked), group_sums(masked * values), jnp.sum(weight...  212 us
    ppermute x32, starting transfers between devices, shifted_2(): lax.ppermute(value, axis, [(source, source + steps) for source in range(l...  162 us
    psum x1, blocking collectives, per_device(): lax.psum((grad_first_w, grad_second_w), ('scene', 'space'))  131 us
    unnamed x604, local copies, waits for them, and re-layouts  60.2 us
    gather x32, local copies, waits for them, and re-layouts, halo_cube(): planes[lax.dynamic_index_in_dim(safe_list, target, 0, keepdims=False)]  35.8 us
    another operation x32, other arithmetic  32.1 us
  transfers between devices with their start and end apart: 32, of which 0 were waited for; matrix products, arithmetic and copies ran while one was open for 5% of the time, Pallas kernels for 0%

commit v1 on v0

v1 whole, which is shorter than its diff:
```python
import jax
import jax.numpy as jnp
from jax import lax
from jax.experimental import pallas as pl
from jax.experimental.pallas import tpu as pltpu
from jax.sharding import PartitionSpec as P

EDGE = 4
SLOTS = 4
VOX = 64
C = 128
CAP = 10
PEERS = 64
PLANE = 16
SHARE = 54
GROUP_COUNT = 64 * 4
EPS = 1e-05

directions = [
    (ordinal // 9 - 1, ordinal // 3 % 3 - 1, ordinal % 3 - 1)
    for ordinal in range(27)
    if ordinal != 13
]
offsets = (1, -1, 3, -3, 4, -4, 5, -5)
LANES = 11
ZERO_PLANE = 3 * CAP

f32 = jnp.float32
bf16 = jnp.bfloat16
VMEM_BYTES = 40 * 1024 * 1024


def group_total(row):
    lane = lax.broadcasted_iota(jnp.int32, row.shape, 1)
    row = row + jnp.where(lane % 2 == 0, pltpu.roll(row, C - 1, 1), pltpu.roll(row, 1, 1))
    return row + jnp.where(lane % 4 < 2, pltpu.roll(row, C - 2, 1), pltpu.roll(row, 2, 1))


def pack_stats(rows):
    rows = [jnp.broadcast_to(row, (8, C)) for row in rows]
    lane = lax.broadcasted_iota(jnp.int32, (8, C), 1)
    packed = jnp.zeros((8, C), f32)
    for n, row in enumerate(rows):
        packed = jnp.where(lane % 4 == n, group_total(row), packed)
    return packed


def unpack_stat(packed, n):
    lane = lax.broadcasted_iota(jnp.int32, packed.shape, 1)
    return group_total(jnp.where(lane % 4 == n, packed, 0.0))


def total_of(stats_ref):
    return jnp.broadcast_to(jnp.sum(stats_ref[...], axis=0, keepdims=True), (8, C))


def norm_stats(stats_ref):
    packed = total_of(stats_ref)
    count = unpack_stat(packed, 2) * (GROUP_COUNT / 4)
    mean = unpack_stat(packed, 0) / count
    inv = lax.rsqrt(unpack_stat(packed, 1) / count - mean * mean + EPS)
    return mean[0:1], inv[0:1], count[0:1]


def sigmoid(n):
    return 1.0 / (1.0 + jnp.exp(-n))


def slot_weight(active_ref, s):
    return active_ref[0, s].astype(f32)


def planes_of(src, dst):
    for s in range(SLOTS):
        dst[6 * s] = src[s, 0:16]
        dst[6 * s + 1] = src[s, 48:64]
        for a in range(4):
            dst[6 * s + 2, 4 * a : 4 * a + 4] = src[s, 16 * a : 16 * a + 4]
            dst[6 * s + 3, 4 * a : 4 * a + 4] = src[s, 16 * a + 12 : 16 * a + 16]
        dst[6 * s + 4] = src[s, pl.ds(0, 16, stride=4)]
        dst[6 * s + 5] = src[s, pl.ds(3, 16, stride=4)]


def fill_sends(list_ref, me, planes_a, planes_b, outs):
    for out, offset in zip(outs, (0,) + offsets):
        target = jnp.clip(me + offset, 0, PEERS - 1)
        for k in range(CAP):
            plane = jnp.maximum(list_ref[target, k], 0)
            out[k] = planes_a[plane].astype(out.dtype)
            out[CAP + k] = planes_b[plane].astype(out.dtype)


def lane_start(offset):
    return (5 - offset) * CAP


def place_halo(pad, table, own_ref, pos_ref, me):
    def one_slot(s, carry):
        for n, (d0, d1, d2) in enumerate(directions):
            owner = own_ref[s, n]
            index = jnp.where(owner >= 0, (owner - me + 5) * CAP + pos_ref[s, n], ZERO_PLANE)
            cells = [(5 if d > 0 else 0, 0 if d > 0 else 3) for d in (d0, d1, d2)]
            (a_to, _), (b_to, b_from), (c_to, c_from) = cells

            def row(r, count=1):
                return table[index, r : r + count]

            if d0 != 0:
                if d1 == 0 and d2 == 0:
                    for b in range(4):
                        pad[s, a_to, 1 + b, 1:5] = row(4 * b, 4)
                elif d2 == 0:
                    pad[s, a_to, b_to, 1:5] = row(4 * b_from, 4)
                elif d1 == 0:
                    for b in range(4):
                        pad[s, a_to, 1 + b, c_to : c_to + 1] = row(4 * b + c_from)
                else:
                    pad[s, a_to, b_to, c_to : c_to + 1] = row(4 * b_from + c_from)
            elif d1 != 0:
                for a in range(4):
                    if d2 == 0:
                        pad[s, 1 + a, b_to, 1:5] = row(4 * a, 4)
                    else:
                        pad[s, 1 + a, b_to, c_to : c_to + 1] = row(4 * a + c_from)
            else:
                for a in range(4):
                    for b in range(4):
                        pad[s, 1 + a, 1 + b, c_to : c_to + 1] = row(4 * a + b)
        return carry

    lax.fori_loop(0, SLOTS, one_slot, 0)


def place_interior(pad, field):
    for s in range(SLOTS):
        for a in range(4):
            for b in range(4):
                pad[s, 1 + a, 1 + b, 1:5] = field[s, 16 * a + 4 * b : 16 * a + 4 * b + 4]


def windows_of(pad, cols):
    def one_layer(t, carry):
        s, a = t // 6, t % 6
        sub = lax.broadcasted_iota(jnp.int32, (8, C), 0)
        layer = [pad[s, a, b] for b in range(6)]
        for k2 in range(3):
            low = [pltpu.roll(v, (8 - k2) % 8, 0) if k2 else v for v in layer]
            high = [pltpu.roll(v, 4 - k2, 0) for v in layer]
            pair = [jnp.where(sub < 4, low[b], high[b + 1]) for b in range(5)]
            for k1 in range(3):
                tile = jnp.concatenate([pair[k1], pair[k1 + 2]], axis=0)
                cols[3 * k1 + k2, s, a] = tile.astype(bf16)
        return carry

    lax.fori_loop(0, SLOTS * 6, one_layer, 0)


def window(cols, k0, k1, k2):
    return cols[3 * k1 + k2, :, k0 : k0 + 4].reshape(SLOTS * VOX, C)


def conv(cols, weight):
    total = jnp.zeros((SLOTS * VOX, C), f32)
    for k0 in range(3):
        left = jnp.concatenate([window(cols, k0, j // 3, j % 3) for j in range(9)], axis=1)
        right = weight[9 * k0 : 9 * k0 + 9].reshape(9 * C, C)
        total = total + jnp.dot(left, right, preferred_element_type=f32)
    return total


def conv_back(cols, weight):
    total = jnp.zeros((SLOTS * VOX, C), f32)
    for k0 in range(3):
        left = jnp.concatenate(
            [window(cols, 2 - k0, 2 - j // 3, 2 - j % 3) for j in range(9)], axis=1
        )
        right = jnp.concatenate([weight[9 * k0 + j] for j in range(9)], axis=1)
        total = total + lax.dot_general(
            left, right, (((1,), (1,)), ((), ())), preferred_element_type=f32
        )
    return total


def weight_grad(cols, grad, out):
    for k0 in range(3):
        left = jnp.concatenate([window(cols, k0, j // 3, j % 3) for j in range(9)], axis=1)
        out[9 * C * k0 : 9 * C * (k0 + 1)] = lax.dot_general(
            left, grad, (((0,), (0,)), ((), ())), preferred_element_type=f32
        )


def send_kernel(feat, gout, active, send_list, stats, *rest):
    outs, (wide_f, wide_g, planes_f, planes_g) = rest[:9], rest[9:]
    me = lax.axis_index("space")
    wide_f[...] = feat[...].astype(f32)
    wide_g[...] = gout[...].astype(f32)
    planes_of(wide_f, planes_f)
    planes_of(wide_g, planes_g)
    fill_sends(send_list, me, planes_f, planes_g, outs)
    total = jnp.zeros((1, C), f32)
    squares = jnp.zeros((1, C), f32)
    slots = 0.0
    for s in range(SLOTS):
        w = slot_weight(active, s)
        x = wide_f[s]
        total = total + w * jnp.sum(x, axis=0, keepdims=True)
        squares = squares + w * jnp.sum(x * x, axis=0, keepdims=True)
        slots = slots + w
    packed = pack_stats([total, squares, jnp.full((1, C), slots, f32)])
    stats[...] = jnp.broadcast_to(packed[0:1], (PEERS, C))


def first_kernel(
    feat, gout, active, owners, positions, send_list, stats1, gain1, bias1, w1, w2, *rest
):
    tables, rest = rest[:9], rest[9:]
    middle, gas, cols_a, stats2 = rest[:4]
    outs, (table_f, table_g, pad, cols_g, act, planes_m, planes_g) = rest[4:13], rest[13:]
    me = lax.axis_index("space")
    mean, inv, _ = norm_stats(stats1)

    def act_of(x):
        n = (x - mean) * inv * gain1[...] + bias1[...]
        return n * sigmoid(n)

    for tab, offset in zip(tables, (0,) + offsets):
        start = lane_start(offset)
        table_f[start : start + CAP] = act_of(tab[0:CAP].astype(f32))
        table_g[start : start + CAP] = tab[CAP : 2 * CAP].astype(f32)
    table_f[ZERO_PLANE] = jnp.zeros((PLANE, C), f32)
    table_g[ZERO_PLANE] = jnp.zeros((PLANE, C), f32)
    for s in range(SLOTS):
        act[s] = slot_weight(active, s) * act_of(feat[s].astype(f32))
    place_interior(pad, act)
    place_halo(pad, table_f, owners, positions, me)
    windows_of(pad, cols_a)
    middle[...] = conv(cols_a, w1).reshape(SLOTS, VOX, C)
    for s in range(SLOTS):
        act[s] = jnp.where(active[0, s] > 0, gout[s].astype(f32), 0.0)
    place_interior(pad, act)
    place_halo(pad, table_g, owners, positions, me)
    windows_of(pad, cols_g)
    gas[...] = conv_back(cols_g, w2).reshape(SLOTS, VOX, C)
    planes_of(middle, planes_m)
    planes_of(gas, planes_g)
    fill_sends(send_list, me, planes_m, planes_g, outs)
    total = jnp.zeros((1, C), f32)
    squares = jnp.zeros((1, C), f32)
    slots = 0.0
    for s in range(SLOTS):
        w = slot_weight(active, s)
        x = middle[s]
        total = total + w * jnp.sum(x, axis=0, keepdims=True)
        squares = squares + w * jnp.sum(x * x, axis=0, keepdims=True)
        slots = slots + w
    packed = pack_stats([total, squares, jnp.full((1, C), slots, f32)])
    stats2[...] = jnp.broadcast_to(packed[0:1], (PEERS, C))


def second_kernel(
    feat, gout, active, owners, positions, middle, gas, stats2, gain2, bias2, w2, *rest
):
    tables, rest = rest[:9], rest[9:]
    block, stats3, grad_w, table, pad, cols, act = rest
    me = lax.axis_index("space")
    mean, inv, _ = norm_stats(stats2)
    gain = gain2[...]
    bias = bias2[...]
    for tab, offset in zip(tables, (0,) + offsets):
        start = lane_start(offset)
        n = (tab[0:CAP] - mean) * inv * gain + bias
        table[start : start + CAP] = n * sigmoid(n)
    table[ZERO_PLANE] = jnp.zeros((PLANE, C), f32)
    sum_q = jnp.zeros((1, C), f32)
    sum_c = jnp.zeros((1, C), f32)
    for s in range(SLOTS):
        w = slot_weight(active, s)
        hat = (middle[s] - mean) * inv
        n = hat * gain + bias
        sg = sigmoid(n)
        act[s] = w * (n * sg)
        q = gas[s] * w * sg * (1.0 + n * (1.0 - sg)) * gain
        sum_q = sum_q + jnp.sum(q, axis=0, keepdims=True)
        sum_c = sum_c + jnp.sum(q * hat, axis=0, keepdims=True)
    packed = pack_stats([sum_q, sum_c])
    stats3[...] = jnp.broadcast_to(packed[0:1], (PEERS, C))
    place_interior(pad, act)
    place_halo(pad, table, owners, positions, me)
    windows_of(pad, cols)
    out = conv(cols, w2).reshape(SLOTS, VOX, C)
    for s in range(SLOTS):
        w = slot_weight(active, s)
        block[s] = ((feat[s].astype(f32) + out[s]) * w).astype(bf16)
        act[s] = jnp.where(active[0, s] > 0, gout[s].astype(f32), 0.0)
    weight_grad(cols, act[...].astype(bf16).reshape(SLOTS * VOX, C), grad_w)


def third_kernel(
    feat,
    active,
    owners,
    positions,
    middle,
    gas,
    stats1,
    stats2,
    stats3,
    gain1,
    bias1,
    gain2,
    bias2,
    w1,
    cols_a,
    grad_w2,
    *rest,
):
    tables, rest = rest[:9], rest[9:]
    q1, share, table, pad, cols, act, grad_w1 = rest
    me = lax.axis_index("space")
    mean, inv, count = norm_stats(stats2)
    gain = gain2[...]
    bias = bias2[...]
    packed = total_of(stats3)
    mean_q = unpack_stat(packed, 0)[0:1] / count
    mean_c = unpack_stat(packed, 1)[0:1] / count

    def grad_of(x, g):
        hat = (x - mean) * inv
        n = hat * gain + bias
        sg = sigmoid(n)
        q = g * sg * (1.0 + n * (1.0 - sg)) * gain
        return (inv * (q - mean_q - hat * mean_c)).astype(bf16).astype(f32)

    for tab, offset in zip(tables, (0,) + offsets):
        start = lane_start(offset)
        table[start : start + CAP] = grad_of(tab[0:CAP], tab[CAP : 2 * CAP])
    table[ZERO_PLANE] = jnp.zeros((PLANE, C), f32)
    for s in range(SLOTS):
        act[s] = slot_weight(active, s) * grad_of(middle[s], gas[s])
    place_interior(pad, act)
    place_halo(pad, table, owners, positions, me)
    windows_of(pad, cols)
    gaf = conv_back(cols, w1).reshape(SLOTS, VOX, C)
    mean1, inv1, _ = norm_stats(stats1)
    sum_q = jnp.zeros((1, C), f32)
    sum_c = jnp.zeros((1, C), f32)
    for s in range(SLOTS):
        hat = (feat[s].astype(f32) - mean1) * inv1
        n = hat * gain1[...] + bias1[...]
        sg = sigmoid(n)
        q = gaf[s] * slot_weight(active, s) * sg * (1.0 + n * (1.0 - sg)) * gain1[...]
        q1[s] = q
        sum_q = sum_q + jnp.sum(q, axis=0, keepdims=True)
        sum_c = sum_c + jnp.sum(q * hat, axis=0, keepdims=True)
    packed = pack_stats([sum_q, sum_c])
    weight_grad(cols_a, act[...].astype(bf16).reshape(SLOTS * VOX, C), grad_w1)
    for p in range(PEERS):
        core, chip = p % 2, p // 2
        share[core, chip, 0:SHARE] = grad_w1[SHARE * p : SHARE * (p + 1)]
        share[core, chip, 56 : 56 + SHARE] = grad_w2[SHARE * p : SHARE * (p + 1)]
        share[core, chip, SHARE : SHARE + 1] = packed[0:1]
        share[core, chip, SHARE + 1 : SHARE + 2] = packed[0:1]
        share[core, chip, 56 + SHARE : 112] = jnp.zeros((2, C), f32)


def last_kernel(feat, gout, active, stats1, q1, parts, gain1, grad_in, rows):
    total = parts[0]
    for n in range(1, 32):
        total = total + parts[n]
    mean1, inv1, count = norm_stats(stats1)
    packed = jnp.broadcast_to(total[SHARE : SHARE + 1], (8, C))
    mean_q = unpack_stat(packed, 0)[0:1] / count
    mean_c = unpack_stat(packed, 1)[0:1] / count
    for s in range(SLOTS):
        hat = (feat[s].astype(f32) - mean1) * inv1
        back = slot_weight(active, s) * inv1 * (q1[s] - mean_q - hat * mean_c)
        top = jnp.where(active[0, s] > 0, gout[s].astype(f32), 0.0)
        grad_in[s] = (top + back).astype(bf16)
    for n in range(8):
        rows[n] = total


vmem = pl.BlockSpec(memory_space=pltpu.VMEM)
smem = pl.BlockSpec(memory_space=pltpu.SMEM)


def call(kernel, specs, out_shape, scratch, args):
    return pl.pallas_call(
        kernel,
        in_specs=specs,
        out_specs=[vmem] * len(out_shape),
        out_shape=out_shape,
        scratch_shapes=scratch,
        compiler_params=pltpu.CompilerParams(vmem_limit_bytes=VMEM_BYTES),
    )(*args)


def shape(*dims, dtype=f32):
    return jax.ShapeDtypeStruct(dims, dtype)


def shifted(value, steps):
    leading, last = max(0, -steps), min(PEERS, PEERS - steps)
    return lax.ppermute(value, "space", [(n, n + steps) for n in range(leading, last)])


def exchange(sends):
    return [sends[0]] + [shifted(block, offset) for block, offset in zip(sends[1:], offsets)]


def spread(stats):
    return lax.all_to_all(stats, "space", 0, 0, tiled=True)


core_groups = [[2 * n, 2 * n + 1] for n in range(PEERS // 2)]
chip_groups = [list(range(core, PEERS, 2)) for core in range(2)]


def per_device(
    features,
    active,
    neighbor_owner,
    record_position,
    send_list,
    conv_first,
    conv_second,
    gain_first,
    bias_first,
    gain_second,
    bias_second,
    grad_output,
):
    feat = features[0]
    gout = grad_output[0]
    owners = neighbor_owner[0]
    positions = record_position[0]
    lists = send_list[0, 0]
    gain1, bias1 = gain_first.reshape(1, C), bias_first.reshape(1, C)
    gain2, bias2 = gain_second.reshape(1, C), bias_second.reshape(1, C)
    field = (SLOTS, VOX, C)
    planes = pltpu.VMEM((24, PLANE, C), f32)
    wide = pltpu.VMEM(field, f32)
    table = pltpu.VMEM((LANES * CAP, PLANE, C), f32)
    pad = pltpu.VMEM((SLOTS, 6, 6, 8, C), f32)
    cols_shape = (9, SLOTS, 6, PLANE, C)
    cols = pltpu.VMEM(cols_shape, bf16)

    stats1, *sends = call(
        send_kernel,
        [vmem, vmem, smem, smem],
        [shape(PEERS, C)] + [shape(2 * CAP, PLANE, C, dtype=bf16)] * 9,
        [wide, wide, planes, planes],
        (feat, gout, active, lists),
    )
    tables0 = exchange(sends)
    stats1 = spread(stats1)

    middle, gas, cols_a, stats2, *sends = call(
        first_kernel,
        [vmem, vmem, smem, smem, smem, smem] + [vmem] * 14,
        [shape(*field), shape(*field), shape(*cols_shape, dtype=bf16), shape(PEERS, C)]
        + [shape(2 * CAP, PLANE, C)] * 9,
        [table, table, pad, cols, wide, planes, planes],
        (feat, gout, active, owners, positions, lists, stats1, gain1, bias1)
        + (conv_first, conv_second, *tables0),
    )
    tables1 = exchange(sends)
    stats2 = spread(stats2)

    block, stats3, grad_w2 = call(
        second_kernel,
        [vmem, vmem, smem, smem, smem] + [vmem] * 15,
        [shape(*field, dtype=bf16), shape(PEERS, C), shape(27 * C, C)],
        [table, pad, cols, wide],
        (feat, gout, active, owners, positions, middle, gas, stats2, gain2, bias2)
        + (conv_second, *tables1),
    )
    stats3 = spread(stats3)

    q1, share = call(
        third_kernel,
        [vmem, smem, smem, smem] + [vmem] * 21,
        [shape(*field), shape(2, PEERS // 2, 112, C)],
        [table, pad, cols, wide, pltpu.VMEM((27 * C, C), f32)],
        (feat, active, owners, positions, middle, gas, stats1, stats2, stats3)
        + (gain1, bias1, gain2, bias2, conv_first, cols_a, grad_w2, *tables1),
    )
    share = lax.all_to_all(share, "space", 0, 0, axis_index_groups=core_groups)
    share = share[0] + share[1]
    share = lax.all_to_all(share, "space", 0, 0, axis_index_groups=chip_groups)

    grad_in, rows = call(
        last_kernel,
        [vmem, vmem, smem, vmem, vmem, vmem, vmem],
        [shape(*field, dtype=bf16), shape(8, 112, C)],
        [],
        (feat, gout, active, stats1, q1, share, gain1),
    )
    rows = lax.all_to_all(rows, "scene", 0, 0)
    rows = jnp.sum(rows, axis=0).astype(bf16)
    return (block[None], grad_in[None], rows[:SHARE], rows[56 : 56 + SHARE])


def solution(mesh):
    return jax.shard_map(
        per_device,
        mesh=mesh,
        in_specs=(
            P("scene", "space", None, None),
            P("scene", "space"),
            P("scene", "space", None),
            P("scene", "space", None),
            P("scene", "space", None, None),
            P(),
            P(),
            P(),
            P(),
            P(),
            P(),
            P("scene", "space", None, None),
        ),
        out_specs=(
            P("scene", "space", None, None),
            P("scene", "space", None, None),
            P("space", None),
            P("space", None),
        ),
        check_vma=False,
    )
```

time: 967 us -> 219 us (0.23)
  the two profiles are of different devices: /device:TPU:2 before, /device:TPU:64 now
where the time goes in v1:
time: 219 us; the launch traced here: 218 us
  blocking collectives  144 us (66%)
  starting transfers between devices  47.9 us (22%)
  Pallas kernels  15.1 us (7%)
  local copies, waits for them, and re-layouts  9.42 us (4%)
    all_to_all x3, blocking collectives, spread(): return lax.all_to_all(stats, 'space', 0, 0, tiled=True)  65.3 us
    all_to_all x1, blocking collectives, per_device(): share = lax.all_to_all(share, 'space', 0, 0, axis_index_groups=chip_groups)  50 us
    ppermute x16, starting transfers between devices, shifted(): lax.ppermute(value, 'space', [(n, n + steps) for n in range(leading, last)])  47.9 us
    all_to_all x1, blocking collectives, per_device(): rows = lax.all_to_all(rows, 'scene', 0, 0)  22.4 us
    pallas_call x5, Pallas kernels, call(): pl.pallas_call(kernel, in_specs=specs, out_specs=[vmem] * len(out_shape),...  15.1 us
    unnamed x33, local copies, waits for them, and re-layouts  8.81 us
    all_to_all x1, blocking collectives, per_device(): share = lax.all_to_all(share, 'space', 0, 0, axis_index_groups=core_groups)  6.68 us
  transfers between devices with their start and end apart: 16, of which 0 were waited for; matrix products, arithmetic and copies ran while one was open for 0% of the time, Pallas kernels for 0%

profile of v1, /device:TPU:64, one launch (start us, length us, event | category | flops | bytes accessed | tf_op | source)
XLA Modules:
  0.0 218.0 jit_solution(3827909702708753077)
XLA Ops:
  0.7 0.8 copy.17
  1.4 0.8 copy-done.4
  2.3 0.8 copy-done.5
  3.1 0.7 copy-done.10
  3.8 1.3 shard_map.147
  5.1 1.9 collective-permute-start
  7.1 3.6 %collective-permute-start.1 = (bf16[20,16,128]{2,1,0:T(8,128)(2,1)S(1)}, bf16[20,16,128]{2,1,0:T(8,128)(2,1)S(1)}, u32[]{:S(2)}, u32[]{:S(2)}) collective-permute-start(bf16[20,16,128]{2,1,0:T(8,128)(2,1)S(1)} %get-tuple-element.37), channel_id=1, source_target_pairs={{1,0},{2,1},{3,2},{4,3},{5,4},{6,5},{7,6},{8,7},{9,8},{10,9},{11,1... | collective-permute-start | bytes 245768 | tf_op jit(solution)/shard_map/ppermute | solution.py:404
  10.7 4.6 %collective-permute-start.2 = (bf16[20,16,128]{2,1,0:T(8,128)(2,1)S(1)}, bf16[20,16,128]{2,1,0:T(8,128)(2,1)S(1)}, u32[]{:S(2)}, u32[]{:S(2)}) collective-permute-start(bf16[20,16,128]{2,1,0:T(8,128)(2,1)S(1)} %get-tuple-element.38), channel_id=1, source_target_pairs={{0,3},{1,4},{2,5},{3,6},{4,7},{5,8},{6,9},{7,10},{8,11},{9,12},{10... | collective-permute-start | bytes 245768 | tf_op jit(solution)/shard_map/ppermute | solution.py:404
  15.4 1.3 collective-permute-start.3
  16.7 7.0 %collective-permute-start.4 = (bf16[20,16,128]{2,1,0:T(8,128)(2,1)S(1)}, bf16[20,16,128]{2,1,0:T(8,128)(2,1)S(1)}, u32[]{:S(2)}, u32[]{:S(2)}) collective-permute-start(bf16[20,16,128]{2,1,0:T(8,128)(2,1)S(1)} %get-tuple-element.40), channel_id=1, source_target_pairs={{0,4},{1,5},{2,6},{3,7},{4,8},{5,9},{6,10},{7,11},{8,12},{9,13},{1... | collective-permute-start | bytes 245768 | tf_op jit(solution)/shard_map/ppermute | solution.py:404
  23.7 1.3 collective-permute-start.5
  25.0 0.0 collective-permute-done.1.rest_2_
  25.0 6.1 %collective-permute-start.6 = (bf16[20,16,128]{2,1,0:T(8,128)(2,1)S(1)}, bf16[20,16,128]{2,1,0:T(8,128)(2,1)S(1)}, u32[]{:S(2)}, u32[]{:S(2)}) collective-permute-start(bf16[20,16,128]{2,1,0:T(8,128)(2,1)S(1)} %get-tuple-element.42), channel_id=1, source_target_pairs={{0,5},{1,6},{2,7},{3,8},{4,9},{5,10},{6,11},{7,12},{8,13},{9,14},{... | collective-permute-start | bytes 245768 | tf_op jit(solution)/shard_map/ppermute | solution.py:404
  31.1 1.3 collective-permute-start.7
  32.4 25.1 %all_to_all.48 = f32[64,1,128]{2,1,0:T(1,128)S(1)} all-to-all(f32[64,1,128]{2,1,0:T(1,128)S(1)} %bitcast.43), channel_id=1, replica_groups=mesh['scene'=8,'space'=64] {'space'}, dimensions={0} | all-to-all | bytes 65536 | tf_op jit(solution)/shard_map/all_to_all | solution.py:412
  57.5 0.0 collective-permute-done.6.rest_7_
  57.5 0.0 copy-start
  57.5 1.2 copy-done
  58.7 1.2 copy-done.2
  59.9 0.7 copy-done.7
  60.6 0.7 copy-done.9
  61.2 0.7 copy-done.11
  61.9 0.7 copy-done.12
  62.6 0.7 copy-done.13
  63.2 5.2 %shard_map.148 = (f32[4,64,128]{2,1,0:T(8,128)S(1)}, f32[4,64,128]{2,1,0:T(8,128)S(1)}, bf16[9,4,6,16,128]{4,3,2,1,0:T(8,128)(2,1)S(1)}, f32[64,128]{1,0:T(8,128...) custom-call(bf16[4,64,128]{2,1,0:T(8,128)(2,1)S(1)} %bitcast.26, ...), custom_call_target="tpu_custom_call" | custom-call | tf_op jit(solution)/shard_map/pallas_call | solution.py:388
  68.4 0.0 copy-start.3
  68.4 0.0 copy-start.8
  68.4 2.1 collective-permute-start.8
  70.5 3.6 %collective-permute-start.9 = (f32[20,16,128]{2,1,0:T(8,128)S(1)}, f32[20,16,128]{2,1,0:T(8,128)S(1)}, u32[]{:S(2)}, u32[]{:S(2)}) collective-permute-start(f32[20,16,128]{2,1,0:T(8,128)S(1)} %get-tuple-element.49), channel_id=1, source_target_pairs={{1,0},{2,1},{3,2},{4,3},{5,4},{6,5},{7,6},{8,7},{9,8},{10,9},{11,1... | collective-permute-start | bytes 491528 | tf_op jit(solution)/shard_map/ppermute | solution.py:404
  74.1 1.3 collective-permute-start.10
  75.4 1.3 collective-permute-start.11
  76.7 6.5 %collective-permute-start.12 = (f32[20,16,128]{2,1,0:T(8,128)S(1)}, f32[20,16,128]{2,1,0:T(8,128)S(1)}, u32[]{:S(2)}, u32[]{:S(2)}) collective-permute-start(f32[20,16,128]{2,1,0:T(8,128)S(1)} %get-tuple-element.52), channel_id=1, source_target_pairs={{0,4},{1,5},{2,6},{3,7},{4,8},{5,9},{6,10},{7,11},{8,12},{9,13},{1... | collective-permute-start | bytes 491528 | tf_op jit(solution)/shard_map/ppermute | solution.py:404
  83.2 1.3 collective-permute-start.13
  84.5 3.4 %collective-permute-start.14 = (f32[20,16,128]{2,1,0:T(8,128)S(1)}, f32[20,16,128]{2,1,0:T(8,128)S(1)}, u32[]{:S(2)}, u32[]{:S(2)}) collective-permute-start(f32[20,16,128]{2,1,0:T(8,128)S(1)} %get-tuple-element.54), channel_id=1, source_target_pairs={{0,5},{1,6},{2,7},{3,8},{4,9},{5,10},{6,11},{7,12},{8,13},{9,14},{... | collective-permute-start | bytes 491528 | tf_op jit(solution)/shard_map/ppermute | solution.py:404
  87.9 0.0 collective-permute-done.10.rest_3_
  87.9 1.3 collective-permute-start.15
  89.2 26.9 %all_to_all.49 = f32[64,1,128]{2,1,0:T(1,128)S(1)} all-to-all(f32[64,1,128]{2,1,0:T(1,128)S(1)} %bitcast.42), channel_id=1, replica_groups=mesh['scene'=8,'space'=64] {'space'}, dimensions={0} | all-to-all | bytes 65536 | tf_op jit(solution)/shard_map/all_to_all | solution.py:412
  116.2 0.0 collective-permute-done.13.rest_6_
  116.2 3.4 %shard_map.149 = (bf16[4,64,128]{2,1,0:T(8,128)(2,1)}, f32[64,128]{1,0:T(8,128)S(1)}, f32[3456,128]{1,0:T(8,128)S(1)}) custom-call(bf16[4,64,128]{2,1,0:T(8,128)(2,1)S(1)} %bitcast.27, bf16[4,64,128]{2,1,0:T(8,128)(2,1)S(1)} %bitcast.32, s32[1,4]{1,0:T(1,128)S(1)} %copy-done.11, s32[4,26]{1,0:T(4,128)S(1)} %bitcast.46, s32[4,26]{1,0:T(4,128)S(1)} %bitcast.49, ...), custom_call_target="tpu_custom_call" | custom-call | tf_op jit(solution)/shard_map/pallas_call | solution.py:388
  119.6 13.3 %all_to_all.50 = f32[64,1,128]{2,1,0:T(1,128)S(1)} all-to-all(f32[64,1,128]{2,1,0:T(1,128)S(1)} %bitcast.44), channel_id=1, replica_groups=mesh['scene'=8,'space'=64] {'space'}, dimensions={0} | all-to-all | bytes 65536 | tf_op jit(solution)/shard_map/all_to_all | solution.py:412
  132.9 3.8 %shard_map.150 = (f32[4,64,128]{2,1,0:T(8,128)S(1)}, f32[2,32,112,128]{3,2,1,0:T(8,128)S(1)}) custom-call(bf16[4,64,128]{2,1,0:T(8,128)(2,1)S(1)} %bitcast.28, s32[1,4]{1,0:T(1,128)S(1)} %copy-done.11, s32[4,26]{1,0:T(4,128)S(1)} %bitcast.47, s32[4,26]{1,0:T(4,128)S(1)} %bitcast.50, f32[4,64,128]{2,1,0:T(8,128)S(1)} %get-tuple-element.44.middle, ...), custom_call_target="tpu_custom_call" | custom-call | tf_op jit(solution)/shard_map/pallas_call | solution.py:388
  136.7 6.7 %all_to_all.51 = f32[2,32,112,128]{3,2,1,0:T(8,128)S(1)} all-to-all(f32[2,32,112,128]{3,2,1,0:T(8,128)S(1)} %get-tuple-element.61), channel_id=1, replica_groups={{0,1},{2,3},{4,5},{6,7},{8,9},{10,11},{12,13},{14,15},{16,17},{18,19},{..., dimensions={0} | all-to-all | bytes 7340032 | tf_op jit(solution)/shard_map/all_to_all | solution.py:488
  143.4 0.2 fusion
  143.6 0.0 copy-start.6
  143.6 50.0 %all_to_all.52.parts = f32[32,112,128]{2,1,0:T(8,128)S(1)} all-to-all(f32[32,112,128]{2,1,0:T(8,128)S(1)} %fusion), channel_id=1, replica_groups={{0,2,4,6,8,10,12,14,16,18,20,22,24,26,28,30,32,34,36,38,40,42,44,46,48,..., dimensions={0} | all-to-all | bytes 3670016 | tf_op jit(solution)/shard_map/all_to_all | solution.py:490
  193.6 1.4 shard_map.151
  195.0 22.4 %all_to_all.53 = f32[8,112,128]{2,1,0:T(8,128)S(1)} all-to-all(f32[8,112,128]{2,1,0:T(8,128)S(1)} %get-tuple-element.63), channel_id=1, replica_groups=mesh['scene'=8,'space'=64] {'scene'}, dimensions={0} | all-to-all | bytes 917504 | tf_op jit(solution)/shard_map/all_to_all | solution.py:499
  217.4 0.6 fusion.1
  (31 shorter events, 0.1 us)
Async XLA Ops:
  0.6 115.6 %copy-start.15 = (f32[128]{0:T(128)S(1)}, f32[128]{0:T(128)}, u32[]{:S(2)}) copy-start(f32[128]{0:T(128)} %param.22) | copy-start | bytes 1540
  0.6 115.6 %copy-start.14 = (f32[128]{0:T(128)S(1)}, f32[128]{0:T(128)}, u32[]{:S(2)}) copy-start(f32[128]{0:T(128)} %param.21) | copy-start | bytes 1540
  1.4 0.8 copy-start.4
  2.3 0.8 copy-start.5
  3.1 0.7 copy-start.10
  5.1 18.6 %collective-permute-start = (bf16[20,16,128]{2,1,0:T(8,128)(2,1)S(1)}, bf16[20,16,128]{2,1,0:T(8,128)(2,1)S(1)}, u32[]{:S(2)}, u32[]{:S(2)}) collective-permute-start(bf16[20,16,128]{2,1,0:T(8,128)(2,1)S(1)} %get-tuple-element.36), channel_id=1, source_target_pairs={{0,1},{1,2},{2,3},{3,4},{4,5},{5,6},{6,7},{7,8},{8,9},{9,10},{10,1... | collective-permute-start | bytes 245768 | tf_op jit(solution)/shard_map/ppermute | solution.py:404
  7.1 17.9 %collective-permute-start.1 = (bf16[20,16,128]{2,1,0:T(8,128)(2,1)S(1)}, bf16[20,16,128]{2,1,0:T(8,128)(2,1)S(1)}, u32[]{:S(2)}, u32[]{:S(2)}) collective-permute-start(bf16[20,16,128]{2,1,0:T(8,128)(2,1)S(1)} %get-tuple-element.37), channel_id=1, source_target_pairs={{1,0},{2,1},{3,2},{4,3},{5,4},{6,5},{7,6},{8,7},{9,8},{10,9},{11,1... | collective-permute-start | bytes 245768 | tf_op jit(solution)/shard_map/ppermute | solution.py:404
  10.7 20.4 %collective-permute-start.2 = (bf16[20,16,128]{2,1,0:T(8,128)(2,1)S(1)}, bf16[20,16,128]{2,1,0:T(8,128)(2,1)S(1)}, u32[]{:S(2)}, u32[]{:S(2)}) collective-permute-start(bf16[20,16,128]{2,1,0:T(8,128)(2,1)S(1)} %get-tuple-element.38), channel_id=1, source_target_pairs={{0,3},{1,4},{2,5},{3,6},{4,7},{5,8},{6,9},{7,10},{8,11},{9,12},{10... | collective-permute-start | bytes 245768 | tf_op jit(solution)/shard_map/ppermute | solution.py:404
  15.4 42.2 %collective-permute-start.3 = (bf16[20,16,128]{2,1,0:T(8,128)(2,1)S(1)}, bf16[20,16,128]{2,1,0:T(8,128)(2,1)S(1)}, u32[]{:S(2)}, u32[]{:S(2)}) collective-permute-start(bf16[20,16,128]{2,1,0:T(8,128)(2,1)S(1)} %get-tuple-element.39), channel_id=1, source_target_pairs={{3,0},{4,1},{5,2},{6,3},{7,4},{8,5},{9,6},{10,7},{11,8},{12,9},{13... | collective-permute-start | bytes 245768 | tf_op jit(solution)/shard_map/ppermute | solution.py:404
  16.7 40.9 %collective-permute-start.4 = (bf16[20,16,128]{2,1,0:T(8,128)(2,1)S(1)}, bf16[20,16,128]{2,1,0:T(8,128)(2,1)S(1)}, u32[]{:S(2)}, u32[]{:S(2)}) collective-permute-start(bf16[20,16,128]{2,1,0:T(8,128)(2,1)S(1)} %get-tuple-element.40), channel_id=1, source_target_pairs={{0,4},{1,5},{2,6},{3,7},{4,8},{5,9},{6,10},{7,11},{8,12},{9,13},{1... | collective-permute-start | bytes 245768 | tf_op jit(solution)/shard_map/ppermute | solution.py:404
  23.7 33.8 %collective-permute-start.5 = (bf16[20,16,128]{2,1,0:T(8,128)(2,1)S(1)}, bf16[20,16,128]{2,1,0:T(8,128)(2,1)S(1)}, u32[]{:S(2)}, u32[]{:S(2)}) collective-permute-start(bf16[20,16,128]{2,1,0:T(8,128)(2,1)S(1)} %get-tuple-element.41), channel_id=1, source_target_pairs={{4,0},{5,1},{6,2},{7,3},{8,4},{9,5},{10,6},{11,7},{12,8},{13,9},{1... | collective-permute-start | bytes 245768 | tf_op jit(solution)/shard_map/ppermute | solution.py:404
  25.0 32.5 %collective-permute-start.6 = (bf16[20,16,128]{2,1,0:T(8,128)(2,1)S(1)}, bf16[20,16,128]{2,1,0:T(8,128)(2,1)S(1)}, u32[]{:S(2)}, u32[]{:S(2)}) collective-permute-start(bf16[20,16,128]{2,1,0:T(8,128)(2,1)S(1)} %get-tuple-element.42), channel_id=1, source_target_pairs={{0,5},{1,6},{2,7},{3,8},{4,9},{5,10},{6,11},{7,12},{8,13},{9,14},{... | collective-permute-start | bytes 245768 | tf_op jit(solution)/shard_map/ppermute | solution.py:404
  31.1 26.4 %collective-permute-start.7 = (bf16[20,16,128]{2,1,0:T(8,128)(2,1)S(1)}, bf16[20,16,128]{2,1,0:T(8,128)(2,1)S(1)}, u32[]{:S(2)}, u32[]{:S(2)}) collective-permute-start(bf16[20,16,128]{2,1,0:T(8,128)(2,1)S(1)} %get-tuple-element.43), channel_id=1, source_target_pairs={{5,0},{6,1},{7,2},{8,3},{9,4},{10,5},{11,6},{12,7},{13,8},{14,9},{... | collective-permute-start | bytes 245768 | tf_op jit(solution)/shard_map/ppermute | solution.py:404
  57.5 1.2 copy-start
  58.7 1.2 copy-start.2
  59.9 0.7 copy-start.7
  60.6 0.7 copy-start.9
  61.2 0.7 copy-start.11
  61.9 0.7 copy-start.12
  62.6 0.7 copy-start.13
  63.2 53.0 %copy-start.1 = (bf16[27,128,128]{2,1,0:T(8,128)(2,1)S(1)}, bf16[27,128,128]{2,1,0:T(8,128)(2,1)}, u32[]{:S(2)}) copy-start(bf16[27,128,128]{2,1,0:T(8,128)(2,1)} %w2.3) | copy-start | bytes 2654212
  68.4 64.5 %copy-start.3 = (bf16[27,128,128]{2,1,0:T(8,128)(2,1)S(1)}, bf16[27,128,128]{2,1,0:T(8,128)(2,1)}, u32[]{:S(2)}) copy-start(bf16[27,128,128]{2,1,0:T(8,128)(2,1)} %w1.3) | copy-start | bytes 2654212
  68.4 64.5 %copy-start.8 = (s32[1,4,26]{2,1,0:T(4,128)S(1)}, s32[1,4,26]{2,1,0:T(4,128)}, u32[]{:S(2)}) copy-start(s32[1,4,26]{2,1,0:T(4,128)} %param.14) | copy-start | bytes 1252
  68.4 14.8 %collective-permute-start.8 = (f32[20,16,128]{2,1,0:T(8,128)S(1)}, f32[20,16,128]{2,1,0:T(8,128)S(1)}, u32[]{:S(2)}, u32[]{:S(2)}) collective-permute-start(f32[20,16,128]{2,1,0:T(8,128)S(1)} %get-tuple-element.48), channel_id=1, source_target_pairs={{0,1},{1,2},{2,3},{3,4},{4,5},{5,6},{6,7},{7,8},{8,9},{9,10},{10,1... | collective-permute-start | bytes 491528 | tf_op jit(solution)/shard_map/ppermute | solution.py:404
  70.5 14.1 %collective-permute-start.9 = (f32[20,16,128]{2,1,0:T(8,128)S(1)}, f32[20,16,128]{2,1,0:T(8,128)S(1)}, u32[]{:S(2)}, u32[]{:S(2)}) collective-permute-start(f32[20,16,128]{2,1,0:T(8,128)S(1)} %get-tuple-element.49), channel_id=1, source_target_pairs={{1,0},{2,1},{3,2},{4,3},{5,4},{6,5},{7,6},{8,7},{9,8},{10,9},{11,1... | collective-permute-start | bytes 491528 | tf_op jit(solution)/shard_map/ppermute | solution.py:404
  74.1 13.8 %collective-permute-start.10 = (f32[20,16,128]{2,1,0:T(8,128)S(1)}, f32[20,16,128]{2,1,0:T(8,128)S(1)}, u32[]{:S(2)}, u32[]{:S(2)}) collective-permute-start(f32[20,16,128]{2,1,0:T(8,128)S(1)} %get-tuple-element.50), channel_id=1, source_target_pairs={{0,3},{1,4},{2,5},{3,6},{4,7},{5,8},{6,9},{7,10},{8,11},{9,12},{10... | collective-permute-start | bytes 491528 | tf_op jit(solution)/shard_map/ppermute | solution.py:404
  75.4 40.7 %collective-permute-start.11 = (f32[20,16,128]{2,1,0:T(8,128)S(1)}, f32[20,16,128]{2,1,0:T(8,128)S(1)}, u32[]{:S(2)}, u32[]{:S(2)}) collective-permute-start(f32[20,16,128]{2,1,0:T(8,128)S(1)} %get-tuple-element.51), channel_id=1, source_target_pairs={{3,0},{4,1},{5,2},{6,3},{7,4},{8,5},{9,6},{10,7},{11,8},{12,9},{13... | collective-permute-start | bytes 491528 | tf_op jit(solution)/shard_map/ppermute | solution.py:404
  76.7 39.4 %collective-permute-start.12 = (f32[20,16,128]{2,1,0:T(8,128)S(1)}, f32[20,16,128]{2,1,0:T(8,128)S(1)}, u32[]{:S(2)}, u32[]{:S(2)}) collective-permute-start(f32[20,16,128]{2,1,0:T(8,128)S(1)} %get-tuple-element.52), channel_id=1, source_target_pairs={{0,4},{1,5},{2,6},{3,7},{4,8},{5,9},{6,10},{7,11},{8,12},{9,13},{1... | collective-permute-start | bytes 491528 | tf_op jit(solution)/shard_map/ppermute | solution.py:404
  83.2 32.9 %collective-permute-start.13 = (f32[20,16,128]{2,1,0:T(8,128)S(1)}, f32[20,16,128]{2,1,0:T(8,128)S(1)}, u32[]{:S(2)}, u32[]{:S(2)}) collective-permute-start(f32[20,16,128]{2,1,0:T(8,128)S(1)} %get-tuple-element.53), channel_id=1, source_target_pairs={{4,0},{5,1},{6,2},{7,3},{8,4},{9,5},{10,6},{11,7},{12,8},{13,9},{1... | collective-permute-start | bytes 491528 | tf_op jit(solution)/shard_map/ppermute | solution.py:404
  84.5 31.6 %collective-permute-start.14 = (f32[20,16,128]{2,1,0:T(8,128)S(1)}, f32[20,16,128]{2,1,0:T(8,128)S(1)}, u32[]{:S(2)}, u32[]{:S(2)}) collective-permute-start(f32[20,16,128]{2,1,0:T(8,128)S(1)} %get-tuple-element.54), channel_id=1, source_target_pairs={{0,5},{1,6},{2,7},{3,8},{4,9},{5,10},{6,11},{7,12},{8,13},{9,14},{... | collective-permute-start | bytes 491528 | tf_op jit(solution)/shard_map/ppermute | solution.py:404
  87.9 28.3 %collective-permute-start.15 = (f32[20,16,128]{2,1,0:T(8,128)S(1)}, f32[20,16,128]{2,1,0:T(8,128)S(1)}, u32[]{:S(2)}, u32[]{:S(2)}) collective-permute-start(f32[20,16,128]{2,1,0:T(8,128)S(1)} %get-tuple-element.55), channel_id=1, source_target_pairs={{5,0},{6,1},{7,2},{8,3},{9,4},{10,5},{11,6},{12,7},{13,8},{14,9},{... | collective-permute-start | bytes 491528 | tf_op jit(solution)/shard_map/ppermute | solution.py:404
  143.6 50.0 %copy-start.6 = (bf16[1,4,64,128]{3,2,1,0:T(8,128)(2,1)S(1)}, bf16[1,4,64,128]{3,2,1,0:T(8,128)(2,1)}, u32[]{:S(2)}) copy-start(bf16[1,4,64,128]{3,2,1,0:T(8,128)(2,1)} %param.23) | copy-start | bytes 196612

commit v2 on v1

--- a/solution.py
+++ b/solution.py
@@ -21,9 +21,9 @@
     for ordinal in range(27)
     if ordinal != 13
 ]
-offsets = (1, -1, 3, -3, 4, -4, 5, -5)
+PLANES = 24
 LANES = 11
-ZERO_PLANE = 3 * CAP
+ZERO_PLANE = 3 * PLANES
 
 f32 = jnp.float32
 bf16 = jnp.bfloat16
@@ -70,35 +70,46 @@
     return active_ref[0, s].astype(f32)
 
 
-def planes_of(src, dst):
-    for s in range(SLOTS):
-        dst[6 * s] = src[s, 0:16]
-        dst[6 * s + 1] = src[s, 48:64]
+def planes_of(src, dst, start):
+    for s in range(SLOTS):
+        dst[start + 6 * s] = src[s, 0:16]
+        dst[start + 6 * s + 1] = src[s, 48:64]
         for a in range(4):
-            dst[6 * s + 2, 4 * a : 4 * a + 4] = src[s, 16 * a : 16 * a + 4]
-            dst[6 * s + 3, 4 * a : 4 * a + 4] = src[s, 16 * a + 12 : 16 * a + 16]
-        dst[6 * s + 4] = src[s, pl.ds(0, 16, stride=4)]
-        dst[6 * s + 5] = src[s, pl.ds(3, 16, stride=4)]
-
-
-def fill_sends(list_ref, me, planes_a, planes_b, outs):
-    for out, offset in zip(outs, (0,) + offsets):
-        target = jnp.clip(me + offset, 0, PEERS - 1)
-        for k in range(CAP):
-            plane = jnp.maximum(list_ref[target, k], 0)
-            out[k] = planes_a[plane].astype(out.dtype)
-            out[CAP + k] = planes_b[plane].astype(out.dtype)
-
-
-def lane_start(offset):
-    return (5 - offset) * CAP
-
-
-def place_halo(pad, table, own_ref, pos_ref, me):
+            dst[start + 6 * s + 2, 4 * a : 4 * a + 4] = src[s, 16 * a : 16 * a + 4]
+            dst[start + 6 * s + 3, 4 * a : 4 * a + 4] = src[s, 16 * a + 12 : 16 * a + 16]
+        dst[start + 6 * s + 4] = src[s, pl.ds(0, 16, stride=4)]
+        dst[start + 6 * s + 5] = src[s, pl.ds(3, 16, stride=4)]
+
+
+def far_distance(device):
+    return 4 - 8 * ((device >> 2) & 1)
+
+
+def near_distance(device):
+    return 1 - 2 * (device & 1)
+
+
+def fill_table(table, fields, scratch, me, make):
+    near = near_distance(me)
+    turn = 0
+    for ref, base in zip(fields, (0, near, -near)):
+        far = far_distance((me + base) & (PEERS - 1))
+        for entry, more in enumerate((0, far, -far)):
+            start = (base + more + 5) * PLANES
+            buffer = scratch.at[turn % 2]
+            turn += 1
+            for s in range(SLOTS):
+                buffer[s] = make(ref, entry, s)
+            planes_of(buffer, table, start)
+    table[ZERO_PLANE] = jnp.zeros((PLANE, C), f32)
+
+
+def place_halo(pad, table, own_ref, pos_ref, ids_ref, me):
     def one_slot(s, carry):
         for n, (d0, d1, d2) in enumerate(directions):
             owner = own_ref[s, n]
-            index = jnp.where(owner >= 0, (owner - me + 5) * CAP + pos_ref[s, n], ZERO_PLANE)
+            plane = jnp.clip(ids_ref[jnp.maximum(owner, 0), pos_ref[s, n]], 0, PLANES - 1)
+            index = jnp.where(owner >= 0, (owner - me + 5) * PLANES + plane, ZERO_PLANE)
             cells = [(5 if d > 0 else 0, 0 if d > 0 else 3) for d in (d0, d1, d2)]
             (a_to, _), (b_to, b_from), (c_to, c_from) = cells
 
@@ -189,33 +200,31 @@
         )
 
 
-def send_kernel(feat, gout, active, send_list, stats, *rest):
-    outs, (wide_f, wide_g, planes_f, planes_g) = rest[:9], rest[9:]
-    me = lax.axis_index("space")
-    wide_f[...] = feat[...].astype(f32)
-    wide_g[...] = gout[...].astype(f32)
-    planes_of(wide_f, planes_f)
-    planes_of(wide_g, planes_g)
-    fill_sends(send_list, me, planes_f, planes_g, outs)
+def start_kernel(feat, gout, active, send_list, stats, both):
+    both[0] = feat[...]
+    both[1] = gout[...]
     total = jnp.zeros((1, C), f32)
     squares = jnp.zeros((1, C), f32)
     slots = 0.0
     for s in range(SLOTS):
         w = slot_weight(active, s)
-        x = wide_f[s]
+        x = feat[s].astype(f32)
         total = total + w * jnp.sum(x, axis=0, keepdims=True)
         squares = squares + w * jnp.sum(x * x, axis=0, keepdims=True)
         slots = slots + w
     packed = pack_stats([total, squares, jnp.full((1, C), slots, f32)])
-    stats[...] = jnp.broadcast_to(packed[0:1], (PEERS, C))
+    record = lax.broadcasted_iota(jnp.int32, (CAP, C), 0)
+    lane = lax.broadcasted_iota(jnp.int32, (CAP, C), 1)
+    select = jnp.where(lane == 4 * record + 3, 1.0, 0.0).astype(bf16)
+    ids = jnp.dot(send_list[...].astype(bf16), select, preferred_element_type=f32)
+    stats[...] = ids + packed[0:1]
 
 
 def first_kernel(
-    feat, gout, active, owners, positions, send_list, stats1, gain1, bias1, w1, w2, *rest
+    feat, gout, active, owners, positions, ids, stats1, gain1, bias1, w1, w2, *rest
 ):
-    tables, rest = rest[:9], rest[9:]
-    middle, gas, cols_a, stats2 = rest[:4]
-    outs, (table_f, table_g, pad, cols_g, act, planes_m, planes_g) = rest[4:13], rest[13:]
+    fields, rest = rest[:3], rest[3:]
+    middle, gas, cols_a, stats2, both, table, pad, cols_g, act, scratch = rest
     me = lax.axis_index("space")
     mean, inv, _ = norm_stats(stats1)
 
@@ -223,27 +232,22 @@
         n = (x - mean) * inv * gain1[...] + bias1[...]
         return n * sigmoid(n)
 
-    for tab, offset in zip(tables, (0,) + offsets):
-        start = lane_start(offset)
-        table_f[start : start + CAP] = act_of(tab[0:CAP].astype(f32))
-        table_g[start : start + CAP] = tab[CAP : 2 * CAP].astype(f32)
-    table_f[ZERO_PLANE] = jnp.zeros((PLANE, C), f32)
-    table_g[ZERO_PLANE] = jnp.zeros((PLANE, C), f32)
+    fill_table(table, fields, scratch, me, lambda ref, e, s: act_of(ref[e, 0, s].astype(f32)))
     for s in range(SLOTS):
         act[s] = slot_weight(active, s) * act_of(feat[s].astype(f32))
     place_interior(pad, act)
-    place_halo(pad, table_f, owners, positions, me)
+    place_halo(pad, table, owners, positions, ids, me)
     windows_of(pad, cols_a)
     middle[...] = conv(cols_a, w1).reshape(SLOTS, VOX, C)
+    fill_table(table, fields, scratch, me, lambda ref, e, s: ref[e, 1, s].astype(f32))
     for s in range(SLOTS):
         act[s] = jnp.where(active[0, s] > 0, gout[s].astype(f32), 0.0)
     place_interior(pad, act)
-    place_halo(pad, table_g, owners, positions, me)
+    place_halo(pad, table, owners, positions, ids, me)
     windows_of(pad, cols_g)
     gas[...] = conv_back(cols_g, w2).reshape(SLOTS, VOX, C)
-    planes_of(middle, planes_m)
-    planes_of(gas, planes_g)
-    fill_sends(send_list, me, planes_m, planes_g, outs)
+    both[0] = middle[...].astype(bf16)
+    both[1] = gas[...].astype(bf16)
     total = jnp.zeros((1, C), f32)
     squares = jnp.zeros((1, C), f32)
     slots = 0.0
@@ -258,19 +262,20 @@
 
 
 def second_kernel(
-    feat, gout, active, owners, positions, middle, gas, stats2, gain2, bias2, w2, *rest
+    feat, gout, active, owners, positions, ids, middle, gas, stats2, gain2, bias2, w2, *rest
 ):
-    tables, rest = rest[:9], rest[9:]
-    block, stats3, grad_w, table, pad, cols, act = rest
+    fields, rest = rest[:3], rest[3:]
+    block, stats3, grad_w, table, pad, cols, act, scratch = rest
     me = lax.axis_index("space")
     mean, inv, _ = norm_stats(stats2)
     gain = gain2[...]
     bias = bias2[...]
-    for tab, offset in zip(tables, (0,) + offsets):
-        start = lane_start(offset)
-        n = (tab[0:CAP] - mean) * inv * gain + bias
-        table[start : start + CAP] = n * sigmoid(n)
-    table[ZERO_PLANE] = jnp.zeros((PLANE, C), f32)
+
+    def act_of(ref, e, s):
+        n = (ref[e, 0, s].astype(f32) - mean) * inv * gain + bias
+        return n * sigmoid(n)
+
+    fill_table(table, fields, scratch, me, act_of)
     sum_q = jnp.zeros((1, C), f32)
     sum_c = jnp.zeros((1, C), f32)
     for s in range(SLOTS):
@@ -285,7 +290,7 @@
     packed = pack_stats([sum_q, sum_c])
     stats3[...] = jnp.broadcast_to(packed[0:1], (PEERS, C))
     place_interior(pad, act)
-    place_halo(pad, table, owners, positions, me)
+    place_halo(pad, table, owners, positions, ids, me)
     windows_of(pad, cols)
     out = conv(cols, w2).reshape(SLOTS, VOX, C)
     for s in range(SLOTS):
@@ -300,6 +305,7 @@
     active,
     owners,
     positions,
+    ids,
     middle,
     gas,
     stats1,
@@ -314,8 +320,8 @@
     grad_w2,
     *rest,
 ):
-    tables, rest = rest[:9], rest[9:]
-    q1, share, table, pad, cols, act, grad_w1 = rest
+    fields, rest = rest[:3], rest[3:]
+    q1, share, table, pad, cols, act, scratch, grad_w1 = rest
     me = lax.axis_index("space")
     mean, inv, count = norm_stats(stats2)
     gain = gain2[...]
@@ -331,14 +337,17 @@
         q = g * sg * (1.0 + n * (1.0 - sg)) * gain
         return (inv * (q - mean_q - hat * mean_c)).astype(bf16).astype(f32)
 
-    for tab, offset in zip(tables, (0,) + offsets):
-        start = lane_start(offset)
-        table[start : start + CAP] = grad_of(tab[0:CAP], tab[CAP : 2 * CAP])
-    table[ZERO_PLANE] = jnp.zeros((PLANE, C), f32)
+    fill_table(
+        table,
+        fields,
+        scratch,
+        me,
+        lambda ref, e, s: grad_of(ref[e, 0, s].astype(f32), ref[e, 1, s].astype(f32)),
+    )
     for s in range(SLOTS):
         act[s] = slot_weight(active, s) * grad_of(middle[s], gas[s])
     place_interior(pad, act)
-    place_halo(pad, table, owners, positions, me)
+    place_halo(pad, table, owners, positions, ids, me)
     windows_of(pad, cols)
     gaf = conv_back(cols, w1).reshape(SLOTS, VOX, C)
     mean1, inv1, _ = norm_stats(stats1)
@@ -399,13 +408,19 @@
     return jax.ShapeDtypeStruct(dims, dtype)
 
 
-def shifted(value, steps):
-    leading, last = max(0, -steps), min(PEERS, PEERS - steps)
-    return lax.ppermute(value, "space", [(n, n + steps) for n in range(leading, last)])
-
-
-def exchange(sends):
-    return [sends[0]] + [shifted(block, offset) for block, offset in zip(sends[1:], offsets)]
+def pairs_of(step, first):
+    lower = [n for n in range(PEERS) if n // step % 2 == first]
+    return [(n, (n + step) % PEERS) for n in lower] + [((n + step) % PEERS, n) for n in lower]
+
+
+far_pairs = (pairs_of(4, 0), pairs_of(4, 1))
+near_pairs = (pairs_of(1, 0), pairs_of(1, 1))
+
+
+def exchange(fields):
+    far = [lax.ppermute(fields, "space", pairs) for pairs in far_pairs]
+    three = jnp.stack([fields, *far])
+    return [three] + [lax.ppermute(three, "space", pairs) for pairs in near_pairs]
 
 
 def spread(stats):
@@ -438,52 +453,53 @@
     gain1, bias1 = gain_first.reshape(1, C), bias_first.reshape(1, C)
     gain2, bias2 = gain_second.reshape(1, C), bias_second.reshape(1, C)
     field = (SLOTS, VOX, C)
-    planes = pltpu.VMEM((24, PLANE, C), f32)
     wide = pltpu.VMEM(field, f32)
-    table = pltpu.VMEM((LANES * CAP, PLANE, C), f32)
+    scratch = pltpu.VMEM((2, *field), f32)
+    table = pltpu.VMEM((LANES * PLANES, PLANE, C), f32)
     pad = pltpu.VMEM((SLOTS, 6, 6, 8, C), f32)
     cols_shape = (9, SLOTS, 6, PLANE, C)
     cols = pltpu.VMEM(cols_shape, bf16)
 
-    stats1, *sends = call(
-        send_kernel,
-        [vmem, vmem, smem, smem],
-        [shape(PEERS, C)] + [shape(2 * CAP, PLANE, C, dtype=bf16)] * 9,
-        [wide, wide, planes, planes],
+    stats1, both = call(
+        start_kernel,
+        [vmem, vmem, smem, vmem],
+        [shape(PEERS, C), shape(2, *field, dtype=bf16)],
+        [],
         (feat, gout, active, lists),
     )
-    tables0 = exchange(sends)
+    fields0 = exchange(both)
     stats1 = spread(stats1)
-
-    middle, gas, cols_a, stats2, *sends = call(
+    ids = stats1[:, 3 : 4 * CAP : 4].astype(jnp.int32)
+
+    middle, gas, cols_a, stats2, both = call(
         first_kernel,
-        [vmem, vmem, smem, smem, smem, smem] + [vmem] * 14,
+        [vmem, vmem, smem, smem, smem, smem] + [vmem] * 8,
         [shape(*field), shape(*field), shape(*cols_shape, dtype=bf16), shape(PEERS, C)]
-        + [shape(2 * CAP, PLANE, C)] * 9,
-        [table, table, pad, cols, wide, planes, planes],
-        (feat, gout, active, owners, positions, lists, stats1, gain1, bias1)
-        + (conv_first, conv_second, *tables0),
-    )
-    tables1 = exchange(sends)
+        + [shape(2, *field, dtype=bf16)],
+        [table, pad, cols, wide, scratch],
+        (feat, gout, active, owners, positions, ids, stats1, gain1, bias1)
+        + (conv_first, conv_second, *fields0),
+    )
+    fields1 = exchange(both)
     stats2 = spread(stats2)
 
     block, stats3, grad_w2 = call(
         second_kernel,
-        [vmem, vmem, smem, smem, smem] + [vmem] * 15,
+        [vmem, vmem, smem, smem, smem, smem] + [vmem] * 9,
         [shape(*field, dtype=bf16), shape(PEERS, C), shape(27 * C, C)],
-        [table, pad, cols, wide],
-        (feat, gout, active, owners, positions, middle, gas, stats2, gain2, bias2)
-        + (conv_second, *tables1),
+        [table, pad, cols, wide, scratch],
+        (feat, gout, active, owners, positions, ids, middle, gas, stats2, gain2, bias2)
+        + (conv_second, *fields1),
     )
     stats3 = spread(stats3)
 
     q1, share = call(
         third_kernel,
-        [vmem, smem, smem, smem] + [vmem] * 21,
+        [vmem, smem, smem, smem, smem] + [vmem] * 15,
         [shape(*field), shape(2, PEERS // 2, 112, C)],
-        [table, pad, cols, wide, pltpu.VMEM((27 * C, C), f32)],
-        (feat, active, owners, positions, middle, gas, stats1, stats2, stats3)
-        + (gain1, bias1, gain2, bias2, conv_first, cols_a, grad_w2, *tables1),
+        [table, pad, cols, wide, scratch, pltpu.VMEM((27 * C, C), f32)],
+        (feat, active, owners, positions, ids, middle, gas, stats1, stats2, stats3)
+        + (gain1, bias1, gain2, bias2, conv_first, cols_a, grad_w2, *fields1),
     )
     share = lax.all_to_all(share, "space", 0, 0, axis_index_groups=core_groups)
     share = share[0] + share[1]

time: 219 us -> 201 us (0.918)
  starting transfers between devices: 47.9 us -> 29.7 us
  blocking collectives: 144 us -> 126 us
  waiting for transfers between devices: 0.04 us -> 14.4 us
  Pallas kernels: 15.1 us -> 17.9 us
    all_to_all x3, blocking collectives: 65.3 us -> 47 us  [spread(): return lax.all_to_all(stats, 'space', 0, 0, tiled=True)]
    ppermute x16 -> x8, starting transfers between devices: 47.9 us -> 29.7 us  [the longest x4 20.1 us: exchange(): far = [lax.ppermute(fields, 'space', pairs) for pairs in far_pairs]]
    ppermute x16 -> x8, waiting for transfers between devices: 0.04 us -> 14.4 us  [the longest x4 14.4 us: exchange(): far = [lax.ppermute(fields, 'space', pairs) for pairs in far_pairs]]
    pallas_call x5, Pallas kernels: 15.1 us -> 17.9 us  [call(): pl.pallas_call(kernel, in_specs=specs, out_specs=[vmem] * len(out_shape),...]
    unnamed x33 -> x39, local copies, waits for them, and re-layouts: 8.81 us -> 10.5 us
  transfers between devices with their start and end apart: 16 -> 8, of which waited for: 0 -> 4; matrix products, arithmetic and copies ran while one was open for 0% -> 0% of each run, Pallas kernels for 0% -> 0%
where the time goes in v2:
time: 201 us; the launch traced here: 200 us
  blocking collectives  126 us (63%)
  starting transfers between devices  29.7 us (15%)
  Pallas kernels  17.9 us (9%)
  waiting for transfers between devices  14.4 us (7%)
  local copies, waits for them, and re-layouts  11.2 us (6%)
    all_to_all x1, blocking collectives, per_device(): share = lax.all_to_all(share, 'space', 0, 0, axis_index_groups=chip_groups)  50 us
    all_to_all x3, blocking collectives, spread(): return lax.all_to_all(stats, 'space', 0, 0, tiled=True)  47 us
    all_to_all x1, blocking collectives, per_device(): rows = lax.all_to_all(rows, 'scene', 0, 0)  22.4 us
    ppermute x4, starting transfers between devices, exchange(): far = [lax.ppermute(fields, 'space', pairs) for pairs in far_pairs]  20.1 us
    pallas_call x5, Pallas kernels, call(): pl.pallas_call(kernel, in_specs=specs, out_specs=[vmem] * len(out_shape),...  17.9 us
    ppermute x4, waiting for transfers between devices, exchange(): far = [lax.ppermute(fields, 'space', pairs) for pairs in far_pairs]  14.4 us
    unnamed x39, local copies, waits for them, and re-layouts  10.5 us
    ppermute x4, starting transfers between devices, exchange(): lax.ppermute(three, 'space', pairs)  9.59 us
  transfers between devices with their start and end apart: 8, of which 4 were waited for; matrix products, arithmetic and copies ran while one was open for 0% of the time, Pallas kernels for 0%

profile of v2, /device:TPU:64, one launch (start us, length us, event | category | flops | bytes accessed | tf_op | source)
XLA Modules:
  0.0 200.4 jit_solution(12004195330072427505)
XLA Ops:
  0.6 0.8 copy.17
  1.4 0.8 copy-done.4
  2.2 0.8 copy-done.6
  3.1 0.7 copy-done.11
  3.7 0.7 shard_map.147
  4.5 12.2 %collective-permute-start.1 = (bf16[2,4,64,128]{3,2,1,0:T(8,128)(2,1)S(1)}, bf16[2,4,64,128]{3,2,1,0:T(8,128)(2,1)S(1)}, u32[]{:S(2)}, u32[]{:S(2)}) collective-permute-start(bf16[2,4,64,128]{3,2,1,0:T(8,128)(2,1)S(1)} %get-tuple-element.19), channel_id=1, source_target_pairs={{4,8},{5,9},{6,10},{7,11},{12,16},{13,17},{14,18},{15,19},{20,24},... | collective-permute-start | bytes 393224 | tf_op jit(solution)/shard_map/ppermute | solution.py:421
  16.7 1.9 collective-permute-start
  18.6 4.5 %collective-permute-done.1 = bf16[2,4,64,128]{3,2,1,0:T(8,128)(2,1)S(1)} collective-permute-done((bf16[2,4,64,128]{3,2,1,0:T(8,128)(2,1)S(1)}, bf16[2,4,64,128]{3,2,1,0:T(8,128)(2,1)S(1)}, u32[]{:S(2)}, u32[]{:S(2)}) %collective-permute-start.1) | collective-permute-done | bytes 131104 | tf_op jit(solution)/shard_map/ppermute | solution.py:421
  23.1 1.5 collective-permute-done
  24.6 3.8 %collective-permute-start.3 = (bf16[3,2,4,64,128]{4,3,2,1,0:T(8,128)(2,1)S(1)}, bf16[3,2,4,64,128]{4,3,2,1,0:T(8,128)(2,1)S(1)}, u32[]{:S(2)}, u32[]{:S(2)}) collective-permute-start(bf16[3,2,4,64,128]{4,3,2,1,0:T(8,128)(2,1)S(1)} %pad_maximum_fusion.rest_0_), channel_id=1, source_target_pairs={{1,2},{3,4},{5,6},{7,8},{9,10},{11,12},{13,14},{15,16},{17,18},{19... | collective-permute-start | bytes 1179656 | tf_op jit(solution)/shard_map/ppermute | solution.py:423
  28.4 1.9 collective-permute-start.2
  30.4 17.0 %all_to_all.48 = f32[64,1,128]{2,1,0:T(1,128)S(1)} all-to-all(f32[64,1,128]{2,1,0:T(1,128)S(1)} %bitcast.51), channel_id=1, replica_groups=mesh['scene'=8,'space'=64] {'space'}, dimensions={0} | all-to-all | bytes 65536 | tf_op jit(solution)/shard_map/all_to_all | solution.py:427
  47.3 0.1 slice.15
  47.5 0.0 collective-permute-done.3.rest_2_
  47.5 0.0 collective-permute-done.2.rest_1_
  47.5 0.0 copy-start
  47.5 1.2 copy-done
  48.7 1.2 copy-done.2
  49.9 0.8 copy-done.5
  50.7 0.8 copy-done.7
  51.6 0.7 copy-done.9
  52.2 0.7 copy-done.10
  52.9 0.7 copy-done.12
  53.6 0.7 copy-done.13
  54.2 0.7 copy-done.15
  54.9 6.1 %shard_map.148 = (f32[4,64,128]{2,1,0:T(8,128)S(1)}, f32[4,64,128]{2,1,0:T(8,128)S(1)}, bf16[9,4,6,16,128]{4,3,2,1,0:T(8,128)(2,1)S(1)}, f32[64,128]{1,0:T(8,128)S(1)}, bf16[2,4,64,128]{3,2,1,0:T(8,128)(2,1)S(1)}) custom-call(bf16[4,64,128]{2,1,0:T(8,128)(2,1)S(1)} %bitcast.32, bf16[4,64,128]{2,1,0:T(8,128)(2,1)S(1)} %bitcast.37, s32[1,4]{1,0:T(1,128)S(1)} %copy-done.12, ...), custom_call_target="tpu_custom_call" | custom-call | tf_op jit(solution)/shard_map/pallas_call | solution.py:397
  61.0 0.0 copy-start.3
  61.0 0.0 copy-start.14
  61.0 0.0 copy-start.16
  61.0 4.0 %collective-permute-start.5 = (bf16[2,4,64,128]{3,2,1,0:T(8,128)(2,1)S(1)}, bf16[2,4,64,128]{3,2,1,0:T(8,128)(2,1)S(1)}, u32[]{:S(2)}, u32[]{:S(2)}) collective-permute-start(bf16[2,4,64,128]{3,2,1,0:T(8,128)(2,1)S(1)} %get-tuple-element.23), channel_id=1, source_target_pairs={{4,8},{5,9},{6,10},{7,11},{12,16},{13,17},{14,18},{15,19},{20,24},... | collective-permute-start | bytes 393224 | tf_op jit(solution)/shard_map/ppermute | solution.py:421
  65.0 2.0 collective-permute-start.4
  67.0 8.3 %collective-permute-done.5 = bf16[2,4,64,128]{3,2,1,0:T(8,128)(2,1)S(1)} collective-permute-done((bf16[2,4,64,128]{3,2,1,0:T(8,128)(2,1)S(1)}, bf16[2,4,64,128]{3,2,1,0:T(8,128)(2,1)S(1)}, u32[]{:S(2)}, u32[]{:S(2)}) %collective-permute-start.5) | collective-permute-done | bytes 131104 | tf_op jit(solution)/shard_map/ppermute | solution.py:421
  75.3 0.1 collective-permute-done.4
  75.5 1.9 collective-permute-start.7
  77.4 1.9 collective-permute-start.6
  79.3 16.8 %all_to_all.49 = f32[64,1,128]{2,1,0:T(1,128)S(1)} all-to-all(f32[64,1,128]{2,1,0:T(1,128)S(1)} %bitcast.50), channel_id=1, replica_groups=mesh['scene'=8,'space'=64] {'space'}, dimensions={0} | all-to-all | bytes 65536 | tf_op jit(solution)/shard_map/all_to_all | solution.py:427
  96.1 0.0 collective-permute-done.7.rest_2_
  96.1 0.0 collective-permute-done.6.rest_1_
  96.1 4.5 %shard_map.149 = (bf16[4,64,128]{2,1,0:T(8,128)(2,1)}, f32[64,128]{1,0:T(8,128)S(1)}, f32[3456,128]{1,0:T(8,128)S(1)}) custom-call(bf16[4,64,128]{2,1,0:T(8,128)(2,1)S(1)} %bitcast.33, bf16[4,64,128]{2,1,0:T(8,128)(2,1)S(1)} %bitcast.38, s32[1,4]{1,0:T(1,128)S(1)} %copy-done.12, s32[4,26]{1,0:T(4,128)S(1)} %bitcast.54, s32[4,26]{1,0:T(4,128)S(1)} %bitcast.57, ...), custom_call_target="tpu_custom_call" | custom-call | tf_op jit(solution)/shard_map/pallas_call | solution.py:397
  100.7 13.3 %all_to_all.50 = f32[64,1,128]{2,1,0:T(1,128)S(1)} all-to-all(f32[64,1,128]{2,1,0:T(1,128)S(1)} %bitcast.52), channel_id=1, replica_groups=mesh['scene'=8,'space'=64] {'space'}, dimensions={0} | all-to-all | bytes 65536 | tf_op jit(solution)/shard_map/all_to_all | solution.py:427
  114.0 5.1 %shard_map.150 = (f32[4,64,128]{2,1,0:T(8,128)S(1)}, f32[2,32,112,128]{3,2,1,0:T(8,128)S(1)}) custom-call(bf16[4,64,128]{2,1,0:T(8,128)(2,1)S(1)} %bitcast.34, s32[1,4]{1,0:T(1,128)S(1)} %copy-done.12, s32[4,26]{1,0:T(4,128)S(1)} %bitcast.55, s32[4,26]{1,0:T(4,128)S(1)} %bitcast.58, s32[64,10]{1,0:T(8,128)S(1)} %convert_element_type.6.ids, ...), custom_call_target="tpu_custom_call" | custom-call | tf_op jit(solution)/shard_map/pallas_call | solution.py:397
  119.1 6.7 %all_to_all.51 = f32[2,32,112,128]{3,2,1,0:T(8,128)S(1)} all-to-all(f32[2,32,112,128]{3,2,1,0:T(8,128)S(1)} %get-tuple-element.29), channel_id=1, replica_groups={{0,1},{2,3},{4,5},{6,7},{8,9},{10,11},{12,13},{14,15},{16,17},{18,19},{..., dimensions={0} | all-to-all | bytes 7340032 | tf_op jit(solution)/shard_map/all_to_all | solution.py:504
  125.8 0.2 fusion
  126.0 0.0 copy-start.8
  126.0 50.0 %all_to_all.52.parts = f32[32,112,128]{2,1,0:T(8,128)S(1)} all-to-all(f32[32,112,128]{2,1,0:T(8,128)S(1)} %fusion), channel_id=1, replica_groups={{0,2,4,6,8,10,12,14,16,18,20,22,24,26,28,30,32,34,36,38,40,42,44,46,48,..., dimensions={0} | all-to-all | bytes 3670016 | tf_op jit(solution)/shard_map/all_to_all | solution.py:506
  176.0 1.4 shard_map.151
  177.4 22.4 %all_to_all.53 = f32[8,112,128]{2,1,0:T(8,128)S(1)} all-to-all(f32[8,112,128]{2,1,0:T(8,128)S(1)} %get-tuple-element.31), channel_id=1, replica_groups=mesh['scene'=8,'space'=64] {'scene'}, dimensions={0} | all-to-all | bytes 917504 | tf_op jit(solution)/shard_map/all_to_all | solution.py:515
  199.8 0.6 fusion.1
  (25 shorter events, 0.2 us)
Async XLA Ops:
  1.4 0.8 copy-start.4
  2.2 0.8 copy-start.6
  3.1 0.7 copy-start.11
  4.5 18.6 %collective-permute-start.1 = (bf16[2,4,64,128]{3,2,1,0:T(8,128)(2,1)S(1)}, bf16[2,4,64,128]{3,2,1,0:T(8,128)(2,1)S(1)}, u32[]{:S(2)}, u32[]{:S(2)}) collective-permute-start(bf16[2,4,64,128]{3,2,1,0:T(8,128)(2,1)S(1)} %get-tuple-element.19), channel_id=1, source_target_pairs={{4,8},{5,9},{6,10},{7,11},{12,16},{13,17},{14,18},{15,19},{20,24},... | collective-permute-start | bytes 393224 | tf_op jit(solution)/shard_map/ppermute | solution.py:421
  16.7 7.8 %collective-permute-start = (bf16[2,4,64,128]{3,2,1,0:T(8,128)(2,1)S(1)}, bf16[2,4,64,128]{3,2,1,0:T(8,128)(2,1)S(1)}, u32[]{:S(2)}, u32[]{:S(2)}) collective-permute-start(bf16[2,4,64,128]{3,2,1,0:T(8,128)(2,1)S(1)} %get-tuple-element.19), channel_id=1, source_target_pairs={{0,4},{1,5},{2,6},{3,7},{8,12},{9,13},{10,14},{11,15},{16,20},{17,... | collective-permute-start | bytes 393224 | tf_op jit(solution)/shard_map/ppermute | solution.py:421
  24.6 22.9 %collective-permute-start.3 = (bf16[3,2,4,64,128]{4,3,2,1,0:T(8,128)(2,1)S(1)}, bf16[3,2,4,64,128]{4,3,2,1,0:T(8,128)(2,1)S(1)}, u32[]{:S(2)}, u32[]{:S(2)}) collective-permute-start(bf16[3,2,4,64,128]{4,3,2,1,0:T(8,128)(2,1)S(1)} %pad_maximum_fusion.rest_0_), channel_id=1, source_target_pairs={{1,2},{3,4},{5,6},{7,8},{9,10},{11,12},{13,14},{15,16},{17,18},{19... | collective-permute-start | bytes 1179656 | tf_op jit(solution)/shard_map/ppermute | solution.py:423
  28.4 19.1 %collective-permute-start.2 = (bf16[3,2,4,64,128]{4,3,2,1,0:T(8,128)(2,1)S(1)}, bf16[3,2,4,64,128]{4,3,2,1,0:T(8,128)(2,1)S(1)}, u32[]{:S(2)}, u32[]{:S(2)}) collective-permute-start(bf16[3,2,4,64,128]{4,3,2,1,0:T(8,128)(2,1)S(1)} %pad_maximum_fusion.rest_0_), channel_id=1, source_target_pairs={{0,1},{2,3},{4,5},{6,7},{8,9},{10,11},{12,13},{14,15},{16,17},{18,... | collective-permute-start | bytes 1179656 | tf_op jit(solution)/shard_map/ppermute | solution.py:423
  47.5 1.2 copy-start
  48.7 1.2 copy-start.2
  49.9 0.8 copy-start.5
  50.7 0.8 copy-start.7
  51.5 0.7 copy-start.9
  52.2 0.7 copy-start.10
  52.9 0.7 copy-start.12
  53.6 0.7 copy-start.13
  54.2 0.7 copy-start.15
  54.9 41.2 %copy-start.1 = (bf16[27,128,128]{2,1,0:T(8,128)(2,1)S(1)}, bf16[27,128,128]{2,1,0:T(8,128)(2,1)}, u32[]{:S(2)}) copy-start(bf16[27,128,128]{2,1,0:T(8,128)(2,1)} %w2.3) | copy-start | bytes 2654212
  54.9 41.2 %copy-start.17 = (f32[128]{0:T(128)S(1)}, f32[128]{0:T(128)}, u32[]{:S(2)}) copy-start(f32[128]{0:T(128)} %param.21) | copy-start | bytes 1540
  54.9 41.2 %copy-start.18 = (f32[128]{0:T(128)S(1)}, f32[128]{0:T(128)}, u32[]{:S(2)}) copy-start(f32[128]{0:T(128)} %param.22) | copy-start | bytes 1540
  61.0 53.0 %copy-start.3 = (bf16[27,128,128]{2,1,0:T(8,128)(2,1)S(1)}, bf16[27,128,128]{2,1,0:T(8,128)(2,1)}, u32[]{:S(2)}) copy-start(bf16[27,128,128]{2,1,0:T(8,128)(2,1)} %w1.3) | copy-start | bytes 2654212
  61.0 53.0 %copy-start.14 = (f32[128]{0:T(128)S(1)}, f32[128]{0:T(128)}, u32[]{:S(2)}) copy-start(f32[128]{0:T(128)} %param.19) | copy-start | bytes 1540
  61.0 53.0 %copy-start.16 = (f32[128]{0:T(128)S(1)}, f32[128]{0:T(128)}, u32[]{:S(2)}) copy-start(f32[128]{0:T(128)} %param.20) | copy-start | bytes 1540
  61.0 14.3 %collective-permute-start.5 = (bf16[2,4,64,128]{3,2,1,0:T(8,128)(2,1)S(1)}, bf16[2,4,64,128]{3,2,1,0:T(8,128)(2,1)S(1)}, u32[]{:S(2)}, u32[]{:S(2)}) collective-permute-start(bf16[2,4,64,128]{3,2,1,0:T(8,128)(2,1)S(1)} %get-tuple-element.23), channel_id=1, source_target_pairs={{4,8},{5,9},{6,10},{7,11},{12,16},{13,17},{14,18},{15,19},{20,24},... | collective-permute-start | bytes 393224 | tf_op jit(solution)/shard_map/ppermute | solution.py:421
  65.0 10.4 %collective-permute-start.4 = (bf16[2,4,64,128]{3,2,1,0:T(8,128)(2,1)S(1)}, bf16[2,4,64,128]{3,2,1,0:T(8,128)(2,1)S(1)}, u32[]{:S(2)}, u32[]{:S(2)}) collective-permute-start(bf16[2,4,64,128]{3,2,1,0:T(8,128)(2,1)S(1)} %get-tuple-element.23), channel_id=1, source_target_pairs={{0,4},{1,5},{2,6},{3,7},{8,12},{9,13},{10,14},{11,15},{16,20},{17,... | collective-permute-start | bytes 393224 | tf_op jit(solution)/shard_map/ppermute | solution.py:421
  75.5 20.6 %collective-permute-start.7 = (bf16[3,2,4,64,128]{4,3,2,1,0:T(8,128)(2,1)S(1)}, bf16[3,2,4,64,128]{4,3,2,1,0:T(8,128)(2,1)S(1)}, u32[]{:S(2)}, u32[]{:S(2)}) collective-permute-start(bf16[3,2,4,64,128]{4,3,2,1,0:T(8,128)(2,1)S(1)} %pad_maximum_fusion.1.rest_0_), channel_id=1, source_target_pairs={{1,2},{3,4},{5,6},{7,8},{9,10},{11,12},{13,14},{15,16},{17,18},{19... | collective-permute-start | bytes 1179656 | tf_op jit(solution)/shard_map/ppermute | solution.py:423
  77.4 18.7 %collective-permute-start.6 = (bf16[3,2,4,64,128]{4,3,2,1,0:T(8,128)(2,1)S(1)}, bf16[3,2,4,64,128]{4,3,2,1,0:T(8,128)(2,1)S(1)}, u32[]{:S(2)}, u32[]{:S(2)}) collective-permute-start(bf16[3,2,4,64,128]{4,3,2,1,0:T(8,128)(2,1)S(1)} %pad_maximum_fusion.1.rest_0_), channel_id=1, source_target_pairs={{0,1},{2,3},{4,5},{6,7},{8,9},{10,11},{12,13},{14,15},{16,17},{18,... | collective-permute-start | bytes 1179656 | tf_op jit(solution)/shard_map/ppermute | solution.py:423
  126.0 50.0 %copy-start.8 = (bf16[1,4,64,128]{3,2,1,0:T(8,128)(2,1)S(1)}, bf16[1,4,64,128]{3,2,1,0:T(8,128)(2,1)}, u32[]{:S(2)}) copy-start(bf16[1,4,64,128]{3,2,1,0:T(8,128)(2,1)} %param.23) | copy-start | bytes 196612

commit v3 on v2

--- a/solution.py
+++ b/solution.py
@@ -50,8 +50,9 @@
     return group_total(jnp.where(lane % 4 == n, packed, 0.0))
 
 
-def total_of(stats_ref):
-    return jnp.broadcast_to(jnp.sum(stats_ref[...], axis=0, keepdims=True), (8, C))
+def total_of(stats_ref, part=0):
+    row = jnp.sum(stats_ref[:, C * part : C * (part + 1)], axis=0, keepdims=True)
+    return jnp.broadcast_to(row, (8, C))
 
 
 def norm_stats(stats_ref):
@@ -192,12 +193,58 @@
     return total
 
 
-def weight_grad(cols, grad, out):
+def weight_grad(cols, grad, centre, out):
+    right = jnp.concatenate([grad, jnp.ones((SLOTS * VOX, C), bf16)], axis=1)
     for k0 in range(3):
         left = jnp.concatenate([window(cols, k0, j // 3, j % 3) for j in range(9)], axis=1)
-        out[9 * C * k0 : 9 * C * (k0 + 1)] = lax.dot_general(
-            left, grad, (((0,), (0,)), ((), ())), preferred_element_type=f32
+        both = lax.dot_general(
+            left, right, (((0,), (0,)), ((), ())), preferred_element_type=f32
         )
+        out[9 * C * k0 : 9 * C * (k0 + 1)] = both[:, :C] - both[:, C:] * centre
+
+
+def window_sums(cols):
+    ones = jnp.ones((8, SLOTS * VOX), bf16)
+    rows = []
+    for k0 in range(3):
+        left = jnp.concatenate([window(cols, k0, j // 3, j % 3) for j in range(9)], axis=1)
+        total = jnp.dot(ones, left, preferred_element_type=f32)
+        rows += [total[0:1, C * j : C * (j + 1)] for j in range(9)]
+    return rows
+
+
+def store_shares(rows, out, part):
+    lane = lax.broadcasted_iota(jnp.int32, (1, C), 1)
+    for p in range(PEERS):
+        k, skip = divmod(SHARE * p, C)
+        line = rows[k] if skip == 0 else pltpu.roll(rows[k], C - skip, 1)
+        if skip + SHARE > C:
+            line = jnp.where(lane < C - skip, line, pltpu.roll(rows[k + 1], C - skip, 1))
+        line = jnp.where(lane < SHARE, line, 0.0)
+        out[p : p + 1, C * part : C * (part + 1)] = line
+
+
+def grad_centre(stats1, count):
+    return total_of(stats1, 1)[0:1] / (count / 4)
+
+
+def middle_centre(stats2, stats3, count, mean, inv, mean_q, mean_c):
+    voxels = count / 4
+    sum_hat = (total_of(stats2, 1)[0:1] - voxels * mean) * inv
+    sum_q = total_of(stats3, 1)[0:1]
+    return inv * (sum_q - voxels * mean_q - sum_hat * mean_c) / voxels
+
+
+def outer(shares, centre):
+    first = lax.broadcasted_iota(jnp.int32, (8, C), 0) == 0
+    left = jnp.where(first, jnp.broadcast_to(shares, (8, C)), 0.0)
+    return lax.dot_general(
+        left,
+        jnp.broadcast_to(centre, (8, C)),
+        (((0,), (0,)), ((), ())),
+        precision=lax.Precision.HIGHEST,
+        preferred_element_type=f32,
+    )
 
 
 def start_kernel(feat, gout, active, send_list, stats, both):
@@ -205,10 +252,12 @@
     both[1] = gout[...]
     total = jnp.zeros((1, C), f32)
     squares = jnp.zeros((1, C), f32)
+    grads = jnp.zeros((1, C), f32)
     slots = 0.0
     for s in range(SLOTS):
         w = slot_weight(active, s)
         x = feat[s].astype(f32)
+        grads = grads + w * jnp.sum(gout[s].astype(f32), axis=0, keepdims=True)
         total = total + w * jnp.sum(x, axis=0, keepdims=True)
         squares = squares + w * jnp.sum(x * x, axis=0, keepdims=True)
         slots = slots + w
@@ -217,7 +266,8 @@
     lane = lax.broadcasted_iota(jnp.int32, (CAP, C), 1)
     select = jnp.where(lane == 4 * record + 3, 1.0, 0.0).astype(bf16)
     ids = jnp.dot(send_list[...].astype(bf16), select, preferred_element_type=f32)
-    stats[...] = ids + packed[0:1]
+    stats[:, 0:C] = ids + packed[0:1]
+    stats[:, C : 2 * C] = jnp.broadcast_to(grads, (PEERS, C))
 
 
 def first_kernel(
@@ -258,16 +308,31 @@
         squares = squares + w * jnp.sum(x * x, axis=0, keepdims=True)
         slots = slots + w
     packed = pack_stats([total, squares, jnp.full((1, C), slots, f32)])
-    stats2[...] = jnp.broadcast_to(packed[0:1], (PEERS, C))
+    stats2[:, 0:C] = jnp.broadcast_to(packed[0:1], (PEERS, C))
+    stats2[:, C : 2 * C] = jnp.broadcast_to(total, (PEERS, C))
+    store_shares(window_sums(cols_a), stats2, 2)
 
 
 def second_kernel(
-    feat, gout, active, owners, positions, ids, middle, gas, stats2, gain2, bias2, w2, *rest
+    feat,
+    gout,
+    active,
+    owners,
+    positions,
+    ids,
+    middle,
+    gas,
+    stats1,
+    stats2,
+    gain2,
+    bias2,
+    w2,
+    *rest,
 ):
     fields, rest = rest[:3], rest[3:]
     block, stats3, grad_w, table, pad, cols, act, scratch = rest
     me = lax.axis_index("space")
-    mean, inv, _ = norm_stats(stats2)
+    mean, inv, count = norm_stats(stats2)
     gain = gain2[...]
     bias = bias2[...]
 
@@ -288,16 +353,19 @@
         sum_q = sum_q + jnp.sum(q, axis=0, keepdims=True)
         sum_c = sum_c + jnp.sum(q * hat, axis=0, keepdims=True)
     packed = pack_stats([sum_q, sum_c])
-    stats3[...] = jnp.broadcast_to(packed[0:1], (PEERS, C))
+    stats3[:, 0:C] = jnp.broadcast_to(packed[0:1], (PEERS, C))
+    stats3[:, C : 2 * C] = jnp.broadcast_to(sum_q, (PEERS, C))
     place_interior(pad, act)
     place_halo(pad, table, owners, positions, ids, me)
     windows_of(pad, cols)
+    store_shares(window_sums(cols), stats3, 2)
     out = conv(cols, w2).reshape(SLOTS, VOX, C)
     for s in range(SLOTS):
         w = slot_weight(active, s)
         block[s] = ((feat[s].astype(f32) + out[s]) * w).astype(bf16)
         act[s] = jnp.where(active[0, s] > 0, gout[s].astype(f32), 0.0)
-    weight_grad(cols, act[...].astype(bf16).reshape(SLOTS * VOX, C), grad_w)
+    centre = grad_centre(stats1, count)
+    weight_grad(cols, act[...].astype(bf16).reshape(SLOTS * VOX, C), centre, grad_w)
 
 
 def third_kernel(
@@ -362,7 +430,8 @@
         sum_q = sum_q + jnp.sum(q, axis=0, keepdims=True)
         sum_c = sum_c + jnp.sum(q * hat, axis=0, keepdims=True)
     packed = pack_stats([sum_q, sum_c])
-    weight_grad(cols_a, act[...].astype(bf16).reshape(SLOTS * VOX, C), grad_w1)
+    centre = middle_centre(stats2, stats3, count, mean, inv, mean_q, mean_c)
+    weight_grad(cols_a, act[...].astype(bf16).reshape(SLOTS * VOX, C), centre, grad_w1)
     for p in range(PEERS):
         core, chip = p % 2, p // 2
         share[core, chip, 0:SHARE] = grad_w1[SHARE * p : SHARE * (p + 1)]
@@ -372,12 +441,30 @@
         share[core, chip, 56 + SHARE : 112] = jnp.zeros((2, C), f32)
 
 
-def last_kernel(feat, gout, active, stats1, q1, parts, gain1, grad_in, rows):
-    total = parts[0]
-    for n in range(1, 32):
-        total = total + parts[n]
+def pair_kernel(pair, out):
+    for n in range(PEERS // 2):
+        total = pair[0, n] + pair[1, n]
+        row = total[SHARE : SHARE + 1]
+        high = row.astype(bf16)
+        left = row - high.astype(f32)
+        middle = left.astype(bf16)
+        low = (left - middle.astype(f32)).astype(bf16)
+        at = lax.broadcasted_iota(jnp.int32, (112, C), 0)
+        total = jnp.where(at == SHARE, high.astype(f32), total)
+        total = jnp.where(at == SHARE + 1, middle.astype(f32), total)
+        total = jnp.where(at == 56 + SHARE, low.astype(f32), total)
+        out[n] = total.astype(bf16)
+
+
+def last_kernel(
+    feat, gout, active, stats1, stats2, stats3, q1, parts, gain1, grad_in, rows
+):
+    total = parts[0].astype(f32)
+    for n in range(1, PEERS // 2):
+        total = total + parts[n].astype(f32)
     mean1, inv1, count = norm_stats(stats1)
-    packed = jnp.broadcast_to(total[SHARE : SHARE + 1], (8, C))
+    packed = total[SHARE : SHARE + 1] + total[SHARE + 1 : SHARE + 2] + total[110:111]
+    packed = jnp.broadcast_to(packed, (8, C))
     mean_q = unpack_stat(packed, 0)[0:1] / count
     mean_c = unpack_stat(packed, 1)[0:1] / count
     for s in range(SLOTS):
@@ -385,8 +472,17 @@
         back = slot_weight(active, s) * inv1 * (q1[s] - mean_q - hat * mean_c)
         top = jnp.where(active[0, s] > 0, gout[s].astype(f32), 0.0)
         grad_in[s] = (top + back).astype(bf16)
+    mean, inv, _ = norm_stats(stats2)
+    packed = total_of(stats3)
+    mean_q = unpack_stat(packed, 0)[0:1] / count
+    mean_c = unpack_stat(packed, 1)[0:1] / count
+    centre1 = middle_centre(stats2, stats3, count, mean, inv, mean_q, mean_c)
+    centre2 = grad_centre(stats1, count)
+    first = total[0:56] + outer(total_of(stats2, 2)[0:1], centre1)[0:56]
+    second = total[56:112] + outer(total_of(stats3, 2)[0:1], centre2)[0:56]
     for n in range(8):
-        rows[n] = total
+        rows[n, 0:56] = first
+        rows[n, 56:112] = second
 
 
 vmem = pl.BlockSpec(memory_space=pltpu.VMEM)
@@ -463,7 +559,7 @@
     stats1, both = call(
         start_kernel,
         [vmem, vmem, smem, vmem],
-        [shape(PEERS, C), shape(2, *field, dtype=bf16)],
+        [shape(PEERS, 2 * C), shape(2, *field, dtype=bf16)],
         [],
         (feat, gout, active, lists),
     )
@@ -474,7 +570,7 @@
     middle, gas, cols_a, stats2, both = call(
         first_kernel,
         [vmem, vmem, smem, smem, smem, smem] + [vmem] * 8,
-        [shape(*field), shape(*field), shape(*cols_shape, dtype=bf16), shape(PEERS, C)]
+        [shape(*field), shape(*field), shape(*cols_shape, dtype=bf16), shape(PEERS, 3 * C)]
         + [shape(2, *field, dtype=bf16)],
         [table, pad, cols, wide, scratch],
         (feat, gout, active, owners, positions, ids, stats1, gain1, bias1)
@@ -485,10 +581,10 @@
 
     block, stats3, grad_w2 = call(
         second_kernel,
-        [vmem, vmem, smem, smem, smem, smem] + [vmem] * 9,
-        [shape(*field, dtype=bf16), shape(PEERS, C), shape(27 * C, C)],
+        [vmem, vmem, smem, smem, smem, smem] + [vmem] * 10,
+        [shape(*field, dtype=bf16), shape(PEERS, 3 * C), shape(27 * C, C)],
         [table, pad, cols, wide, scratch],
-        (feat, gout, active, owners, positions, ids, middle, gas, stats2, gain2, bias2)
+        (feat, gout, active, owners, positions, ids, middle, gas, stats1, stats2, gain2, bias2)
         + (conv_second, *fields1),
     )
     stats3 = spread(stats3)
@@ -502,15 +598,17 @@
         + (gain1, bias1, gain2, bias2, conv_first, cols_a, grad_w2, *fields1),
     )
     share = lax.all_to_all(share, "space", 0, 0, axis_index_groups=core_groups)
-    share = share[0] + share[1]
+    (share,) = call(
+        pair_kernel, [vmem], [shape(PEERS // 2, 112, C, dtype=bf16)], [], (share,)
+    )
     share = lax.all_to_all(share, "space", 0, 0, axis_index_groups=chip_groups)
 
     grad_in, rows = call(
         last_kernel,
-        [vmem, vmem, smem, vmem, vmem, vmem, vmem],
+        [vmem, vmem, smem] + [vmem] * 6,
         [shape(*field, dtype=bf16), shape(8, 112, C)],
         [],
-        (feat, gout, active, stats1, q1, share, gain1),
+        (feat, gout, active, stats1, stats2, stats3, q1, share, gain1),
     )
     rows = lax.all_to_all(rows, "scene", 0, 0)
     rows = jnp.sum(rows, axis=0).astype(bf16)

time: 201 us -> 185 us (0.920)
  the two profiles are of different devices: /device:TPU:64 before, /device:TPU:66 now
where the time goes in v3:
time: 185 us; the launch traced here: 184 us
  blocking collectives  110 us (59%)
  starting transfers between devices  28.1 us (15%)
  Pallas kernels  18.7 us (10%)
  waiting for transfers between devices  14.5 us (8%)
  local copies, waits for them, and re-layouts  11.6 us (6%)
    all_to_all x3, blocking collectives, spread(): return lax.all_to_all(stats, 'space', 0, 0, tiled=True)  50.2 us
    all_to_all x1, blocking collectives, per_device(): share = lax.all_to_all(share, 'space', 0, 0, axis_index_groups=chip_groups)  30.5 us
    all_to_all x1, blocking collectives, per_device(): rows = lax.all_to_all(rows, 'scene', 0, 0)  22.5 us
    pallas_call x6, Pallas kernels, call(): pl.pallas_call(kernel, in_specs=specs, out_specs=[vmem] * len(out_shape),...  18.7 us
    ppermute x4, starting transfers between devices, exchange(): far = [lax.ppermute(fields, 'space', pairs) for pairs in far_pairs]  18.4 us
    ppermute x4, waiting for transfers between devices, exchange(): far = [lax.ppermute(fields, 'space', pairs) for pairs in far_pairs]  14.5 us
    unnamed x44, local copies, waits for them, and re-layouts  10.6 us
    ppermute x4, starting transfers between devices, exchange(): lax.ppermute(three, 'space', pairs)  9.69 us
  transfers between devices with their start and end apart: 8, of which 4 were waited for; matrix products, arithmetic and copies ran while one was open for 0% of the time, Pallas kernels for 0%

profile of v3, /device:TPU:66, one launch (start us, length us, event | category | flops | bytes accessed | tf_op | source)
XLA Modules:
  0.0 183.8 jit_solution(7848377662974357675)
XLA Ops:
  0.6 0.0 copy-start.1
  0.6 0.9 copy.17
  1.5 0.8 copy-done.4
  2.3 0.8 copy-done.7
  3.2 0.7 copy-done.12
  3.8 0.7 shard_map.147
  4.6 10.0 %collective-permute-start.1 = (bf16[2,4,64,128]{3,2,1,0:T(8,128)(2,1)S(1)}, bf16[2,4,64,128]{3,2,1,0:T(8,128)(2,1)S(1)}, u32[]{:S(2)}, u32[]{:S(2)}) collective-permute-start(bf16[2,4,64,128]{3,2,1,0:T(8,128)(2,1)S(1)} %get-tuple-element.19), channel_id=1, source_target_pairs={{4,8},{5,9},{6,10},{7,11},{12,16},{13,17},{14,18},{15,19},{20,24},... | collective-permute-start | bytes 393224 | tf_op jit(solution)/shard_map/ppermute | solution.py:517
  14.6 2.5 %collective-permute-start = (bf16[2,4,64,128]{3,2,1,0:T(8,128)(2,1)S(1)}, bf16[2,4,64,128]{3,2,1,0:T(8,128)(2,1)S(1)}, u32[]{:S(2)}, u32[]{:S(2)}) collective-permute-start(bf16[2,4,64,128]{3,2,1,0:T(8,128)(2,1)S(1)} %get-tuple-element.19), channel_id=1, source_target_pairs={{0,4},{1,5},{2,6},{3,7},{8,12},{9,13},{10,14},{11,15},{16,20},{17,... | collective-permute-start | bytes 393224 | tf_op jit(solution)/shard_map/ppermute | solution.py:517
  17.1 3.9 %collective-permute-done.1 = bf16[2,4,64,128]{3,2,1,0:T(8,128)(2,1)S(1)} collective-permute-done((bf16[2,4,64,128]{3,2,1,0:T(8,128)(2,1)S(1)}, bf16[2,4,64,128]{3,2,1,0:T(8,128)(2,1)S(1)}, u32[]{:S(2)}, u32[]{:S(2)}) %collective-permute-start.1) | collective-permute-done | bytes 131104 | tf_op jit(solution)/shard_map/ppermute | solution.py:517
  21.0 1.9 %collective-permute-done = bf16[2,4,64,128]{3,2,1,0:T(8,128)(2,1)S(1)} collective-permute-done((bf16[2,4,64,128]{3,2,1,0:T(8,128)(2,1)S(1)}, bf16[2,4,64,128]{3,2,1,0:T(8,128)(2,1)S(1)}, u32[]{:S(2)}, u32[]{:S(2)}) %collective-permute-start) | collective-permute-done | bytes 131104 | tf_op jit(solution)/shard_map/ppermute | solution.py:517
  22.9 1.9 %collective-permute-start.3 = (bf16[3,2,4,64,128]{4,3,2,1,0:T(8,128)(2,1)S(1)}, bf16[3,2,4,64,128]{4,3,2,1,0:T(8,128)(2,1)S(1)}, u32[]{:S(2)}, u32[]{:S(2)}) collective-permute-start(bf16[3,2,4,64,128]{4,3,2,1,0:T(8,128)(2,1)S(1)} %pad_maximum_fusion.rest_0_), channel_id=1, source_target_pairs={{1,2},{3,4},{5,6},{7,8},{9,10},{11,12},{13,14},{15,16},{17,18},{19... | collective-permute-start | bytes 1179656 | tf_op jit(solution)/shard_map/ppermute | solution.py:519
  24.9 3.9 %collective-permute-start.2 = (bf16[3,2,4,64,128]{4,3,2,1,0:T(8,128)(2,1)S(1)}, bf16[3,2,4,64,128]{4,3,2,1,0:T(8,128)(2,1)S(1)}, u32[]{:S(2)}, u32[]{:S(2)}) collective-permute-start(bf16[3,2,4,64,128]{4,3,2,1,0:T(8,128)(2,1)S(1)} %pad_maximum_fusion.rest_0_), channel_id=1, source_target_pairs={{0,1},{2,3},{4,5},{6,7},{8,9},{10,11},{12,13},{14,15},{16,17},{18,... | collective-permute-start | bytes 1179656 | tf_op jit(solution)/shard_map/ppermute | solution.py:519
  28.8 0.1 copy.18
  28.9 18.2 %all_to_all.48 = f32[64,1,256]{2,1,0:T(1,128)S(1)} all-to-all(f32[64,1,256]{2,1,0:T(1,128)S(1)} %copy.18), channel_id=1, replica_groups=mesh['scene'=8,'space'=64] {'space'}, dimensions={0} | all-to-all | bytes 131072 | tf_op jit(solution)/shard_map/all_to_all | solution.py:523
  47.1 0.1 slice.9
  47.3 0.0 collective-permute-done.3.rest_2_
  47.3 0.0 collective-permute-done.2.rest_1_
  47.3 0.0 copy-start
  47.3 1.2 copy-done
  48.5 1.2 copy-done.2
  49.6 0.8 copy-done.5
  50.5 0.8 copy-done.8
  51.3 0.7 copy-done.10
  52.0 0.7 copy-done.11
  52.7 0.7 copy-done.13
  53.3 0.7 copy-done.15
  54.0 0.7 copy-done.17
  54.6 6.3 %shard_map.148 = (f32[4,64,128]{2,1,0:T(8,128)S(1)}, f32[4,64,128]{2,1,0:T(8,128)S(1)}, bf16[9,4,6,16,128]{4,3,2,1,0:T(8,128)(2,1)S(1)}, f32[64,384]{1,0:T(8,128)S(1)}, bf16[2,4,64,128]{3,2,1,0:T(8,128)(2,1)S(1)}) custom-call(bf16[4,64,128]{2,1,0:T(8,128)(2,1)S(1)} %bitcast.35, bf16[4,64,128]{2,1,0:T(8,128)(2,1)S(1)} %bitcast.43, s32[1,4]{1,0:T(1,128)S(1)} %copy-done.13, ...), custom_call_target="tpu_custom_call" | custom-call | tf_op jit(solution)/shard_map/pallas_call | solution.py:493
  60.9 4.0 %collective-permute-start.5 = (bf16[2,4,64,128]{3,2,1,0:T(8,128)(2,1)S(1)}, bf16[2,4,64,128]{3,2,1,0:T(8,128)(2,1)S(1)}, u32[]{:S(2)}, u32[]{:S(2)}) collective-permute-start(bf16[2,4,64,128]{3,2,1,0:T(8,128)(2,1)S(1)} %get-tuple-element.23), channel_id=1, source_target_pairs={{4,8},{5,9},{6,10},{7,11},{12,16},{13,17},{14,18},{15,19},{20,24},... | collective-permute-start | bytes 393224 | tf_op jit(solution)/shard_map/ppermute | solution.py:517
  64.9 1.9 %collective-permute-start.4 = (bf16[2,4,64,128]{3,2,1,0:T(8,128)(2,1)S(1)}, bf16[2,4,64,128]{3,2,1,0:T(8,128)(2,1)S(1)}, u32[]{:S(2)}, u32[]{:S(2)}) collective-permute-start(bf16[2,4,64,128]{3,2,1,0:T(8,128)(2,1)S(1)} %get-tuple-element.23), channel_id=1, source_target_pairs={{0,4},{1,5},{2,6},{3,7},{8,12},{9,13},{10,14},{11,15},{16,20},{17,... | collective-permute-start | bytes 393224 | tf_op jit(solution)/shard_map/ppermute | solution.py:517
  66.9 7.3 %collective-permute-done.5 = bf16[2,4,64,128]{3,2,1,0:T(8,128)(2,1)S(1)} collective-permute-done((bf16[2,4,64,128]{3,2,1,0:T(8,128)(2,1)S(1)}, bf16[2,4,64,128]{3,2,1,0:T(8,128)(2,1)S(1)}, u32[]{:S(2)}, u32[]{:S(2)}) %collective-permute-start.5) | collective-permute-done | bytes 131104 | tf_op jit(solution)/shard_map/ppermute | solution.py:517
  74.2 1.4 collective-permute-done.4
  75.6 1.9 %collective-permute-start.7 = (bf16[3,2,4,64,128]{4,3,2,1,0:T(8,128)(2,1)S(1)}, bf16[3,2,4,64,128]{4,3,2,1,0:T(8,128)(2,1)S(1)}, u32[]{:S(2)}, u32[]{:S(2)}) collective-permute-start(bf16[3,2,4,64,128]{4,3,2,1,0:T(8,128)(2,1)S(1)} %pad_maximum_fusion.1.rest_0_), channel_id=1, source_target_pairs={{1,2},{3,4},{5,6},{7,8},{9,10},{11,12},{13,14},{15,16},{17,18},{19... | collective-permute-start | bytes 1179656 | tf_op jit(solution)/shard_map/ppermute | solution.py:519
  77.5 1.9 %collective-permute-start.6 = (bf16[3,2,4,64,128]{4,3,2,1,0:T(8,128)(2,1)S(1)}, bf16[3,2,4,64,128]{4,3,2,1,0:T(8,128)(2,1)S(1)}, u32[]{:S(2)}, u32[]{:S(2)}) collective-permute-start(bf16[3,2,4,64,128]{4,3,2,1,0:T(8,128)(2,1)S(1)} %pad_maximum_fusion.1.rest_0_), channel_id=1, source_target_pairs={{0,1},{2,3},{4,5},{6,7},{8,9},{10,11},{12,13},{14,15},{16,17},{18,... | collective-permute-start | bytes 1179656 | tf_op jit(solution)/shard_map/ppermute | solution.py:519
  79.5 0.1 copy.19
  79.6 17.6 %all_to_all.49 = f32[64,1,384]{2,1,0:T(1,128)S(1)} all-to-all(f32[64,1,384]{2,1,0:T(1,128)S(1)} %copy.19), channel_id=1, replica_groups=mesh['scene'=8,'space'=64] {'space'}, dimensions={0} | all-to-all | bytes 196608 | tf_op jit(solution)/shard_map/all_to_all | solution.py:523
  97.2 0.0 collective-permute-done.7.rest_2_
  97.2 0.0 collective-permute-done.6.rest_1_
  97.3 4.8 %shard_map.149 = (bf16[4,64,128]{2,1,0:T(8,128)(2,1)}, f32[64,384]{1,0:T(8,128)S(1)}, f32[3456,128]{1,0:T(8,128)S(1)}) custom-call(bf16[4,64,128]{2,1,0:T(8,128)(2,1)S(1)} %bitcast.36, bf16[4,64,128]{2,1,0:T(8,128)(2,1)S(1)} %bitcast.44, s32[1,4]{1,0:T(1,128)S(1)} %copy-done.13, s32[4,26]{1,0:T(4,128)S(1)} %bitcast.55, s32[4,26]{1,0:T(4,128)S(1)} %bitcast.58, ...), custom_call_target="tpu_custom_call" | custom-call | tf_op jit(solution)/shard_map/pallas_call | solution.py:493
  102.0 0.1 copy.20
  102.1 14.3 %all_to_all.50 = f32[64,1,384]{2,1,0:T(1,128)S(1)} all-to-all(f32[64,1,384]{2,1,0:T(1,128)S(1)} %copy.20), channel_id=1, replica_groups=mesh['scene'=8,'space'=64] {'space'}, dimensions={0} | all-to-all | bytes 196608 | tf_op jit(solution)/shard_map/all_to_all | solution.py:523
  116.5 5.1 %shard_map.150 = (f32[4,64,128]{2,1,0:T(8,128)S(1)}, f32[2,32,112,128]{3,2,1,0:T(8,128)S(1)}) custom-call(bf16[4,64,128]{2,1,0:T(8,128)(2,1)S(1)} %bitcast.37, s32[1,4]{1,0:T(1,128)S(1)} %copy-done.13, s32[4,26]{1,0:T(4,128)S(1)} %bitcast.56, s32[4,26]{1,0:T(4,128)S(1)} %bitcast.59, s32[64,10]{1,0:T(8,128)S(1)} %convert_element_type.6.ids, ...), custom_call_target="tpu_custom_call" | custom-call | tf_op jit(solution)/shard_map/pallas_call | solution.py:493
  121.6 6.7 %all_to_all.51.pair = f32[2,32,112,128]{3,2,1,0:T(8,128)S(1)} all-to-all(f32[2,32,112,128]{3,2,1,0:T(8,128)S(1)} %get-tuple-element.29), channel_id=1, replica_groups={{0,1},{2,3},{4,5},{6,7},{8,9},{10,11},{12,13},{14,15},{16,17},{18,19},{..., dimensions={0} | all-to-all | bytes 7340032 | tf_op jit(solution)/shard_map/all_to_all | solution.py:600
  128.3 0.2 shard_map.151
  128.5 30.5 %all_to_all.52.parts = bf16[32,112,128]{2,1,0:T(8,128)(2,1)S(1)} all-to-all(bf16[32,112,128]{2,1,0:T(8,128)(2,1)S(1)} %shard_map.151), channel_id=1, replica_groups={{0,2,4,6,8,10,12,14,16,18,20,22,24,26,28,30,32,34,36,38,40,42,44,46,48,..., dimensions={0} | all-to-all | bytes 1835008 | tf_op jit(solution)/shard_map/all_to_all | solution.py:604
  159.0 1.7 shard_map.152
  160.7 22.5 %all_to_all.53 = f32[8,112,128]{2,1,0:T(8,128)S(1)} all-to-all(f32[8,112,128]{2,1,0:T(8,128)S(1)} %get-tuple-element.31), channel_id=1, replica_groups=mesh['scene'=8,'space'=64] {'scene'}, dimensions={0} | all-to-all | bytes 917504 | tf_op jit(solution)/shard_map/all_to_all | solution.py:613
  183.2 0.6 fusion
  (33 shorter events, 0.2 us)
Async XLA Ops:
  0.6 96.6 %copy-start.1 = (bf16[27,128,128]{2,1,0:T(8,128)(2,1)S(1)}, bf16[27,128,128]{2,1,0:T(8,128)(2,1)}, u32[]{:S(2)}) copy-start(bf16[27,128,128]{2,1,0:T(8,128)(2,1)} %w2.3) | copy-start | bytes 2654212
  1.5 0.8 copy-start.4
  2.3 0.8 copy-start.7
  3.2 0.7 copy-start.12
  3.8 93.4 %copy-start.18 = (f32[128]{0:T(128)S(1)}, f32[128]{0:T(128)}, u32[]{:S(2)}) copy-start(f32[128]{0:T(128)} %param.21) | copy-start | bytes 1540
  3.8 93.4 %copy-start.19 = (f32[128]{0:T(128)S(1)}, f32[128]{0:T(128)}, u32[]{:S(2)}) copy-start(f32[128]{0:T(128)} %param.22) | copy-start | bytes 1540
  4.6 16.4 %collective-permute-start.1 = (bf16[2,4,64,128]{3,2,1,0:T(8,128)(2,1)S(1)}, bf16[2,4,64,128]{3,2,1,0:T(8,128)(2,1)S(1)}, u32[]{:S(2)}, u32[]{:S(2)}) collective-permute-start(bf16[2,4,64,128]{3,2,1,0:T(8,128)(2,1)S(1)} %get-tuple-element.19), channel_id=1, source_target_pairs={{4,8},{5,9},{6,10},{7,11},{12,16},{13,17},{14,18},{15,19},{20,24},... | collective-permute-start | bytes 393224 | tf_op jit(solution)/shard_map/ppermute | solution.py:517
  14.6 8.3 %collective-permute-start = (bf16[2,4,64,128]{3,2,1,0:T(8,128)(2,1)S(1)}, bf16[2,4,64,128]{3,2,1,0:T(8,128)(2,1)S(1)}, u32[]{:S(2)}, u32[]{:S(2)}) collective-permute-start(bf16[2,4,64,128]{3,2,1,0:T(8,128)(2,1)S(1)} %get-tuple-element.19), channel_id=1, source_target_pairs={{0,4},{1,5},{2,6},{3,7},{8,12},{9,13},{10,14},{11,15},{16,20},{17,... | collective-permute-start | bytes 393224 | tf_op jit(solution)/shard_map/ppermute | solution.py:517
  22.9 24.3 %collective-permute-start.3 = (bf16[3,2,4,64,128]{4,3,2,1,0:T(8,128)(2,1)S(1)}, bf16[3,2,4,64,128]{4,3,2,1,0:T(8,128)(2,1)S(1)}, u32[]{:S(2)}, u32[]{:S(2)}) collective-permute-start(bf16[3,2,4,64,128]{4,3,2,1,0:T(8,128)(2,1)S(1)} %pad_maximum_fusion.rest_0_), channel_id=1, source_target_pairs={{1,2},{3,4},{5,6},{7,8},{9,10},{11,12},{13,14},{15,16},{17,18},{19... | collective-permute-start | bytes 1179656 | tf_op jit(solution)/shard_map/ppermute | solution.py:519
  24.9 22.4 %collective-permute-start.2 = (bf16[3,2,4,64,128]{4,3,2,1,0:T(8,128)(2,1)S(1)}, bf16[3,2,4,64,128]{4,3,2,1,0:T(8,128)(2,1)S(1)}, u32[]{:S(2)}, u32[]{:S(2)}) collective-permute-start(bf16[3,2,4,64,128]{4,3,2,1,0:T(8,128)(2,1)S(1)} %pad_maximum_fusion.rest_0_), channel_id=1, source_target_pairs={{0,1},{2,3},{4,5},{6,7},{8,9},{10,11},{12,13},{14,15},{16,17},{18,... | collective-permute-start | bytes 1179656 | tf_op jit(solution)/shard_map/ppermute | solution.py:519
  47.3 1.2 copy-start
  48.5 1.2 copy-start.2
  49.6 0.8 copy-start.5
  50.5 0.8 copy-start.8
  51.3 0.7 copy-start.10
  52.0 0.7 copy-start.11
  52.7 0.7 copy-start.13
  53.3 0.7 copy-start.15
  54.0 0.7 copy-start.17
  54.6 61.9 %copy-start.3 = (bf16[27,128,128]{2,1,0:T(8,128)(2,1)S(1)}, bf16[27,128,128]{2,1,0:T(8,128)(2,1)}, u32[]{:S(2)}) copy-start(bf16[27,128,128]{2,1,0:T(8,128)(2,1)} %w1.3) | copy-start | bytes 2654212
  60.9 13.3 %collective-permute-start.5 = (bf16[2,4,64,128]{3,2,1,0:T(8,128)(2,1)S(1)}, bf16[2,4,64,128]{3,2,1,0:T(8,128)(2,1)S(1)}, u32[]{:S(2)}, u32[]{:S(2)}) collective-permute-start(bf16[2,4,64,128]{3,2,1,0:T(8,128)(2,1)S(1)} %get-tuple-element.23), channel_id=1, source_target_pairs={{4,8},{5,9},{6,10},{7,11},{12,16},{13,17},{14,18},{15,19},{20,24},... | collective-permute-start | bytes 393224 | tf_op jit(solution)/shard_map/ppermute | solution.py:517
  64.9 10.6 %collective-permute-start.4 = (bf16[2,4,64,128]{3,2,1,0:T(8,128)(2,1)S(1)}, bf16[2,4,64,128]{3,2,1,0:T(8,128)(2,1)S(1)}, u32[]{:S(2)}, u32[]{:S(2)}) collective-permute-start(bf16[2,4,64,128]{3,2,1,0:T(8,128)(2,1)S(1)} %get-tuple-element.23), channel_id=1, source_target_pairs={{0,4},{1,5},{2,6},{3,7},{8,12},{9,13},{10,14},{11,15},{16,20},{17,... | collective-permute-start | bytes 393224 | tf_op jit(solution)/shard_map/ppermute | solution.py:517
  75.6 21.6 %collective-permute-start.7 = (bf16[3,2,4,64,128]{4,3,2,1,0:T(8,128)(2,1)S(1)}, bf16[3,2,4,64,128]{4,3,2,1,0:T(8,128)(2,1)S(1)}, u32[]{:S(2)}, u32[]{:S(2)}) collective-permute-start(bf16[3,2,4,64,128]{4,3,2,1,0:T(8,128)(2,1)S(1)} %pad_maximum_fusion.1.rest_0_), channel_id=1, source_target_pairs={{1,2},{3,4},{5,6},{7,8},{9,10},{11,12},{13,14},{15,16},{17,18},{19... | collective-permute-start | bytes 1179656 | tf_op jit(solution)/shard_map/ppermute | solution.py:519
  77.5 19.7 %collective-permute-start.6 = (bf16[3,2,4,64,128]{4,3,2,1,0:T(8,128)(2,1)S(1)}, bf16[3,2,4,64,128]{4,3,2,1,0:T(8,128)(2,1)S(1)}, u32[]{:S(2)}, u32[]{:S(2)}) collective-permute-start(bf16[3,2,4,64,128]{4,3,2,1,0:T(8,128)(2,1)S(1)} %pad_maximum_fusion.1.rest_0_), channel_id=1, source_target_pairs={{0,1},{2,3},{4,5},{6,7},{8,9},{10,11},{12,13},{14,15},{16,17},{18,... | collective-permute-start | bytes 1179656 | tf_op jit(solution)/shard_map/ppermute | solution.py:519
  128.3 30.7 %copy-start.6 = (bf16[1,4,64,128]{3,2,1,0:T(8,128)(2,1)S(1)}, bf16[1,4,64,128]{3,2,1,0:T(8,128)(2,1)}, u32[]{:S(2)}) copy-start(bf16[1,4,64,128]{3,2,1,0:T(8,128)(2,1)} %param.12) | copy-start | bytes 196612
  128.3 30.7 %copy-start.9 = (bf16[1,4,64,128]{3,2,1,0:T(8,128)(2,1)S(1)}, bf16[1,4,64,128]{3,2,1,0:T(8,128)(2,1)}, u32[]{:S(2)}) copy-start(bf16[1,4,64,128]{3,2,1,0:T(8,128)(2,1)} %param.23) | copy-start | bytes 196612
  128.3 30.7 %copy-start.14 = (s32[1,4]{1,0:T(1,128)S(1)}, s32[1,4]{1,0:T(1,128)}, u32[]{:S(2)}) copy-start(s32[1,4]{1,0:T(1,128)} %active.9) | copy-start | bytes 52
  128.3 30.7 %copy-start.16 = (f32[128]{0:T(128)S(1)}, f32[128]{0:T(128)}, u32[]{:S(2)}) copy-start(f32[128]{0:T(128)} %param.19) | copy-start | bytes 1540

commit v4 on v3

--- a/solution.py
+++ b/solution.py
@@ -105,12 +105,34 @@
     table[ZERO_PLANE] = jnp.zeros((PLANE, C), f32)
 
 
-def place_halo(pad, table, own_ref, pos_ref, ids_ref, me):
+def find_planes(owners, positions, ids, index, me):
+    def one_slot(s, carry):
+        for n in range(26):
+            owner = owners[s, n]
+            plane = ids[jnp.maximum(owner, 0), 4 * positions[s, n] + 3]
+            plane = jnp.clip(plane, 0, PLANES - 1)
+            index[s, n] = jnp.where(
+                owner >= 0, (owner - me + 5) * PLANES + plane, ZERO_PLANE
+            )
+        return carry
+
+    lax.fori_loop(0, SLOTS, one_slot, 0)
+
+
+def fetch(sources, targets, sems):
+    copies = [
+        pltpu.make_async_copy(source, target, sems.at[n])
+        for n, (source, target) in enumerate(zip(sources, targets))
+    ]
+    for copy in copies:
+        copy.start()
+    return copies
+
+
+def place_halo(pad, table, index_ref):
     def one_slot(s, carry):
         for n, (d0, d1, d2) in enumerate(directions):
-            owner = own_ref[s, n]
-            plane = jnp.clip(ids_ref[jnp.maximum(owner, 0), pos_ref[s, n]], 0, PLANES - 1)
-            index = jnp.where(owner >= 0, (owner - me + 5) * PLANES + plane, ZERO_PLANE)
+            index = index_ref[s, n]
             cells = [(5 if d > 0 else 0, 0 if d > 0 else 3) for d in (d0, d1, d2)]
             (a_to, _), (b_to, b_from), (c_to, c_from) = cells
 
@@ -247,9 +269,13 @@
     )
 
 
-def start_kernel(feat, gout, active, send_list, stats, both):
-    both[0] = feat[...]
-    both[1] = gout[...]
+def start_kernel(feat_in, gout_in, active_in, list_in, stats, both, active, send_list, sems):
+    feat, gout = both.at[0], both.at[1]
+    copies = fetch(
+        (active_in, list_in, feat_in, gout_in), (active, send_list, feat, gout), sems
+    )
+    for copy in copies:
+        copy.wait()
     total = jnp.zeros((1, C), f32)
     squares = jnp.zeros((1, C), f32)
     grads = jnp.zeros((1, C), f32)
@@ -271,30 +297,49 @@
 
 
 def first_kernel(
-    feat, gout, active, owners, positions, ids, stats1, gain1, bias1, w1, w2, *rest
+    active_in, own_in, pos_in, gain_in, bias_in, w1_in, w2_in, stats1, *rest
 ):
     fields, rest = rest[:3], rest[3:]
-    middle, gas, cols_a, stats2, both, table, pad, cols_g, act, scratch = rest
+    middle, gas, cols_a, stats2, both, index = rest[:6]
+    table, pad, cols_g, act, scratch, ids_v = rest[6:12]
+    active, owners, positions, ids, gain1, bias1, w1, w2, sems = rest[12:]
     me = lax.axis_index("space")
+    copies = fetch(
+        (gain_in, bias_in, active_in, own_in, pos_in, w1_in, w2_in),
+        (gain1, bias1, active, owners, positions, w1, w2),
+        sems,
+    )
+    ids_v[...] = stats1[:, 0:C].astype(jnp.int32)
+    ids_copy = pltpu.make_async_copy(ids_v, ids, sems.at[7])
+    ids_copy.start()
+    feat, gout = fields[0].at[0, 0], fields[0].at[0, 1]
     mean, inv, _ = norm_stats(stats1)
+    copies[0].wait()
+    copies[1].wait()
 
     def act_of(x):
         n = (x - mean) * inv * gain1[...] + bias1[...]
         return n * sigmoid(n)
 
     fill_table(table, fields, scratch, me, lambda ref, e, s: act_of(ref[e, 0, s].astype(f32)))
+    for copy in copies[2:5]:
+        copy.wait()
+    ids_copy.wait()
+    find_planes(owners, positions, ids, index, me)
     for s in range(SLOTS):
         act[s] = slot_weight(active, s) * act_of(feat[s].astype(f32))
     place_interior(pad, act)
-    place_halo(pad, table, owners, positions, ids, me)
+    place_halo(pad, table, index)
     windows_of(pad, cols_a)
+    copies[5].wait()
     middle[...] = conv(cols_a, w1).reshape(SLOTS, VOX, C)
     fill_table(table, fields, scratch, me, lambda ref, e, s: ref[e, 1, s].astype(f32))
     for s in range(SLOTS):
         act[s] = jnp.where(active[0, s] > 0, gout[s].astype(f32), 0.0)
     place_interior(pad, act)
-    place_halo(pad, table, owners, positions, ids, me)
+    place_halo(pad, table, index)
     windows_of(pad, cols_g)
+    copies[6].wait()
     gas[...] = conv_back(cols_g, w2).reshape(SLOTS, VOX, C)
     both[0] = middle[...].astype(bf16)
     both[1] = gas[...].astype(bf16)
@@ -317,9 +362,7 @@
     feat,
     gout,
     active,
-    owners,
-    positions,
-    ids,
+    index,
     middle,
     gas,
     stats1,
@@ -356,7 +399,7 @@
     stats3[:, 0:C] = jnp.broadcast_to(packed[0:1], (PEERS, C))
     stats3[:, C : 2 * C] = jnp.broadcast_to(sum_q, (PEERS, C))
     place_interior(pad, act)
-    place_halo(pad, table, owners, positions, ids, me)
+    place_halo(pad, table, index)
     windows_of(pad, cols)
     store_shares(window_sums(cols), stats3, 2)
     out = conv(cols, w2).reshape(SLOTS, VOX, C)
@@ -371,9 +414,7 @@
 def third_kernel(
     feat,
     active,
-    owners,
-    positions,
-    ids,
+    index,
     middle,
     gas,
     stats1,
@@ -389,7 +430,7 @@
     *rest,
 ):
     fields, rest = rest[:3], rest[3:]
-    q1, share, table, pad, cols, act, scratch, grad_w1 = rest
+    q1, keep, give, table, pad, cols, act, scratch, grad_w1 = rest
     me = lax.axis_index("space")
     mean, inv, count = norm_stats(stats2)
     gain = gain2[...]
@@ -415,7 +456,7 @@
     for s in range(SLOTS):
         act[s] = slot_weight(active, s) * grad_of(middle[s], gas[s])
     place_interior(pad, act)
-    place_halo(pad, table, owners, positions, ids, me)
+    place_halo(pad, table, index)
     windows_of(pad, cols)
     gaf = conv_back(cols, w1).reshape(SLOTS, VOX, C)
     mean1, inv1, _ = norm_stats(stats1)
@@ -432,18 +473,30 @@
     packed = pack_stats([sum_q, sum_c])
     centre = middle_centre(stats2, stats3, count, mean, inv, mean_q, mean_c)
     weight_grad(cols_a, act[...].astype(bf16).reshape(SLOTS * VOX, C), centre, grad_w1)
-    for p in range(PEERS):
-        core, chip = p % 2, p // 2
-        share[core, chip, 0:SHARE] = grad_w1[SHARE * p : SHARE * (p + 1)]
-        share[core, chip, 56 : 56 + SHARE] = grad_w2[SHARE * p : SHARE * (p + 1)]
-        share[core, chip, SHARE : SHARE + 1] = packed[0:1]
-        share[core, chip, SHARE + 1 : SHARE + 2] = packed[0:1]
-        share[core, chip, 56 + SHARE : 112] = jnp.zeros((2, C), f32)
-
-
-def pair_kernel(pair, out):
+
+    def store(out, core):
+        for chip in range(PEERS // 2):
+            start = SHARE * (2 * chip + core)
+            out[chip, 0:SHARE] = grad_w1[start : start + SHARE]
+            out[chip, 56 : 56 + SHARE] = grad_w2[start : start + SHARE]
+            out[chip, SHARE : SHARE + 1] = packed[0:1]
+            out[chip, SHARE + 1 : SHARE + 2] = packed[0:1]
+            out[chip, 56 + SHARE : 112] = jnp.zeros((2, C), f32)
+
+    @pl.when(me % 2 == 0)
+    def _():
+        store(keep, 0)
+        store(give, 1)
+
+    @pl.when(me % 2 == 1)
+    def _():
+        store(keep, 1)
+        store(give, 0)
+
+
+def pair_kernel(own, other, out):
     for n in range(PEERS // 2):
-        total = pair[0, n] + pair[1, n]
+        total = own[n] + other[n]
         row = total[SHARE : SHARE + 1]
         high = row.astype(bf16)
         left = row - high.astype(f32)
@@ -487,13 +540,14 @@
 
 vmem = pl.BlockSpec(memory_space=pltpu.VMEM)
 smem = pl.BlockSpec(memory_space=pltpu.SMEM)
-
-
-def call(kernel, specs, out_shape, scratch, args):
+hbm = pl.BlockSpec(memory_space=pl.ANY)
+
+
+def call(kernel, specs, out_shape, scratch, args, out_specs=None):
     return pl.pallas_call(
         kernel,
         in_specs=specs,
-        out_specs=[vmem] * len(out_shape),
+        out_specs=out_specs or [vmem] * len(out_shape),
         out_shape=out_shape,
         scratch_shapes=scratch,
         compiler_params=pltpu.CompilerParams(vmem_limit_bytes=VMEM_BYTES),
@@ -513,17 +567,19 @@
 near_pairs = (pairs_of(1, 0), pairs_of(1, 1))
 
 
-def exchange(fields):
+def exchange(fields, stats):
     far = [lax.ppermute(fields, "space", pairs) for pairs in far_pairs]
+    stats = spread(stats)
+    *far, stats = lax.optimization_barrier((*far, stats))
     three = jnp.stack([fields, *far])
-    return [three] + [lax.ppermute(three, "space", pairs) for pairs in near_pairs]
+    near = [lax.ppermute(three, "space", pairs) for pairs in near_pairs]
+    return [three, *near], stats
 
 
 def spread(stats):
     return lax.all_to_all(stats, "space", 0, 0, tiled=True)
 
 
-core_groups = [[2 * n, 2 * n + 1] for n in range(PEERS // 2)]
 chip_groups = [list(range(core, PEERS, 2)) for core in range(2)]
 
 
@@ -558,48 +614,64 @@
 
     stats1, both = call(
         start_kernel,
-        [vmem, vmem, smem, vmem],
+        [hbm, hbm, hbm, hbm],
         [shape(PEERS, 2 * C), shape(2, *field, dtype=bf16)],
-        [],
+        [
+            pltpu.SMEM((1, SLOTS), jnp.int32),
+            pltpu.VMEM((PEERS, CAP), jnp.int32),
+            pltpu.SemaphoreType.DMA((4,)),
+        ],
         (feat, gout, active, lists),
     )
-    fields0 = exchange(both)
-    stats1 = spread(stats1)
-    ids = stats1[:, 3 : 4 * CAP : 4].astype(jnp.int32)
-
-    middle, gas, cols_a, stats2, both = call(
+    fields0, stats1 = exchange(both, stats1)
+
+    middle, gas, cols_a, stats2, both, index = call(
         first_kernel,
-        [vmem, vmem, smem, smem, smem, smem] + [vmem] * 8,
+        [hbm] * 7 + [vmem] * 4,
         [shape(*field), shape(*field), shape(*cols_shape, dtype=bf16), shape(PEERS, 3 * C)]
-        + [shape(2, *field, dtype=bf16)],
-        [table, pad, cols, wide, scratch],
-        (feat, gout, active, owners, positions, ids, stats1, gain1, bias1)
-        + (conv_first, conv_second, *fields0),
-    )
-    fields1 = exchange(both)
-    stats2 = spread(stats2)
+        + [shape(2, *field, dtype=bf16), shape(SLOTS, 26, dtype=jnp.int32)],
+        [table, pad, cols, wide, scratch, pltpu.VMEM((PEERS, C), jnp.int32)]
+        + [
+            pltpu.SMEM((1, SLOTS), jnp.int32),
+            pltpu.SMEM((SLOTS, 26), jnp.int32),
+            pltpu.SMEM((SLOTS, 26), jnp.int32),
+            pltpu.SMEM((PEERS, C), jnp.int32),
+            pltpu.VMEM((1, C), f32),
+            pltpu.VMEM((1, C), f32),
+            pltpu.VMEM((27, C, C), bf16),
+            pltpu.VMEM((27, C, C), bf16),
+            pltpu.SemaphoreType.DMA((8,)),
+        ],
+        (active, owners, positions, gain1, bias1, conv_first, conv_second, stats1, *fields0),
+        [vmem] * 5 + [smem],
+    )
+    fields1, stats2 = exchange(both, stats2)
 
     block, stats3, grad_w2 = call(
         second_kernel,
-        [vmem, vmem, smem, smem, smem, smem] + [vmem] * 10,
+        [vmem, vmem, smem, smem] + [vmem] * 10,
         [shape(*field, dtype=bf16), shape(PEERS, 3 * C), shape(27 * C, C)],
         [table, pad, cols, wide, scratch],
-        (feat, gout, active, owners, positions, ids, middle, gas, stats1, stats2, gain2, bias2)
+        (feat, gout, active, index, middle, gas, stats1, stats2, gain2, bias2)
         + (conv_second, *fields1),
     )
     stats3 = spread(stats3)
 
-    q1, share = call(
+    q1, keep, give = call(
         third_kernel,
-        [vmem, smem, smem, smem, smem] + [vmem] * 15,
-        [shape(*field), shape(2, PEERS // 2, 112, C)],
+        [vmem, smem, smem] + [vmem] * 15,
+        [shape(*field), shape(PEERS // 2, 112, C), shape(PEERS // 2, 112, C)],
         [table, pad, cols, wide, scratch, pltpu.VMEM((27 * C, C), f32)],
-        (feat, active, owners, positions, ids, middle, gas, stats1, stats2, stats3)
+        (feat, active, index, middle, gas, stats1, stats2, stats3)
         + (gain1, bias1, gain2, bias2, conv_first, cols_a, grad_w2, *fields1),
     )
-    share = lax.all_to_all(share, "space", 0, 0, axis_index_groups=core_groups)
+    other = lax.ppermute(give, "space", near_pairs[0])
     (share,) = call(
-        pair_kernel, [vmem], [shape(PEERS // 2, 112, C, dtype=bf16)], [], (share,)
+        pair_kernel,
+        [vmem, vmem],
+        [shape(PEERS // 2, 112, C, dtype=bf16)],
+        [],
+        (keep, other),
     )
     share = lax.all_to_all(share, "space", 0, 0, axis_index_groups=chip_groups)
 

time: 185 us -> 177 us (0.957)
  blocking collectives: 110 us -> 89 us
  starting transfers between devices: 28.1 us -> 45 us
  local copies, waits for them, and re-layouts: 11.6 us -> 9.26 us
  Pallas kernels: 18.7 us -> 16.4 us
    all_to_all x3 -> x2, blocking collectives: 50.2 us -> 36 us  [spread(): return lax.all_to_all(stats, 'space', 0, 0, tiled=True)]
    ppermute x4 -> x5, waiting for transfers between devices: 0.01 us -> 10.1 us  [the longest x4 6.5 us: exchange(): near = [lax.ppermute(three, 'space', pairs) for pairs in near_pairs]]
    all_to_all x0 -> x1, starting transfers between devices: none -> 9.5 us  [spread(): return lax.all_to_all(stats, 'space', 0, 0, tiled=True)]
    ppermute x4, waiting for transfers between devices: 14.5 us -> 5.62 us  [exchange(): far = [lax.ppermute(fields, 'space', pairs) for pairs in far_pairs]]
    all_to_all x1 -> x0, blocking collectives: 6.68 us -> none  [per_device(): share = lax.all_to_all(share, 'space', 0, 0, axis_index_groups=core_groups)]
    ppermute x4 -> x5, starting transfers between devices: 9.69 us -> 14.1 us  [the longest x4 12 us: exchange(): near = [lax.ppermute(three, 'space', pairs) for pairs in near_pairs]]
    ppermute x4, starting transfers between devices: 18.4 us -> 21.4 us  [exchange(): far = [lax.ppermute(fields, 'space', pairs) for pairs in far_pairs]]
    unnamed x44 -> x40, local copies, waits for them, and re-layouts: 10.6 us -> 7.74 us
  transfers between devices with their start and end apart: 8 -> 10, of which waited for: 4 -> 5; matrix products, arithmetic and copies ran while one was open for 0% -> 0% of each run, Pallas kernels for 0% -> 0%
where the time goes in v4:
time: 177 us; the launch traced here: 176 us
  blocking collectives  89 us (50%)
  starting transfers between devices  45 us (25%)
  Pallas kernels  16.4 us (9%)
  waiting for transfers between devices  15.7 us (9%)
  local copies, waits for them, and re-layouts  9.26 us (5%)
    all_to_all x2, blocking collectives, spread(): return lax.all_to_all(stats, 'space', 0, 0, tiled=True)  36 us
    all_to_all x1, blocking collectives, per_device(): share = lax.all_to_all(share, 'space', 0, 0, axis_index_groups=chip_groups)  30.5 us
    all_to_all x1, blocking collectives, per_device(): rows = lax.all_to_all(rows, 'scene', 0, 0)  22.5 us
    ppermute x4, starting transfers between devices, exchange(): far = [lax.ppermute(fields, 'space', pairs) for pairs in far_pairs]  21.4 us
    pallas_call x6, Pallas kernels, call(): pl.pallas_call(kernel, in_specs=specs, out_specs=out_specs or [vmem] * le...  16.4 us
    ppermute x4, starting transfers between devices, exchange(): near = [lax.ppermute(three, 'space', pairs) for pairs in near_pairs]  12 us
    all_to_all x1, starting transfers between devices, spread(): return lax.all_to_all(stats, 'space', 0, 0, tiled=True)  9.5 us
    unnamed x40, local copies, waits for them, and re-layouts  7.74 us
  transfers between devices with their start and end apart: 10, of which 5 were waited for; matrix products, arithmetic and copies ran while one was open for 0% of the time, Pallas kernels for 0%

profile of v4, /device:TPU:66, one launch (start us, length us, event | category | flops | bytes accessed | tf_op | source)
XLA Modules:
  0.0 176.4 jit_solution(12015227928793460647)
XLA Ops:
  0.6 0.0 copy-start
  0.6 0.9 copy.17
  1.5 0.8 copy-done.3
  2.3 0.8 copy-done.5
  3.2 0.7 copy-done.7
  3.8 0.8 shard_map.147
  4.6 10.0 %collective-permute-start.1 = (bf16[2,4,64,128]{3,2,1,0:T(8,128)(2,1)S(1)}, bf16[2,4,64,128]{3,2,1,0:T(8,128)(2,1)S(1)}, u32[]{:S(2)}, u32[]{:S(2)}) collective-permute-start(bf16[2,4,64,128]{3,2,1,0:T(8,128)(2,1)S(1)} %get-tuple-element.26), channel_id=1, source_target_pairs={{4,8},{5,9},{6,10},{7,11},{12,16},{13,17},{14,18},{15,19},{20,24},... | collective-permute-start | bytes 393224 | tf_op jit(solution)/shard_map/ppermute | solution.py:571
  14.6 2.5 %collective-permute-start = (bf16[2,4,64,128]{3,2,1,0:T(8,128)(2,1)S(1)}, bf16[2,4,64,128]{3,2,1,0:T(8,128)(2,1)S(1)}, u32[]{:S(2)}, u32[]{:S(2)}) collective-permute-start(bf16[2,4,64,128]{3,2,1,0:T(8,128)(2,1)S(1)} %get-tuple-element.26), channel_id=1, source_target_pairs={{0,4},{1,5},{2,6},{3,7},{8,12},{9,13},{10,14},{11,15},{16,20},{17,... | collective-permute-start | bytes 393224 | tf_op jit(solution)/shard_map/ppermute | solution.py:571
  17.1 0.1 copy.18
  17.2 16.1 %all_to_all.45 = f32[64,1,256]{2,1,0:T(1,128)S(1)} all-to-all(f32[64,1,256]{2,1,0:T(1,128)S(1)} %copy.18), channel_id=1, replica_groups=mesh['scene'=8,'space'=64] {'space'}, dimensions={0} | all-to-all | bytes 131072 | tf_op jit(solution)/shard_map/all_to_all | solution.py:580
  33.3 0.0 collective-permute-done.1
  33.3 0.0 collective-permute-done
  33.3 2.9 %collective-permute-start.3 = (bf16[3,2,4,64,128]{4,3,2,1,0:T(8,128)(2,1)S(1)}, bf16[3,2,4,64,128]{4,3,2,1,0:T(8,128)(2,1)S(1)}, u32[]{:S(2)}, u32[]{:S(2)}) collective-permute-start(bf16[3,2,4,64,128]{4,3,2,1,0:T(8,128)(2,1)S(1)} %pad_maximum_fusion.rest_0_), channel_id=1, source_target_pairs={{1,2},{3,4},{5,6},{7,8},{9,10},{11,12},{13,14},{15,16},{17,18},{19... | collective-permute-start | bytes 1179656 | tf_op jit(solution)/shard_map/ppermute | solution.py:575
  36.2 1.9 %collective-permute-start.2 = (bf16[3,2,4,64,128]{4,3,2,1,0:T(8,128)(2,1)S(1)}, bf16[3,2,4,64,128]{4,3,2,1,0:T(8,128)(2,1)S(1)}, u32[]{:S(2)}, u32[]{:S(2)}) collective-permute-start(bf16[3,2,4,64,128]{4,3,2,1,0:T(8,128)(2,1)S(1)} %pad_maximum_fusion.rest_0_), channel_id=1, source_target_pairs={{0,1},{2,3},{4,5},{6,7},{8,9},{10,11},{12,13},{14,15},{16,17},{18,... | collective-permute-start | bytes 1179656 | tf_op jit(solution)/shard_map/ppermute | solution.py:575
  38.1 4.3 %collective-permute-done.3.rest_2_ = bf16[3,2,4,64,128]{4,3,2,1,0:T(8,128)(2,1)S(1)} collective-permute-done((bf16[3,2,4,64,128]{4,3,2,1,0:T(8,128)(2,1)S(1)}, bf16[3,2,4,64,128]{4,3,2,1,0:T(8,128)(2,1)S(1)}, u32[]{:S(2)}, u32[]{:S(2)}) %collective-permute-start.3) | collective-permute-done | bytes 393248 | tf_op jit(solution)/shard_map/ppermute | solution.py:575
  42.4 0.0 collective-permute-done.2.rest_1_
  42.4 0.0 copy-done
  42.4 1.2 copy-done.1
  43.6 0.7 copy-done.8
  44.3 0.7 copy-done.10
  44.9 0.7 copy-done.12
  45.6 0.7 copy-done.13
  46.3 0.7 copy-done.14
  46.9 0.0 copy-start.17
  47.0 6.1 %shard_map.148 = (f32[4,64,128]{2,1,0:T(8,128)S(1)}, f32[4,64,128]{2,1,0:T(8,128)S(1)}, bf16[9,4,6,16,128]{4,3,2,1,0:T(8,128)(2,1)S(1)}, f32[64,384]{1,0:T(8,128...) custom-call(s32[1,4]{1,0:T(1,128)S(1)} %copy-done.8, s32[4,26]{1,0:T(4,128)S(1)} %bitcast.54, ...), custom_call_target="tpu_custom_call" | custom-call | tf_op jit(solution)/shard_map/pallas_call | solution.py:547
  53.1 0.7 copy.19
  53.8 9.5 %all-to-all-start.1 = ((f32[64,1,384]{2,1,0:T(1,128)}), f32[64,1,384]{2,1,0:T(1,128)S(1)}, u32[]{:S(2)}, u32[]{:S(2)}) async-start(f32[64,1,384]{2,1,0:T(1,128)} %copy.19), calls=%async_computation.1 | async-start | bytes 196608 | tf_op jit(solution)/shard_map/all_to_all | solution.py:580
  63.3 4.6 %collective-permute-start.5 = (bf16[2,4,64,128]{3,2,1,0:T(8,128)(2,1)S(1)}, bf16[2,4,64,128]{3,2,1,0:T(8,128)(2,1)S(1)}, u32[]{:S(2)}, u32[]{:S(2)}) collective-permute-start(bf16[2,4,64,128]{3,2,1,0:T(8,128)(2,1)S(1)} %get-tuple-element.34), channel_id=1, source_target_pairs={{4,8},{5,9},{6,10},{7,11},{12,16},{13,17},{14,18},{15,19},{20,24},... | collective-permute-start | bytes 393224 | tf_op jit(solution)/shard_map/ppermute | solution.py:571
  67.9 4.4 %collective-permute-start.4 = (bf16[2,4,64,128]{3,2,1,0:T(8,128)(2,1)S(1)}, bf16[2,4,64,128]{3,2,1,0:T(8,128)(2,1)S(1)}, u32[]{:S(2)}, u32[]{:S(2)}) collective-permute-start(bf16[2,4,64,128]{3,2,1,0:T(8,128)(2,1)S(1)} %get-tuple-element.34), channel_id=1, source_target_pairs={{0,4},{1,5},{2,6},{3,7},{8,12},{9,13},{10,14},{11,15},{16,20},{17,... | collective-permute-start | bytes 393224 | tf_op jit(solution)/shard_map/ppermute | solution.py:571
  72.3 0.0 all-to-all-done.1
  72.3 4.5 %collective-permute-done.5 = bf16[2,4,64,128]{3,2,1,0:T(8,128)(2,1)S(1)} collective-permute-done((bf16[2,4,64,128]{3,2,1,0:T(8,128)(2,1)S(1)}, bf16[2,4,64,128]{3,2,1,0:T(8,128)(2,1)S(1)}, u32[]{:S(2)}, u32[]{:S(2)}) %collective-permute-start.5) | collective-permute-done | bytes 131104 | tf_op jit(solution)/shard_map/ppermute | solution.py:571
  76.7 1.2 collective-permute-done.4
  78.0 4.0 %collective-permute-start.7 = (bf16[3,2,4,64,128]{4,3,2,1,0:T(8,128)(2,1)S(1)}, bf16[3,2,4,64,128]{4,3,2,1,0:T(8,128)(2,1)S(1)}, u32[]{:S(2)}, u32[]{:S(2)}) collective-permute-start(bf16[3,2,4,64,128]{4,3,2,1,0:T(8,128)(2,1)S(1)} %pad_maximum_fusion.1.rest_0_), channel_id=1, source_target_pairs={{1,2},{3,4},{5,6},{7,8},{9,10},{11,12},{13,14},{15,16},{17,18},{19... | collective-permute-start | bytes 1179656 | tf_op jit(solution)/shard_map/ppermute | solution.py:575
  81.9 3.2 %collective-permute-start.6 = (bf16[3,2,4,64,128]{4,3,2,1,0:T(8,128)(2,1)S(1)}, bf16[3,2,4,64,128]{4,3,2,1,0:T(8,128)(2,1)S(1)}, u32[]{:S(2)}, u32[]{:S(2)}) collective-permute-start(bf16[3,2,4,64,128]{4,3,2,1,0:T(8,128)(2,1)S(1)} %pad_maximum_fusion.1.rest_0_), channel_id=1, source_target_pairs={{0,1},{2,3},{4,5},{6,7},{8,9},{10,11},{12,13},{14,15},{16,17},{18,... | collective-permute-start | bytes 1179656 | tf_op jit(solution)/shard_map/ppermute | solution.py:575
  85.2 2.2 %collective-permute-done.7.rest_2_ = bf16[3,2,4,64,128]{4,3,2,1,0:T(8,128)(2,1)S(1)} collective-permute-done((bf16[3,2,4,64,128]{4,3,2,1,0:T(8,128)(2,1)S(1)}, bf16[3,2,4,64,128]{4,3,2,1,0:T(8,128)(2,1)S(1)}, u32[]{:S(2)}, u32[]{:S(2)}) %collective-permute-start.7) | collective-permute-done | bytes 393248 | tf_op jit(solution)/shard_map/ppermute | solution.py:575
  87.4 0.0 collective-permute-done.6.rest_1_
  87.4 0.0 copy-done.4
  87.4 3.7 %shard_map.149 = (bf16[4,64,128]{2,1,0:T(8,128)(2,1)}, f32[64,384]{1,0:T(8,128)S(1)}, f32[3456,128]{1,0:T(8,128)S(1)}) custom-call(bf16[4,64,128]{2,1,0:T(8,128)(2,1)S(1)} %bitcast.37, bf16[4,64,128]{2,1,0:T(8,128)(2,1)S(1)} %bitcast.43, s32[1,4]{1,0:T(1,128)S(1)} %copy-done.9, s32[4,26]{1,0:T(4,128)S(1)} %get-tuple-element.31.index, ...), custom_call_target="tpu_custom_call" | custom-call | tf_op jit(solution)/shard_map/pallas_call | solution.py:547
  91.1 0.1 copy.20
  91.2 20.0 %all_to_all.46 = f32[64,1,384]{2,1,0:T(1,128)S(1)} all-to-all(f32[64,1,384]{2,1,0:T(1,128)S(1)} %copy.20), channel_id=1, replica_groups=mesh['scene'=8,'space'=64] {'space'}, dimensions={0} | all-to-all | bytes 196608 | tf_op jit(solution)/shard_map/all_to_all | solution.py:580
  111.2 4.0 %shard_map.150 = (f32[4,64,128]{2,1,0:T(8,128)S(1)}, f32[32,112,128]{2,1,0:T(8,128)S(1)}, f32[32,112,128]{2,1,0:T(8,128)S(1)}) custom-call(bf16[4,64,128]{2,1,0:T(8,128)(2,1)S(1)} %bitcast.38, s32[1,4]{1,0:T(1,128)S(1)} %copy-done.9, s32[4,26]{1,0:T(4,128)S(1)} %get-tuple-element.31.index, f32[4,64,128]{2,1,0:T(8,128)S(1)} %get-tuple-element.32.middle, ...), custom_call_target="tpu_custom_call" | custom-call | tf_op jit(solution)/shard_map/pallas_call | solution.py:547
  115.2 2.1 %collective-permute-start.8 = (f32[32,112,128]{2,1,0:T(8,128)S(1)}, f32[32,112,128]{2,1,0:T(8,128)S(1)}, u32[]{:S(2)}, u32[]{:S(2)}) collective-permute-start(f32[32,112,128]{2,1,0:T(8,128)S(1)} %get-tuple-element.45), channel_id=1, source_target_pairs={{0,1},{2,3},{4,5},{6,7},{8,9},{10,11},{12,13},{14,15},{16,17},{18,... | collective-permute-start | bytes 5505032 | tf_op jit(solution)/shard_map/ppermute | solution.py:668
  117.3 3.6 %collective-permute-done.8.other = f32[32,112,128]{2,1,0:T(8,128)S(1)} collective-permute-done((f32[32,112,128]{2,1,0:T(8,128)S(1)}, f32[32,112,128]{2,1,0:T(8,128)S(1)}, u32[]{:S(2)}, u32[]{:S(2)}) %collective-permute-start.8) | collective-permute-done | bytes 1835040 | tf_op jit(solution)/shard_map/ppermute | solution.py:668
  120.8 0.2 shard_map.151
  121.1 30.5 %all_to_all.47.parts = bf16[32,112,128]{2,1,0:T(8,128)(2,1)S(1)} all-to-all(bf16[32,112,128]{2,1,0:T(8,128)(2,1)S(1)} %shard_map.151), channel_id=1, replica_groups={{0,2,4,6,8,10,12,14,16,18,20,22,24,26,28,30,32,34,36,38,40,42,44,46,48,..., dimensions={0} | all-to-all | bytes 1835008 | tf_op jit(solution)/shard_map/all_to_all | solution.py:676
  151.6 1.6 shard_map.152
  153.3 22.5 %all_to_all.48 = f32[8,112,128]{2,1,0:T(8,128)S(1)} all-to-all(f32[8,112,128]{2,1,0:T(8,128)S(1)} %get-tuple-element.47), channel_id=1, replica_groups=mesh['scene'=8,'space'=64] {'scene'}, dimensions={0} | all-to-all | bytes 917504 | tf_op jit(solution)/shard_map/all_to_all | solution.py:685
  175.8 0.6 fusion
  (29 shorter events, 0.2 us)
Async XLA Ops:
  0.6 41.8 %copy-start = (bf16[27,128,128]{2,1,0:T(8,128)(2,1)S(1)}, bf16[27,128,128]{2,1,0:T(8,128)(2,1)}, u32[]{:S(2)}) copy-start(bf16[27,128,128]{2,1,0:T(8,128)(2,1)} %w2.1) | copy-start | bytes 2654212
  1.5 0.8 copy-start.3
  2.3 0.8 copy-start.5
  3.2 0.7 copy-start.7
  4.6 28.7 %collective-permute-start.1 = (bf16[2,4,64,128]{3,2,1,0:T(8,128)(2,1)S(1)}, bf16[2,4,64,128]{3,2,1,0:T(8,128)(2,1)S(1)}, u32[]{:S(2)}, u32[]{:S(2)}) collective-permute-start(bf16[2,4,64,128]{3,2,1,0:T(8,128)(2,1)S(1)} %get-tuple-element.26), channel_id=1, source_target_pairs={{4,8},{5,9},{6,10},{7,11},{12,16},{13,17},{14,18},{15,19},{20,24},... | collective-permute-start | bytes 393224 | tf_op jit(solution)/shard_map/ppermute | solution.py:571
  14.6 18.6 %collective-permute-start = (bf16[2,4,64,128]{3,2,1,0:T(8,128)(2,1)S(1)}, bf16[2,4,64,128]{3,2,1,0:T(8,128)(2,1)S(1)}, u32[]{:S(2)}, u32[]{:S(2)}) collective-permute-start(bf16[2,4,64,128]{3,2,1,0:T(8,128)(2,1)S(1)} %get-tuple-element.26), channel_id=1, source_target_pairs={{0,4},{1,5},{2,6},{3,7},{8,12},{9,13},{10,14},{11,15},{16,20},{17,... | collective-permute-start | bytes 393224 | tf_op jit(solution)/shard_map/ppermute | solution.py:571
  33.3 9.1 %collective-permute-start.3 = (bf16[3,2,4,64,128]{4,3,2,1,0:T(8,128)(2,1)S(1)}, bf16[3,2,4,64,128]{4,3,2,1,0:T(8,128)(2,1)S(1)}, u32[]{:S(2)}, u32[]{:S(2)}) collective-permute-start(bf16[3,2,4,64,128]{4,3,2,1,0:T(8,128)(2,1)S(1)} %pad_maximum_fusion.rest_0_), channel_id=1, source_target_pairs={{1,2},{3,4},{5,6},{7,8},{9,10},{11,12},{13,14},{15,16},{17,18},{19... | collective-permute-start | bytes 1179656 | tf_op jit(solution)/shard_map/ppermute | solution.py:575
  36.2 6.2 %collective-permute-start.2 = (bf16[3,2,4,64,128]{4,3,2,1,0:T(8,128)(2,1)S(1)}, bf16[3,2,4,64,128]{4,3,2,1,0:T(8,128)(2,1)S(1)}, u32[]{:S(2)}, u32[]{:S(2)}) collective-permute-start(bf16[3,2,4,64,128]{4,3,2,1,0:T(8,128)(2,1)S(1)} %pad_maximum_fusion.rest_0_), channel_id=1, source_target_pairs={{0,1},{2,3},{4,5},{6,7},{8,9},{10,11},{12,13},{14,15},{16,17},{18,... | collective-permute-start | bytes 1179656 | tf_op jit(solution)/shard_map/ppermute | solution.py:575
  42.4 1.2 copy-start.1
  43.6 0.7 copy-start.8
  44.3 0.7 copy-start.10
  44.9 0.7 copy-start.12
  45.6 0.7 copy-start.13
  46.3 0.7 copy-start.14
  46.9 40.4 %copy-start.4 = (bf16[1,4,64,128]{3,2,1,0:T(8,128)(2,1)S(1)}, bf16[1,4,64,128]{3,2,1,0:T(8,128)(2,1)}, u32[]{:S(2)}) copy-start(bf16[1,4,64,128]{3,2,1,0:T(8,128)(2,1)} %param.12) | copy-start | bytes 196612
  46.9 40.4 %copy-start.6 = (bf16[1,4,64,128]{3,2,1,0:T(8,128)(2,1)S(1)}, bf16[1,4,64,128]{3,2,1,0:T(8,128)(2,1)}, u32[]{:S(2)}) copy-start(bf16[1,4,64,128]{3,2,1,0:T(8,128)(2,1)} %param.23) | copy-start | bytes 196612
  46.9 40.4 %copy-start.9 = (s32[1,4]{1,0:T(1,128)S(1)}, s32[1,4]{1,0:T(1,128)}, u32[]{:S(2)}) copy-start(s32[1,4]{1,0:T(1,128)} %active.5) | copy-start | bytes 52
  46.9 40.4 %copy-start.16 = (f32[128]{0:T(128)S(1)}, f32[128]{0:T(128)}, u32[]{:S(2)}) copy-start(f32[128]{0:T(128)} %param.21) | copy-start | bytes 1540
  46.9 40.5 %copy-start.17 = (f32[128]{0:T(128)S(1)}, f32[128]{0:T(128)}, u32[]{:S(2)}) copy-start(f32[128]{0:T(128)} %param.22) | copy-start | bytes 1540
  53.8 18.4 %all-to-all-start.1 = ((f32[64,1,384]{2,1,0:T(1,128)}), f32[64,1,384]{2,1,0:T(1,128)S(1)}, u32[]{:S(2)}, u32[]{:S(2)}) async-start(f32[64,1,384]{2,1,0:T(1,128)} %copy.19), calls=%async_computation.1 | async-start | bytes 196608 | tf_op jit(solution)/shard_map/all_to_all | solution.py:580
  63.3 13.4 %collective-permute-start.5 = (bf16[2,4,64,128]{3,2,1,0:T(8,128)(2,1)S(1)}, bf16[2,4,64,128]{3,2,1,0:T(8,128)(2,1)S(1)}, u32[]{:S(2)}, u32[]{:S(2)}) collective-permute-start(bf16[2,4,64,128]{3,2,1,0:T(8,128)(2,1)S(1)} %get-tuple-element.34), channel_id=1, source_target_pairs={{4,8},{5,9},{6,10},{7,11},{12,16},{13,17},{14,18},{15,19},{20,24},... | collective-permute-start | bytes 393224 | tf_op jit(solution)/shard_map/ppermute | solution.py:571
  67.9 10.0 %collective-permute-start.4 = (bf16[2,4,64,128]{3,2,1,0:T(8,128)(2,1)S(1)}, bf16[2,4,64,128]{3,2,1,0:T(8,128)(2,1)S(1)}, u32[]{:S(2)}, u32[]{:S(2)}) collective-permute-start(bf16[2,4,64,128]{3,2,1,0:T(8,128)(2,1)S(1)} %get-tuple-element.34), channel_id=1, source_target_pairs={{0,4},{1,5},{2,6},{3,7},{8,12},{9,13},{10,14},{11,15},{16,20},{17,... | collective-permute-start | bytes 393224 | tf_op jit(solution)/shard_map/ppermute | solution.py:571
  77.9 33.3 %copy-start.2 = (bf16[27,128,128]{2,1,0:T(8,128)(2,1)S(1)}, bf16[27,128,128]{2,1,0:T(8,128)(2,1)}, u32[]{:S(2)}) copy-start(bf16[27,128,128]{2,1,0:T(8,128)(2,1)} %w1.1) | copy-start | bytes 2654212
  77.9 33.3 %copy-start.11 = (f32[128]{0:T(128)S(1)}, f32[128]{0:T(128)}, u32[]{:S(2)}) copy-start(f32[128]{0:T(128)} %param.19) | copy-start | bytes 1540
  77.9 33.3 %copy-start.15 = (f32[128]{0:T(128)S(1)}, f32[128]{0:T(128)}, u32[]{:S(2)}) copy-start(f32[128]{0:T(128)} %param.20) | copy-start | bytes 1540
  78.0 9.4 %collective-permute-start.7 = (bf16[3,2,4,64,128]{4,3,2,1,0:T(8,128)(2,1)S(1)}, bf16[3,2,4,64,128]{4,3,2,1,0:T(8,128)(2,1)S(1)}, u32[]{:S(2)}, u32[]{:S(2)}) collective-permute-start(bf16[3,2,4,64,128]{4,3,2,1,0:T(8,128)(2,1)S(1)} %pad_maximum_fusion.1.rest_0_), channel_id=1, source_target_pairs={{1,2},{3,4},{5,6},{7,8},{9,10},{11,12},{13,14},{15,16},{17,18},{19... | collective-permute-start | bytes 1179656 | tf_op jit(solution)/shard_map/ppermute | solution.py:575
  81.9 5.4 %collective-permute-start.6 = (bf16[3,2,4,64,128]{4,3,2,1,0:T(8,128)(2,1)S(1)}, bf16[3,2,4,64,128]{4,3,2,1,0:T(8,128)(2,1)S(1)}, u32[]{:S(2)}, u32[]{:S(2)}) collective-permute-start(bf16[3,2,4,64,128]{4,3,2,1,0:T(8,128)(2,1)S(1)} %pad_maximum_fusion.1.rest_0_), channel_id=1, source_target_pairs={{0,1},{2,3},{4,5},{6,7},{8,9},{10,11},{12,13},{14,15},{16,17},{18,... | collective-permute-start | bytes 1179656 | tf_op jit(solution)/shard_map/ppermute | solution.py:575
  115.2 5.7 %collective-permute-start.8 = (f32[32,112,128]{2,1,0:T(8,128)S(1)}, f32[32,112,128]{2,1,0:T(8,128)S(1)}, u32[]{:S(2)}, u32[]{:S(2)}) collective-permute-start(f32[32,112,128]{2,1,0:T(8,128)S(1)} %get-tuple-element.45), channel_id=1, source_target_pairs={{0,1},{2,3},{4,5},{6,7},{8,9},{10,11},{12,13},{14,15},{16,17},{18,... | collective-permute-start | bytes 5505032 | tf_op jit(solution)/shard_map/ppermute | solution.py:668

commit v5 on v4

--- a/solution.py
+++ b/solution.py
@@ -13,6 +13,9 @@
 PEERS = 64
 PLANE = 16
 SHARE = 54
+ROWS = 128
+SUM_ROW = 108
+CENTRE_ROW = 112
 GROUP_COUNT = 64 * 4
 EPS = 1e-05
 
@@ -50,9 +53,8 @@
     return group_total(jnp.where(lane % 4 == n, packed, 0.0))
 
 
-def total_of(stats_ref, part=0):
-    row = jnp.sum(stats_ref[:, C * part : C * (part + 1)], axis=0, keepdims=True)
-    return jnp.broadcast_to(row, (8, C))
+def total_of(stats_ref):
+    return jnp.broadcast_to(jnp.sum(stats_ref[...], axis=0, keepdims=True), (8, C))
 
 
 def norm_stats(stats_ref):
@@ -235,38 +237,23 @@
     return rows
 
 
-def store_shares(rows, out, part):
+def store_shares(rows, out):
     lane = lax.broadcasted_iota(jnp.int32, (1, C), 1)
     for p in range(PEERS):
         k, skip = divmod(SHARE * p, C)
         line = rows[k] if skip == 0 else pltpu.roll(rows[k], C - skip, 1)
         if skip + SHARE > C:
             line = jnp.where(lane < C - skip, line, pltpu.roll(rows[k + 1], C - skip, 1))
-        line = jnp.where(lane < SHARE, line, 0.0)
-        out[p : p + 1, C * part : C * (part + 1)] = line
-
-
-def grad_centre(stats1, count):
-    return total_of(stats1, 1)[0:1] / (count / 4)
-
-
-def middle_centre(stats2, stats3, count, mean, inv, mean_q, mean_c):
-    voxels = count / 4
-    sum_hat = (total_of(stats2, 1)[0:1] - voxels * mean) * inv
-    sum_q = total_of(stats3, 1)[0:1]
-    return inv * (sum_q - voxels * mean_q - sum_hat * mean_c) / voxels
-
-
-def outer(shares, centre):
-    first = lax.broadcasted_iota(jnp.int32, (8, C), 0) == 0
-    left = jnp.where(first, jnp.broadcast_to(shares, (8, C)), 0.0)
-    return lax.dot_general(
-        left,
-        jnp.broadcast_to(centre, (8, C)),
-        (((0,), (0,)), ((), ())),
-        precision=lax.Precision.HIGHEST,
-        preferred_element_type=f32,
-    )
+        out[p : p + 1] = jnp.where(lane < SHARE, line, 0.0)
+
+
+def centre_of(field, active):
+    total = jnp.zeros((1, C), f32)
+    slots = 0.0
+    for s in range(SLOTS):
+        total = total + jnp.sum(field[s], axis=0, keepdims=True)
+        slots = slots + slot_weight(active, s)
+    return (total / (jnp.maximum(slots, 1.0) * VOX)).astype(bf16).astype(f32)
 
 
 def start_kernel(feat_in, gout_in, active_in, list_in, stats, both, active, send_list, sems):
@@ -278,12 +265,10 @@
         copy.wait()
     total = jnp.zeros((1, C), f32)
     squares = jnp.zeros((1, C), f32)
-    grads = jnp.zeros((1, C), f32)
     slots = 0.0
     for s in range(SLOTS):
         w = slot_weight(active, s)
         x = feat[s].astype(f32)
-        grads = grads + w * jnp.sum(gout[s].astype(f32), axis=0, keepdims=True)
         total = total + w * jnp.sum(x, axis=0, keepdims=True)
         squares = squares + w * jnp.sum(x * x, axis=0, keepdims=True)
         slots = slots + w
@@ -291,25 +276,29 @@
     record = lax.broadcasted_iota(jnp.int32, (CAP, C), 0)
     lane = lax.broadcasted_iota(jnp.int32, (CAP, C), 1)
     select = jnp.where(lane == 4 * record + 3, 1.0, 0.0).astype(bf16)
-    ids = jnp.dot(send_list[...].astype(bf16), select, preferred_element_type=f32)
-    stats[:, 0:C] = ids + packed[0:1]
-    stats[:, C : 2 * C] = jnp.broadcast_to(grads, (PEERS, C))
+    ids = lax.dot_general(
+        send_list[:, 0].astype(bf16),
+        select,
+        (((0,), (0,)), ((), ())),
+        preferred_element_type=f32,
+    )
+    stats[...] = ids + packed[0:1]
 
 
 def first_kernel(
     active_in, own_in, pos_in, gain_in, bias_in, w1_in, w2_in, stats1, *rest
 ):
     fields, rest = rest[:3], rest[3:]
-    middle, gas, cols_a, stats2, both, index = rest[:6]
-    table, pad, cols_g, act, scratch, ids_v = rest[6:12]
-    active, owners, positions, ids, gain1, bias1, w1, w2, sems = rest[12:]
+    middle, gas, cols_a, both, index = rest[:5]
+    table, pad, cols_g, act, scratch, ids_v = rest[5:11]
+    active, owners, positions, ids, gain1, bias1, w1, w2, sems = rest[11:]
     me = lax.axis_index("space")
     copies = fetch(
         (gain_in, bias_in, active_in, own_in, pos_in, w1_in, w2_in),
         (gain1, bias1, active, owners, positions, w1, w2),
         sems,
     )
-    ids_v[...] = stats1[:, 0:C].astype(jnp.int32)
+    ids_v[...] = stats1[...].astype(jnp.int32)
     ids_copy = pltpu.make_async_copy(ids_v, ids, sems.at[7])
     ids_copy.start()
     feat, gout = fields[0].at[0, 0], fields[0].at[0, 1]
@@ -343,6 +332,9 @@
     gas[...] = conv_back(cols_g, w2).reshape(SLOTS, VOX, C)
     both[0] = middle[...].astype(bf16)
     both[1] = gas[...].astype(bf16)
+
+
+def sums_kernel(active, middle, stats2):
     total = jnp.zeros((1, C), f32)
     squares = jnp.zeros((1, C), f32)
     slots = 0.0
@@ -353,9 +345,7 @@
         squares = squares + w * jnp.sum(x * x, axis=0, keepdims=True)
         slots = slots + w
     packed = pack_stats([total, squares, jnp.full((1, C), slots, f32)])
-    stats2[:, 0:C] = jnp.broadcast_to(packed[0:1], (PEERS, C))
-    stats2[:, C : 2 * C] = jnp.broadcast_to(total, (PEERS, C))
-    store_shares(window_sums(cols_a), stats2, 2)
+    stats2[...] = jnp.broadcast_to(packed[0:1], (PEERS, C))
 
 
 def second_kernel(
@@ -365,7 +355,6 @@
     index,
     middle,
     gas,
-    stats1,
     stats2,
     gain2,
     bias2,
@@ -373,9 +362,9 @@
     *rest,
 ):
     fields, rest = rest[:3], rest[3:]
-    block, stats3, grad_w, table, pad, cols, act, scratch = rest
+    block, stats3, grad_w, sums2, centre2, table, pad, cols, act, scratch = rest
     me = lax.axis_index("space")
-    mean, inv, count = norm_stats(stats2)
+    mean, inv, _ = norm_stats(stats2)
     gain = gain2[...]
     bias = bias2[...]
 
@@ -396,18 +385,18 @@
         sum_q = sum_q + jnp.sum(q, axis=0, keepdims=True)
         sum_c = sum_c + jnp.sum(q * hat, axis=0, keepdims=True)
     packed = pack_stats([sum_q, sum_c])
-    stats3[:, 0:C] = jnp.broadcast_to(packed[0:1], (PEERS, C))
-    stats3[:, C : 2 * C] = jnp.broadcast_to(sum_q, (PEERS, C))
+    stats3[...] = jnp.broadcast_to(packed[0:1], (PEERS, C))
     place_interior(pad, act)
     place_halo(pad, table, index)
     windows_of(pad, cols)
-    store_shares(window_sums(cols), stats3, 2)
+    store_shares(window_sums(cols), sums2)
     out = conv(cols, w2).reshape(SLOTS, VOX, C)
     for s in range(SLOTS):
         w = slot_weight(active, s)
         block[s] = ((feat[s].astype(f32) + out[s]) * w).astype(bf16)
         act[s] = jnp.where(active[0, s] > 0, gout[s].astype(f32), 0.0)
-    centre = grad_centre(stats1, count)
+    centre = centre_of(act, active)
+    centre2[...] = jnp.broadcast_to(centre, (8, C))
     weight_grad(cols, act[...].astype(bf16).reshape(SLOTS * VOX, C), centre, grad_w)
 
 
@@ -427,10 +416,12 @@
     w1,
     cols_a,
     grad_w2,
+    sums2,
+    centre2,
     *rest,
 ):
     fields, rest = rest[:3], rest[3:]
-    q1, keep, give, table, pad, cols, act, scratch, grad_w1 = rest
+    q1, keep, give, table, pad, cols, act, scratch, grad_w1, sums1 = rest
     me = lax.axis_index("space")
     mean, inv, count = norm_stats(stats2)
     gain = gain2[...]
@@ -471,17 +462,22 @@
         sum_q = sum_q + jnp.sum(q, axis=0, keepdims=True)
         sum_c = sum_c + jnp.sum(q * hat, axis=0, keepdims=True)
     packed = pack_stats([sum_q, sum_c])
-    centre = middle_centre(stats2, stats3, count, mean, inv, mean_q, mean_c)
+    centre = centre_of(act, active)
+    store_shares(window_sums(cols_a), sums1)
     weight_grad(cols_a, act[...].astype(bf16).reshape(SLOTS * VOX, C), centre, grad_w1)
 
     def store(out, core):
         for chip in range(PEERS // 2):
-            start = SHARE * (2 * chip + core)
-            out[chip, 0:SHARE] = grad_w1[start : start + SHARE]
-            out[chip, 56 : 56 + SHARE] = grad_w2[start : start + SHARE]
-            out[chip, SHARE : SHARE + 1] = packed[0:1]
-            out[chip, SHARE + 1 : SHARE + 2] = packed[0:1]
-            out[chip, 56 + SHARE : 112] = jnp.zeros((2, C), f32)
+            p = 2 * chip + core
+            out[chip, 0:SHARE] = grad_w1[SHARE * p : SHARE * (p + 1)]
+            out[chip, SHARE : 2 * SHARE] = grad_w2[SHARE * p : SHARE * (p + 1)]
+            out[chip, SUM_ROW : SUM_ROW + 1] = packed[0:1]
+            out[chip, SUM_ROW + 1 : CENTRE_ROW] = jnp.zeros((3, C), f32)
+            out[chip, CENTRE_ROW : CENTRE_ROW + 1] = sums1[p : p + 1]
+            out[chip, CENTRE_ROW + 1 : CENTRE_ROW + 2] = centre
+            out[chip, CENTRE_ROW + 2 : CENTRE_ROW + 3] = sums2[p : p + 1]
+            out[chip, CENTRE_ROW + 3 : CENTRE_ROW + 4] = centre2[0:1]
+            out[chip, CENTRE_ROW + 4 : 120] = jnp.zeros((4, C), f32)
 
     @pl.when(me % 2 == 0)
     def _():
@@ -495,28 +491,35 @@
 
 
 def pair_kernel(own, other, out):
+    def terms(row, count):
+        parts = []
+        for _ in range(count):
+            parts.append(row.astype(bf16).astype(f32))
+            row = row - parts[-1]
+        return parts
+
     for n in range(PEERS // 2):
-        total = own[n] + other[n]
-        row = total[SHARE : SHARE + 1]
-        high = row.astype(bf16)
-        left = row - high.astype(f32)
-        middle = left.astype(bf16)
-        low = (left - middle.astype(f32)).astype(bf16)
-        at = lax.broadcasted_iota(jnp.int32, (112, C), 0)
-        total = jnp.where(at == SHARE, high.astype(f32), total)
-        total = jnp.where(at == SHARE + 1, middle.astype(f32), total)
-        total = jnp.where(at == 56 + SHARE, low.astype(f32), total)
-        out[n] = total.astype(bf16)
-
-
-def last_kernel(
-    feat, gout, active, stats1, stats2, stats3, q1, parts, gain1, grad_in, rows
-):
+        total = own[n, 0:CENTRE_ROW] + other[n, 0:CENTRE_ROW]
+        at = lax.broadcasted_iota(jnp.int32, (CENTRE_ROW, C), 0)
+        for k, term in enumerate(terms(total[SUM_ROW : SUM_ROW + 1], 3)):
+            total = jnp.where(at == SUM_ROW + k, term, total)
+        out[n, 0:CENTRE_ROW] = total.astype(bf16)
+        more = jnp.zeros((16, C), f32)
+        at = lax.broadcasted_iota(jnp.int32, (16, C), 0)
+        for core, ref in enumerate((own, other)):
+            rows = ref[n, CENTRE_ROW : CENTRE_ROW + 8]
+            lines = terms(rows[0:1], 2) + [rows[1:2]] + terms(rows[2:3], 2) + [rows[3:4]]
+            for k, line in enumerate(lines):
+                more = jnp.where(at == 6 * core + k, line, more)
+        out[n, CENTRE_ROW:ROWS] = more.astype(bf16)
+
+
+def last_kernel(feat, gout, active, stats1, q1, parts, gain1, grad_in, rows):
     total = parts[0].astype(f32)
     for n in range(1, PEERS // 2):
         total = total + parts[n].astype(f32)
     mean1, inv1, count = norm_stats(stats1)
-    packed = total[SHARE : SHARE + 1] + total[SHARE + 1 : SHARE + 2] + total[110:111]
+    packed = jnp.sum(total[SUM_ROW : SUM_ROW + 3], axis=0, keepdims=True)
     packed = jnp.broadcast_to(packed, (8, C))
     mean_q = unpack_stat(packed, 0)[0:1] / count
     mean_c = unpack_stat(packed, 1)[0:1] / count
@@ -525,25 +528,39 @@
         back = slot_weight(active, s) * inv1 * (q1[s] - mean_q - hat * mean_c)
         top = jnp.where(active[0, s] > 0, gout[s].astype(f32), 0.0)
         grad_in[s] = (top + back).astype(bf16)
-    mean, inv, _ = norm_stats(stats2)
-    packed = total_of(stats3)
-    mean_q = unpack_stat(packed, 0)[0:1] / count
-    mean_c = unpack_stat(packed, 1)[0:1] / count
-    centre1 = middle_centre(stats2, stats3, count, mean, inv, mean_q, mean_c)
-    centre2 = grad_centre(stats1, count)
-    first = total[0:56] + outer(total_of(stats2, 2)[0:1], centre1)[0:56]
-    second = total[56:112] + outer(total_of(stats3, 2)[0:1], centre2)[0:56]
-    for n in range(8):
-        rows[n, 0:56] = first
-        rows[n, 56:112] = second
+    left = [[], []]
+    right = [[], []]
+    for n in range(PEERS // 2):
+        more = parts[n, CENTRE_ROW:ROWS].astype(f32)
+        for core in range(2):
+            for weight in range(2):
+                first = 6 * core + 3 * weight
+                line = more[first + 2 : first + 3]
+                left[weight] += [more[first : first + 1], more[first + 1 : first + 2]]
+                right[weight] += [line, line]
+    for weight in range(2):
+        outer = lax.dot_general(
+            jnp.concatenate(left[weight], axis=0).astype(bf16),
+            jnp.concatenate(right[weight], axis=0).astype(bf16),
+            (((0,), (0,)), ((), ())),
+            preferred_element_type=f32,
+        )
+        whole = total[SHARE * weight : SHARE * (weight + 1)] + outer[0:SHARE]
+        for n in range(8):
+            rows[n, 56 * weight : 56 * weight + SHARE] = whole
+            rows[n, 56 * weight + SHARE : 56 * weight + 56] = jnp.zeros((2, C), f32)
 
 
 vmem = pl.BlockSpec(memory_space=pltpu.VMEM)
 smem = pl.BlockSpec(memory_space=pltpu.SMEM)
-hbm = pl.BlockSpec(memory_space=pl.ANY)
+hbm = pl.BlockSpec(memory_space=pltpu.HBM)
 
 
 def call(kernel, specs, out_shape, scratch, args, out_specs=None):
+    args = [
+        pltpu.with_memory_space_constraint(arg, pltpu.HBM) if spec is hbm else arg
+        for spec, arg in zip(specs, args)
+    ]
     return pl.pallas_call(
         kernel,
         in_specs=specs,
@@ -601,7 +618,7 @@
     gout = grad_output[0]
     owners = neighbor_owner[0]
     positions = record_position[0]
-    lists = send_list[0, 0]
+    lists = send_list[0].transpose(2, 0, 1)
     gain1, bias1 = gain_first.reshape(1, C), bias_first.reshape(1, C)
     gain2, bias2 = gain_second.reshape(1, C), bias_second.reshape(1, C)
     field = (SLOTS, VOX, C)
@@ -615,20 +632,20 @@
     stats1, both = call(
         start_kernel,
         [hbm, hbm, hbm, hbm],
-        [shape(PEERS, 2 * C), shape(2, *field, dtype=bf16)],
+        [shape(PEERS, C), shape(2, *field, dtype=bf16)],
         [
             pltpu.SMEM((1, SLOTS), jnp.int32),
-            pltpu.VMEM((PEERS, CAP), jnp.int32),
+            pltpu.VMEM((CAP, 1, PEERS), jnp.int32),
             pltpu.SemaphoreType.DMA((4,)),
         ],
         (feat, gout, active, lists),
     )
     fields0, stats1 = exchange(both, stats1)
 
-    middle, gas, cols_a, stats2, both, index = call(
+    middle, gas, cols_a, both, index = call(
         first_kernel,
         [hbm] * 7 + [vmem] * 4,
-        [shape(*field), shape(*field), shape(*cols_shape, dtype=bf16), shape(PEERS, 3 * C)]
+        [shape(*field), shape(*field), shape(*cols_shape, dtype=bf16)]
         + [shape(2, *field, dtype=bf16), shape(SLOTS, 26, dtype=jnp.int32)],
         [table, pad, cols, wide, scratch, pltpu.VMEM((PEERS, C), jnp.int32)]
         + [
@@ -643,33 +660,36 @@
             pltpu.SemaphoreType.DMA((8,)),
         ],
         (active, owners, positions, gain1, bias1, conv_first, conv_second, stats1, *fields0),
-        [vmem] * 5 + [smem],
-    )
+        [vmem] * 4 + [smem],
+    )
+    (stats2,) = call(sums_kernel, [smem, vmem], [shape(PEERS, C)], [], (active, middle))
     fields1, stats2 = exchange(both, stats2)
 
-    block, stats3, grad_w2 = call(
+    block, stats3, grad_w2, sums2, centre2 = call(
         second_kernel,
-        [vmem, vmem, smem, smem] + [vmem] * 10,
-        [shape(*field, dtype=bf16), shape(PEERS, 3 * C), shape(27 * C, C)],
+        [vmem, vmem, smem, smem] + [vmem] * 9,
+        [shape(*field, dtype=bf16), shape(PEERS, C), shape(27 * C, C)]
+        + [shape(PEERS, C), shape(8, C)],
         [table, pad, cols, wide, scratch],
-        (feat, gout, active, index, middle, gas, stats1, stats2, gain2, bias2)
+        (feat, gout, active, index, middle, gas, stats2, gain2, bias2)
         + (conv_second, *fields1),
     )
     stats3 = spread(stats3)
 
     q1, keep, give = call(
         third_kernel,
-        [vmem, smem, smem] + [vmem] * 15,
-        [shape(*field), shape(PEERS // 2, 112, C), shape(PEERS // 2, 112, C)],
-        [table, pad, cols, wide, scratch, pltpu.VMEM((27 * C, C), f32)],
+        [vmem, smem, smem] + [vmem] * 17,
+        [shape(*field), shape(PEERS // 2, 120, C), shape(PEERS // 2, 120, C)],
+        [table, pad, cols, wide, scratch, pltpu.VMEM((27 * C, C), f32)]
+        + [pltpu.VMEM((PEERS, C), f32)],
         (feat, active, index, middle, gas, stats1, stats2, stats3)
-        + (gain1, bias1, gain2, bias2, conv_first, cols_a, grad_w2, *fields1),
+        + (gain1, bias1, gain2, bias2, conv_first, cols_a, grad_w2, sums2, centre2, *fields1),
     )
     other = lax.ppermute(give, "space", near_pairs[0])
     (share,) = call(
         pair_kernel,
         [vmem, vmem],
-        [shape(PEERS // 2, 112, C, dtype=bf16)],
+        [shape(PEERS // 2, ROWS, C, dtype=bf16)],
         [],
         (keep, other),
     )
@@ -677,10 +697,10 @@
 
     grad_in, rows = call(
         last_kernel,
-        [vmem, vmem, smem] + [vmem] * 6,
+        [vmem, vmem, smem] + [vmem] * 4,
         [shape(*field, dtype=bf16), shape(8, 112, C)],
         [],
-        (feat, gout, active, stats1, stats2, stats3, q1, share, gain1),
+        (feat, gout, active, stats1, q1, share, gain1),
     )
     rows = lax.all_to_all(rows, "scene", 0, 0)
     rows = jnp.sum(rows, axis=0).astype(bf16)

time: 177 us -> 172 us (0.972)
  the two profiles are of different devices: /device:TPU:66 before, /device:TPU:64 now
where the time goes in v5:
time: 172 us; the launch traced here: 171 us
  blocking collectives  108 us (63%)
  starting transfers between devices  31.7 us (18%)
  Pallas kernels  17.2 us (10%)
  waiting for transfers between devices  12.8 us (7%)
    all_to_all x3, blocking collectives, spread(): return lax.all_to_all(stats, 'space', 0, 0, tiled=True)  52.6 us
    all_to_all x1, blocking collectives, per_device(): share = lax.all_to_all(share, 'space', 0, 0, axis_index_groups=chip_groups)  32.8 us
    all_to_all x1, blocking collectives, per_device(): rows = lax.all_to_all(rows, 'scene', 0, 0)  22.8 us
    ppermute x4, starting transfers between devices, exchange(): far = [lax.ppermute(fields, 'space', pairs) for pairs in far_pairs]  20.5 us
    pallas_call x7, Pallas kernels, call(): pl.pallas_call(kernel, in_specs=specs, out_specs=out_specs or [vmem] * le...  17.2 us
    ppermute x4, starting transfers between devices, exchange(): near = [lax.ppermute(three, 'space', pairs) for pairs in near_pairs]  9.35 us
    ppermute x4, waiting for transfers between devices, exchange(): near = [lax.ppermute(three, 'space', pairs) for pairs in near_pairs]  8.82 us
    ppermute x1, waiting for transfers between devices, per_device(): other = lax.ppermute(give, 'space', near_pairs[0])  3.94 us
  transfers between devices with their start and end apart: 9, of which 3 were waited for; matrix products, arithmetic and copies ran while one was open for 0% of the time, Pallas kernels for 0%

profile of v5, /device:TPU:64, one launch (start us, length us, event | category | flops | bytes accessed | tf_op | source)
XLA Modules:
  0.0 171.5 jit_solution(9156807078116425802)
XLA Ops:
  0.6 1.1 shard_map.147
  1.8 0.0 copy-start.4
  1.8 12.2 %collective-permute-start.1 = (bf16[2,4,64,128]{3,2,1,0:T(8,128)(2,1)S(1)}, bf16[2,4,64,128]{3,2,1,0:T(8,128)(2,1)S(1)}, u32[]{:S(2)}, u32[]{:S(2)}) collective-permute-start(bf16[2,4,64,128]{3,2,1,0:T(8,128)(2,1)S(1)} %get-tuple-element.27), channel_id=1, source_target_pairs={{4,8},{5,9},{6,10},{7,11},{12,16},{13,17},{14,18},{15,19},{20,24},... | collective-permute-start | bytes 393224 | tf_op jit(solution)/shard_map/ppermute | solution.py:588
  14.0 1.9 %collective-permute-start = (bf16[2,4,64,128]{3,2,1,0:T(8,128)(2,1)S(1)}, bf16[2,4,64,128]{3,2,1,0:T(8,128)(2,1)S(1)}, u32[]{:S(2)}, u32[]{:S(2)}) collective-permute-start(bf16[2,4,64,128]{3,2,1,0:T(8,128)(2,1)S(1)} %get-tuple-element.27), channel_id=1, source_target_pairs={{0,4},{1,5},{2,6},{3,7},{8,12},{9,13},{10,14},{11,15},{16,20},{17,... | collective-permute-start | bytes 393224 | tf_op jit(solution)/shard_map/ppermute | solution.py:588
  15.9 14.8 %all_to_all.45 = f32[64,1,128]{2,1,0:T(1,128)S(1)} all-to-all(f32[64,1,128]{2,1,0:T(1,128)S(1)} %bitcast.47), channel_id=1, replica_groups=mesh['scene'=8,'space'=64] {'space'}, dimensions={0} | all-to-all | bytes 65536 | tf_op jit(solution)/shard_map/all_to_all | solution.py:597
  30.8 0.0 collective-permute-done.1
  30.8 0.0 collective-permute-done
  30.8 2.8 %collective-permute-start.3 = (bf16[3,2,4,64,128]{4,3,2,1,0:T(8,128)(2,1)S(1)}, bf16[3,2,4,64,128]{4,3,2,1,0:T(8,128)(2,1)S(1)}, u32[]{:S(2)}, u32[]{:S(2)}) collective-permute-start(bf16[3,2,4,64,128]{4,3,2,1,0:T(8,128)(2,1)S(1)} %pad_maximum_fusion.rest_0_), channel_id=1, source_target_pairs={{1,2},{3,4},{5,6},{7,8},{9,10},{11,12},{13,14},{15,16},{17,18},{19... | collective-permute-start | bytes 1179656 | tf_op jit(solution)/shard_map/ppermute | solution.py:592
  33.6 1.9 %collective-permute-start.2 = (bf16[3,2,4,64,128]{4,3,2,1,0:T(8,128)(2,1)S(1)}, bf16[3,2,4,64,128]{4,3,2,1,0:T(8,128)(2,1)S(1)}, u32[]{:S(2)}, u32[]{:S(2)}) collective-permute-start(bf16[3,2,4,64,128]{4,3,2,1,0:T(8,128)(2,1)S(1)} %pad_maximum_fusion.rest_0_), channel_id=1, source_target_pairs={{0,1},{2,3},{4,5},{6,7},{8,9},{10,11},{12,13},{14,15},{16,17},{18,... | collective-permute-start | bytes 1179656 | tf_op jit(solution)/shard_map/ppermute | solution.py:592
  35.5 4.4 %collective-permute-done.3.rest_2_ = bf16[3,2,4,64,128]{4,3,2,1,0:T(8,128)(2,1)S(1)} collective-permute-done((bf16[3,2,4,64,128]{4,3,2,1,0:T(8,128)(2,1)S(1)}, bf16[3,2,4,64,128]{4,3,2,1,0:T(8,128)(2,1)S(1)}, u32[]{:S(2)}, u32[]{:S(2)}) %collective-permute-start.3) | collective-permute-done | bytes 393248 | tf_op jit(solution)/shard_map/ppermute | solution.py:592
  39.9 0.0 collective-permute-done.2.rest_1_
  39.9 0.0 copy-start
  39.9 0.0 copy-start.2
  39.9 0.0 copy-start.7
  39.9 0.0 copy-start.8
  40.0 5.5 %shard_map.148 = (f32[4,64,128]{2,1,0:T(8,128)S(1)}, f32[4,64,128]{2,1,0:T(8,128)S(1)}, bf16[9,4,6,16,128]{4,3,2,1,0:T(8,128)(2,1)S(1)}, bf16[2,4,64,128]{3,2,1,0:T(8,128)(2,1)S(1)}, s32[4,26]{1,0:T(4,128)S(1)}) custom-call(s32[1,4]{1,0:T(1,128)} %active.7, s32[4,26]{1,0:T(4,128)} %bitcast.63, s32[4,26]{1,0:T(4,128)} %bitcast.64, f32[1,128]{1,0:T(1,128)} %bitcast.49, ...), custom_call_target="tpu_custom_call" | custom-call | tf_op jit(solution)/shard_map/pallas_call | solution.py:564
  45.4 0.0 copy-start.1
  45.4 0.0 copy-start.5
  45.5 0.0 copy-start.6
  45.5 4.4 %collective-permute-start.5 = (bf16[2,4,64,128]{3,2,1,0:T(8,128)(2,1)S(1)}, bf16[2,4,64,128]{3,2,1,0:T(8,128)(2,1)S(1)}, u32[]{:S(2)}, u32[]{:S(2)}) collective-permute-start(bf16[2,4,64,128]{3,2,1,0:T(8,128)(2,1)S(1)} %get-tuple-element.35), channel_id=1, source_target_pairs={{4,8},{5,9},{6,10},{7,11},{12,16},{13,17},{14,18},{15,19},{20,24},... | collective-permute-start | bytes 393224 | tf_op jit(solution)/shard_map/ppermute | solution.py:588
  49.9 1.9 %collective-permute-start.4 = (bf16[2,4,64,128]{3,2,1,0:T(8,128)(2,1)S(1)}, bf16[2,4,64,128]{3,2,1,0:T(8,128)(2,1)S(1)}, u32[]{:S(2)}, u32[]{:S(2)}) collective-permute-start(bf16[2,4,64,128]{3,2,1,0:T(8,128)(2,1)S(1)} %get-tuple-element.35), channel_id=1, source_target_pairs={{0,4},{1,5},{2,6},{3,7},{8,12},{9,13},{10,14},{11,15},{16,20},{17,... | collective-permute-start | bytes 393224 | tf_op jit(solution)/shard_map/ppermute | solution.py:588
  51.8 0.0 copy-done.4
  51.8 0.7 shard_map.149
  52.5 21.2 %all_to_all.46 = f32[64,1,128]{2,1,0:T(1,128)S(1)} all-to-all(f32[64,1,128]{2,1,0:T(1,128)S(1)} %bitcast.44), channel_id=1, replica_groups=mesh['scene'=8,'space'=64] {'space'}, dimensions={0} | all-to-all | bytes 65536 | tf_op jit(solution)/shard_map/all_to_all | solution.py:597
  73.7 0.0 collective-permute-done.5
  73.7 0.0 collective-permute-done.4
  73.7 2.8 %collective-permute-start.7 = (bf16[3,2,4,64,128]{4,3,2,1,0:T(8,128)(2,1)S(1)}, bf16[3,2,4,64,128]{4,3,2,1,0:T(8,128)(2,1)S(1)}, u32[]{:S(2)}, u32[]{:S(2)}) collective-permute-start(bf16[3,2,4,64,128]{4,3,2,1,0:T(8,128)(2,1)S(1)} %pad_maximum_fusion.1.rest_0_), channel_id=1, source_target_pairs={{1,2},{3,4},{5,6},{7,8},{9,10},{11,12},{13,14},{15,16},{17,18},{19... | collective-permute-start | bytes 1179656 | tf_op jit(solution)/shard_map/ppermute | solution.py:592
  76.5 1.9 %collective-permute-start.6 = (bf16[3,2,4,64,128]{4,3,2,1,0:T(8,128)(2,1)S(1)}, bf16[3,2,4,64,128]{4,3,2,1,0:T(8,128)(2,1)S(1)}, u32[]{:S(2)}, u32[]{:S(2)}) collective-permute-start(bf16[3,2,4,64,128]{4,3,2,1,0:T(8,128)(2,1)S(1)} %pad_maximum_fusion.1.rest_0_), channel_id=1, source_target_pairs={{0,1},{2,3},{4,5},{6,7},{8,9},{10,11},{12,13},{14,15},{16,17},{18,... | collective-permute-start | bytes 1179656 | tf_op jit(solution)/shard_map/ppermute | solution.py:592
  78.4 4.4 %collective-permute-done.7.rest_2_ = bf16[3,2,4,64,128]{4,3,2,1,0:T(8,128)(2,1)S(1)} collective-permute-done((bf16[3,2,4,64,128]{4,3,2,1,0:T(8,128)(2,1)S(1)}, bf16[3,2,4,64,128]{4,3,2,1,0:T(8,128)(2,1)S(1)}, u32[]{:S(2)}, u32[]{:S(2)}) %collective-permute-start.7) | collective-permute-done | bytes 393248 | tf_op jit(solution)/shard_map/ppermute | solution.py:592
  82.8 0.0 collective-permute-done.6.rest_1_
  82.8 0.0 copy-done
  82.8 0.0 copy-done.2
  82.8 0.0 copy-done.3
  82.8 0.0 copy-done.7
  82.8 0.0 copy-done.8
  82.9 3.7 %shard_map.150 = (bf16[4,64,128]{2,1,0:T(8,128)(2,1)}, f32[64,128]{1,0:T(8,128)S(1)}, f32[3456,128]{1,0:T(8,128)S(1)}, f32[64,128]{1,0:T(8,128)S(1)}, f32[8,128]{1,0:T(8,128)S(1)}) custom-call(bf16[4,64,128]{2,1,0:T(8,128)(2,1)S(1)} %bitcast.32, bf16[4,64,128]{2,1,0:T(8,128)(2,1)S(1)} %bitcast.36, s32[1,4]{1,0:T(1,128)S(1)} %copy-done.4, ...), custom_call_target="tpu_custom_call" | custom-call | tf_op jit(solution)/shard_map/pallas_call | solution.py:564
  86.5 16.6 %all_to_all.47 = f32[64,1,128]{2,1,0:T(1,128)S(1)} all-to-all(f32[64,1,128]{2,1,0:T(1,128)S(1)} %bitcast.48), channel_id=1, replica_groups=mesh['scene'=8,'space'=64] {'space'}, dimensions={0} | all-to-all | bytes 65536 | tf_op jit(solution)/shard_map/all_to_all | solution.py:597
  103.1 0.0 copy-done.1
  103.1 0.0 copy-done.5
  103.1 0.0 copy-done.6
  103.2 4.3 %shard_map.151 = (f32[4,64,128]{2,1,0:T(8,128)S(1)}, f32[32,120,128]{2,1,0:T(8,128)S(1)}, f32[32,120,128]{2,1,0:T(8,128)S(1)}) custom-call(bf16[4,64,128]{2,1,0:T(8,128)(2,1)S(1)} %bitcast.33, s32[1,4]{1,0:T(1,128)S(1)} %copy-done.4, s32[4,26]{1,0:T(4,128)S(1)} %get-tuple-element.32.index, f32[4,64,128]{2,1,0:T(8,128)S(1)} %get-tuple-element.33.middle, ...), custom_call_target="tpu_custom_call" | custom-call | tf_op jit(solution)/shard_map/pallas_call | solution.py:564
  107.5 1.9 %collective-permute-start.8 = (f32[32,120,128]{2,1,0:T(8,128)S(1)}, f32[32,120,128]{2,1,0:T(8,128)S(1)}, u32[]{:S(2)}, u32[]{:S(2)}) collective-permute-start(f32[32,120,128]{2,1,0:T(8,128)S(1)} %get-tuple-element.47), channel_id=1, source_target_pairs={{0,1},{2,3},{4,5},{6,7},{8,9},{10,11},{12,13},{14,15},{16,17},{18,... | collective-permute-start | bytes 5898248 | tf_op jit(solution)/shard_map/ppermute | solution.py:688
  109.4 3.9 %collective-permute-done.8.other = f32[32,120,128]{2,1,0:T(8,128)S(1)} collective-permute-done((f32[32,120,128]{2,1,0:T(8,128)S(1)}, f32[32,120,128]{2,1,0:T(8,128)S(1)}, u32[]{:S(2)}, u32[]{:S(2)}) %collective-permute-start.8) | collective-permute-done | bytes 1966112 | tf_op jit(solution)/shard_map/ppermute | solution.py:688
  113.3 0.4 shard_map.152
  113.7 32.8 %all_to_all.48.parts = bf16[32,128,128]{2,1,0:T(8,128)(2,1)S(1)} all-to-all(bf16[32,128,128]{2,1,0:T(8,128)(2,1)S(1)} %shard_map.152), channel_id=1, replica_groups={{0,2,4,6,8,10,12,14,16,18,20,22,24,26,28,30,32,34,36,38,40,42,44,46,48,..., dimensions={0} | all-to-all | bytes 2097152 | tf_op jit(solution)/shard_map/all_to_all | solution.py:696
  146.5 1.5 shard_map.153
  148.0 22.8 %all_to_all.49 = f32[8,112,128]{2,1,0:T(8,128)S(1)} all-to-all(f32[8,112,128]{2,1,0:T(8,128)S(1)} %get-tuple-element.49), channel_id=1, replica_groups=mesh['scene'=8,'space'=64] {'scene'}, dimensions={0} | all-to-all | bytes 917504 | tf_op jit(solution)/shard_map/all_to_all | solution.py:705
  170.9 0.6 fusion
  (4 shorter events, 0.1 us)
Async XLA Ops:
  1.8 50.0 %copy-start.4 = (s32[1,4]{1,0:T(1,128)S(1)}, s32[1,4]{1,0:T(1,128)}, u32[]{:S(2)}) copy-start(s32[1,4]{1,0:T(1,128)} %active.7) | copy-start | bytes 52
  1.8 29.0 %collective-permute-start.1 = (bf16[2,4,64,128]{3,2,1,0:T(8,128)(2,1)S(1)}, bf16[2,4,64,128]{3,2,1,0:T(8,128)(2,1)S(1)}, u32[]{:S(2)}, u32[]{:S(2)}) collective-permute-start(bf16[2,4,64,128]{3,2,1,0:T(8,128)(2,1)S(1)} %get-tuple-element.27), channel_id=1, source_target_pairs={{4,8},{5,9},{6,10},{7,11},{12,16},{13,17},{14,18},{15,19},{20,24},... | collective-permute-start | bytes 393224 | tf_op jit(solution)/shard_map/ppermute | solution.py:588
  14.0 16.8 %collective-permute-start = (bf16[2,4,64,128]{3,2,1,0:T(8,128)(2,1)S(1)}, bf16[2,4,64,128]{3,2,1,0:T(8,128)(2,1)S(1)}, u32[]{:S(2)}, u32[]{:S(2)}) collective-permute-start(bf16[2,4,64,128]{3,2,1,0:T(8,128)(2,1)S(1)} %get-tuple-element.27), channel_id=1, source_target_pairs={{0,4},{1,5},{2,6},{3,7},{8,12},{9,13},{10,14},{11,15},{16,20},{17,... | collective-permute-start | bytes 393224 | tf_op jit(solution)/shard_map/ppermute | solution.py:588
  30.8 9.1 %collective-permute-start.3 = (bf16[3,2,4,64,128]{4,3,2,1,0:T(8,128)(2,1)S(1)}, bf16[3,2,4,64,128]{4,3,2,1,0:T(8,128)(2,1)S(1)}, u32[]{:S(2)}, u32[]{:S(2)}) collective-permute-start(bf16[3,2,4,64,128]{4,3,2,1,0:T(8,128)(2,1)S(1)} %pad_maximum_fusion.rest_0_), channel_id=1, source_target_pairs={{1,2},{3,4},{5,6},{7,8},{9,10},{11,12},{13,14},{15,16},{17,18},{19... | collective-permute-start | bytes 1179656 | tf_op jit(solution)/shard_map/ppermute | solution.py:592
  33.6 6.3 %collective-permute-start.2 = (bf16[3,2,4,64,128]{4,3,2,1,0:T(8,128)(2,1)S(1)}, bf16[3,2,4,64,128]{4,3,2,1,0:T(8,128)(2,1)S(1)}, u32[]{:S(2)}, u32[]{:S(2)}) collective-permute-start(bf16[3,2,4,64,128]{4,3,2,1,0:T(8,128)(2,1)S(1)} %pad_maximum_fusion.rest_0_), channel_id=1, source_target_pairs={{0,1},{2,3},{4,5},{6,7},{8,9},{10,11},{12,13},{14,15},{16,17},{18,... | collective-permute-start | bytes 1179656 | tf_op jit(solution)/shard_map/ppermute | solution.py:592
  39.9 42.9 %copy-start = (bf16[27,128,128]{2,1,0:T(8,128)(2,1)S(1)}, bf16[27,128,128]{2,1,0:T(8,128)(2,1)}, u32[]{:S(2)}) copy-start(bf16[27,128,128]{2,1,0:T(8,128)(2,1)} %w2.1) | copy-start | bytes 2654212
  39.9 42.9 %copy-start.2 = (bf16[1,4,64,128]{3,2,1,0:T(8,128)(2,1)S(1)}, bf16[1,4,64,128]{3,2,1,0:T(8,128)(2,1)}, u32[]{:S(2)}) copy-start(bf16[1,4,64,128]{3,2,1,0:T(8,128)(2,1)} %param.12) | copy-start | bytes 196612
  39.9 42.9 %copy-start.3 = (bf16[1,4,64,128]{3,2,1,0:T(8,128)(2,1)S(1)}, bf16[1,4,64,128]{3,2,1,0:T(8,128)(2,1)}, u32[]{:S(2)}) copy-start(bf16[1,4,64,128]{3,2,1,0:T(8,128)(2,1)} %param.23) | copy-start | bytes 196612
  39.9 42.9 %copy-start.7 = (f32[128]{0:T(128)S(1)}, f32[128]{0:T(128)}, u32[]{:S(2)}) copy-start(f32[128]{0:T(128)} %param.21) | copy-start | bytes 1540
  39.9 42.9 %copy-start.8 = (f32[128]{0:T(128)S(1)}, f32[128]{0:T(128)}, u32[]{:S(2)}) copy-start(f32[128]{0:T(128)} %param.22) | copy-start | bytes 1540
  45.4 57.7 %copy-start.1 = (bf16[27,128,128]{2,1,0:T(8,128)(2,1)S(1)}, bf16[27,128,128]{2,1,0:T(8,128)(2,1)}, u32[]{:S(2)}) copy-start(bf16[27,128,128]{2,1,0:T(8,128)(2,1)} %w1.1) | copy-start | bytes 2654212
  45.4 57.7 %copy-start.5 = (f32[128]{0:T(128)S(1)}, f32[128]{0:T(128)}, u32[]{:S(2)}) copy-start(f32[128]{0:T(128)} %param.19) | copy-start | bytes 1540
  45.5 57.7 %copy-start.6 = (f32[128]{0:T(128)S(1)}, f32[128]{0:T(128)}, u32[]{:S(2)}) copy-start(f32[128]{0:T(128)} %param.20) | copy-start | bytes 1540
  45.5 28.2 %collective-permute-start.5 = (bf16[2,4,64,128]{3,2,1,0:T(8,128)(2,1)S(1)}, bf16[2,4,64,128]{3,2,1,0:T(8,128)(2,1)S(1)}, u32[]{:S(2)}, u32[]{:S(2)}) collective-permute-start(bf16[2,4,64,128]{3,2,1,0:T(8,128)(2,1)S(1)} %get-tuple-element.35), channel_id=1, source_target_pairs={{4,8},{5,9},{6,10},{7,11},{12,16},{13,17},{14,18},{15,19},{20,24},... | collective-permute-start | bytes 393224 | tf_op jit(solution)/shard_map/ppermute | solution.py:588
  49.9 23.8 %collective-permute-start.4 = (bf16[2,4,64,128]{3,2,1,0:T(8,128)(2,1)S(1)}, bf16[2,4,64,128]{3,2,1,0:T(8,128)(2,1)S(1)}, u32[]{:S(2)}, u32[]{:S(2)}) collective-permute-start(bf16[2,4,64,128]{3,2,1,0:T(8,128)(2,1)S(1)} %get-tuple-element.35), channel_id=1, source_target_pairs={{0,4},{1,5},{2,6},{3,7},{8,12},{9,13},{10,14},{11,15},{16,20},{17,... | collective-permute-start | bytes 393224 | tf_op jit(solution)/shard_map/ppermute | solution.py:588
  73.7 9.1 %collective-permute-start.7 = (bf16[3,2,4,64,128]{4,3,2,1,0:T(8,128)(2,1)S(1)}, bf16[3,2,4,64,128]{4,3,2,1,0:T(8,128)(2,1)S(1)}, u32[]{:S(2)}, u32[]{:S(2)}) collective-permute-start(bf16[3,2,4,64,128]{4,3,2,1,0:T(8,128)(2,1)S(1)} %pad_maximum_fusion.1.rest_0_), channel_id=1, source_target_pairs={{1,2},{3,4},{5,6},{7,8},{9,10},{11,12},{13,14},{15,16},{17,18},{19... | collective-permute-start | bytes 1179656 | tf_op jit(solution)/shard_map/ppermute | solution.py:592
  76.5 6.3 %collective-permute-start.6 = (bf16[3,2,4,64,128]{4,3,2,1,0:T(8,128)(2,1)S(1)}, bf16[3,2,4,64,128]{4,3,2,1,0:T(8,128)(2,1)S(1)}, u32[]{:S(2)}, u32[]{:S(2)}) collective-permute-start(bf16[3,2,4,64,128]{4,3,2,1,0:T(8,128)(2,1)S(1)} %pad_maximum_fusion.1.rest_0_), channel_id=1, source_target_pairs={{0,1},{2,3},{4,5},{6,7},{8,9},{10,11},{12,13},{14,15},{16,17},{18,... | collective-permute-start | bytes 1179656 | tf_op jit(solution)/shard_map/ppermute | solution.py:592
  107.5 5.9 %collective-permute-start.8 = (f32[32,120,128]{2,1,0:T(8,128)S(1)}, f32[32,120,128]{2,1,0:T(8,128)S(1)}, u32[]{:S(2)}, u32[]{:S(2)}) collective-permute-start(f32[32,120,128]{2,1,0:T(8,128)S(1)} %get-tuple-element.47), channel_id=1, source_target_pairs={{0,1},{2,3},{4,5},{6,7},{8,9},{10,11},{12,13},{14,15},{16,17},{18,... | collective-permute-start | bytes 5898248 | tf_op jit(solution)/shard_map/ppermute | solution.py:688

commit v6 on v5

--- a/solution.py
+++ b/solution.py
@@ -92,7 +92,7 @@
     return 1 - 2 * (device & 1)
 
 
-def fill_table(table, fields, scratch, me, make):
+def fill_tables(tables, fields, scratch, me, make):
     near = near_distance(me)
     turn = 0
     for ref, base in zip(fields, (0, near, -near)):
@@ -102,9 +102,12 @@
             buffer = scratch.at[turn % 2]
             turn += 1
             for s in range(SLOTS):
-                buffer[s] = make(ref, entry, s)
-            planes_of(buffer, table, start)
-    table[ZERO_PLANE] = jnp.zeros((PLANE, C), f32)
+                for t, value in enumerate(make(ref.at[entry], s)):
+                    buffer[t, s] = value
+            for t, table in enumerate(tables):
+                planes_of(buffer.at[t], table, start)
+    for table in tables:
+        table[ZERO_PLANE] = jnp.zeros((PLANE, C), f32)
 
 
 def find_planes(owners, positions, ids, index, me):
@@ -290,8 +293,8 @@
 ):
     fields, rest = rest[:3], rest[3:]
     middle, gas, cols_a, both, index = rest[:5]
-    table, pad, cols_g, act, scratch, ids_v = rest[5:11]
-    active, owners, positions, ids, gain1, bias1, w1, w2, sems = rest[11:]
+    table_f, table_g, pad, cols_g, act, scratch, ids_v = rest[5:12]
+    active, owners, positions, ids, gain1, bias1, w1, w2, sems = rest[12:]
     me = lax.axis_index("space")
     copies = fetch(
         (gain_in, bias_in, active_in, own_in, pos_in, w1_in, w2_in),
@@ -310,7 +313,13 @@
         n = (x - mean) * inv * gain1[...] + bias1[...]
         return n * sigmoid(n)
 
-    fill_table(table, fields, scratch, me, lambda ref, e, s: act_of(ref[e, 0, s].astype(f32)))
+    fill_tables(
+        (table_f, table_g),
+        fields,
+        scratch,
+        me,
+        lambda ref, s: (act_of(ref[0, s].astype(f32)), ref[1, s].astype(f32)),
+    )
     for copy in copies[2:5]:
         copy.wait()
     ids_copy.wait()
@@ -318,15 +327,14 @@
     for s in range(SLOTS):
         act[s] = slot_weight(active, s) * act_of(feat[s].astype(f32))
     place_interior(pad, act)
-    place_halo(pad, table, index)
+    place_halo(pad, table_f, index)
     windows_of(pad, cols_a)
     copies[5].wait()
     middle[...] = conv(cols_a, w1).reshape(SLOTS, VOX, C)
-    fill_table(table, fields, scratch, me, lambda ref, e, s: ref[e, 1, s].astype(f32))
     for s in range(SLOTS):
         act[s] = jnp.where(active[0, s] > 0, gout[s].astype(f32), 0.0)
     place_interior(pad, act)
-    place_halo(pad, table, index)
+    place_halo(pad, table_g, index)
     windows_of(pad, cols_g)
     copies[6].wait()
     gas[...] = conv_back(cols_g, w2).reshape(SLOTS, VOX, C)
@@ -348,60 +356,25 @@
     stats2[...] = jnp.broadcast_to(packed[0:1], (PEERS, C))
 
 
-def second_kernel(
-    feat,
-    gout,
-    active,
-    index,
-    middle,
-    gas,
-    stats2,
-    gain2,
-    bias2,
-    w2,
-    *rest,
-):
-    fields, rest = rest[:3], rest[3:]
-    block, stats3, grad_w, sums2, centre2, table, pad, cols, act, scratch = rest
-    me = lax.axis_index("space")
+def second_kernel(active, middle, gas, stats2, gain2, bias2, stats3):
     mean, inv, _ = norm_stats(stats2)
     gain = gain2[...]
-    bias = bias2[...]
-
-    def act_of(ref, e, s):
-        n = (ref[e, 0, s].astype(f32) - mean) * inv * gain + bias
-        return n * sigmoid(n)
-
-    fill_table(table, fields, scratch, me, act_of)
     sum_q = jnp.zeros((1, C), f32)
     sum_c = jnp.zeros((1, C), f32)
     for s in range(SLOTS):
-        w = slot_weight(active, s)
         hat = (middle[s] - mean) * inv
-        n = hat * gain + bias
+        n = hat * gain + bias2[...]
         sg = sigmoid(n)
-        act[s] = w * (n * sg)
-        q = gas[s] * w * sg * (1.0 + n * (1.0 - sg)) * gain
+        q = gas[s] * slot_weight(active, s) * sg * (1.0 + n * (1.0 - sg)) * gain
         sum_q = sum_q + jnp.sum(q, axis=0, keepdims=True)
         sum_c = sum_c + jnp.sum(q * hat, axis=0, keepdims=True)
     packed = pack_stats([sum_q, sum_c])
     stats3[...] = jnp.broadcast_to(packed[0:1], (PEERS, C))
-    place_interior(pad, act)
-    place_halo(pad, table, index)
-    windows_of(pad, cols)
-    store_shares(window_sums(cols), sums2)
-    out = conv(cols, w2).reshape(SLOTS, VOX, C)
-    for s in range(SLOTS):
-        w = slot_weight(active, s)
-        block[s] = ((feat[s].astype(f32) + out[s]) * w).astype(bf16)
-        act[s] = jnp.where(active[0, s] > 0, gout[s].astype(f32), 0.0)
-    centre = centre_of(act, active)
-    centre2[...] = jnp.broadcast_to(centre, (8, C))
-    weight_grad(cols, act[...].astype(bf16).reshape(SLOTS * VOX, C), centre, grad_w)
 
 
 def third_kernel(
     feat,
+    gout,
     active,
     index,
     middle,
@@ -414,14 +387,14 @@
     gain2,
     bias2,
     w1,
+    w2,
     cols_a,
-    grad_w2,
-    sums2,
-    centre2,
     *rest,
 ):
     fields, rest = rest[:3], rest[3:]
-    q1, keep, give, table, pad, cols, act, scratch, grad_w1, sums1 = rest
+    block, q1, keep, give = rest[:4]
+    table_a, table_g, pad, cols, field, own, scratch = rest[4:11]
+    grad_w1, grad_w2, sums1, sums2 = rest[11:]
     me = lax.axis_index("space")
     mean, inv, count = norm_stats(stats2)
     gain = gain2[...]
@@ -430,24 +403,41 @@
     mean_q = unpack_stat(packed, 0)[0:1] / count
     mean_c = unpack_stat(packed, 1)[0:1] / count
 
-    def grad_of(x, g):
+    def both_of(x, g):
         hat = (x - mean) * inv
         n = hat * gain + bias
         sg = sigmoid(n)
         q = g * sg * (1.0 + n * (1.0 - sg)) * gain
-        return (inv * (q - mean_q - hat * mean_c)).astype(bf16).astype(f32)
-
-    fill_table(
-        table,
+        grad = inv * (q - mean_q - hat * mean_c)
+        return n * sg, grad.astype(bf16).astype(f32)
+
+    fill_tables(
+        (table_a, table_g),
         fields,
         scratch,
         me,
-        lambda ref, e, s: grad_of(ref[e, 0, s].astype(f32), ref[e, 1, s].astype(f32)),
-    )
-    for s in range(SLOTS):
-        act[s] = slot_weight(active, s) * grad_of(middle[s], gas[s])
-    place_interior(pad, act)
-    place_halo(pad, table, index)
+        lambda ref, s: both_of(ref[0, s].astype(f32), ref[1, s].astype(f32)),
+    )
+    for s in range(SLOTS):
+        act, grad = both_of(middle[s], gas[s])
+        own[0, s] = slot_weight(active, s) * act
+        own[1, s] = slot_weight(active, s) * grad
+    place_interior(pad, own.at[0])
+    place_halo(pad, table_a, index)
+    windows_of(pad, cols)
+    out = conv(cols, w2).reshape(SLOTS, VOX, C)
+    for s in range(SLOTS):
+        w = slot_weight(active, s)
+        block[s] = ((feat[s].astype(f32) + out[s]) * w).astype(bf16)
+        field[s] = jnp.where(active[0, s] > 0, gout[s].astype(f32), 0.0)
+    store_shares(window_sums(cols), sums2)
+    centre2 = centre_of(field, active)
+    weight_grad(cols, field[...].astype(bf16).reshape(SLOTS * VOX, C), centre2, grad_w2)
+    store_shares(window_sums(cols_a), sums1)
+    centre1 = centre_of(own.at[1], active)
+    weight_grad(cols_a, own[1].astype(bf16).reshape(SLOTS * VOX, C), centre1, grad_w1)
+    place_interior(pad, own.at[1])
+    place_halo(pad, table_g, index)
     windows_of(pad, cols)
     gaf = conv_back(cols, w1).reshape(SLOTS, VOX, C)
     mean1, inv1, _ = norm_stats(stats1)
@@ -462,9 +452,6 @@
         sum_q = sum_q + jnp.sum(q, axis=0, keepdims=True)
         sum_c = sum_c + jnp.sum(q * hat, axis=0, keepdims=True)
     packed = pack_stats([sum_q, sum_c])
-    centre = centre_of(act, active)
-    store_shares(window_sums(cols_a), sums1)
-    weight_grad(cols_a, act[...].astype(bf16).reshape(SLOTS * VOX, C), centre, grad_w1)
 
     def store(out, core):
         for chip in range(PEERS // 2):
@@ -474,9 +461,9 @@
             out[chip, SUM_ROW : SUM_ROW + 1] = packed[0:1]
             out[chip, SUM_ROW + 1 : CENTRE_ROW] = jnp.zeros((3, C), f32)
             out[chip, CENTRE_ROW : CENTRE_ROW + 1] = sums1[p : p + 1]
-            out[chip, CENTRE_ROW + 1 : CENTRE_ROW + 2] = centre
+            out[chip, CENTRE_ROW + 1 : CENTRE_ROW + 2] = centre1
             out[chip, CENTRE_ROW + 2 : CENTRE_ROW + 3] = sums2[p : p + 1]
-            out[chip, CENTRE_ROW + 3 : CENTRE_ROW + 4] = centre2[0:1]
+            out[chip, CENTRE_ROW + 3 : CENTRE_ROW + 4] = centre2
             out[chip, CENTRE_ROW + 4 : 120] = jnp.zeros((4, C), f32)
 
     @pl.when(me % 2 == 0)
@@ -623,7 +610,8 @@
     gain2, bias2 = gain_second.reshape(1, C), bias_second.reshape(1, C)
     field = (SLOTS, VOX, C)
     wide = pltpu.VMEM(field, f32)
-    scratch = pltpu.VMEM((2, *field), f32)
+    two = pltpu.VMEM((2, *field), f32)
+    scratch = pltpu.VMEM((2, 2, *field), f32)
     table = pltpu.VMEM((LANES * PLANES, PLANE, C), f32)
     pad = pltpu.VMEM((SLOTS, 6, 6, 8, C), f32)
     cols_shape = (9, SLOTS, 6, PLANE, C)
@@ -647,7 +635,7 @@
         [hbm] * 7 + [vmem] * 4,
         [shape(*field), shape(*field), shape(*cols_shape, dtype=bf16)]
         + [shape(2, *field, dtype=bf16), shape(SLOTS, 26, dtype=jnp.int32)],
-        [table, pad, cols, wide, scratch, pltpu.VMEM((PEERS, C), jnp.int32)]
+        [table, table, pad, cols, wide, scratch, pltpu.VMEM((PEERS, C), jnp.int32)]
         + [
             pltpu.SMEM((1, SLOTS), jnp.int32),
             pltpu.SMEM((SLOTS, 26), jnp.int32),
@@ -665,25 +653,24 @@
     (stats2,) = call(sums_kernel, [smem, vmem], [shape(PEERS, C)], [], (active, middle))
     fields1, stats2 = exchange(both, stats2)
 
-    block, stats3, grad_w2, sums2, centre2 = call(
+    (stats3,) = call(
         second_kernel,
-        [vmem, vmem, smem, smem] + [vmem] * 9,
-        [shape(*field, dtype=bf16), shape(PEERS, C), shape(27 * C, C)]
-        + [shape(PEERS, C), shape(8, C)],
-        [table, pad, cols, wide, scratch],
-        (feat, gout, active, index, middle, gas, stats2, gain2, bias2)
-        + (conv_second, *fields1),
+        [smem] + [vmem] * 5,
+        [shape(PEERS, C)],
+        [],
+        (active, middle, gas, stats2, gain2, bias2),
     )
     stats3 = spread(stats3)
 
-    q1, keep, give = call(
+    weight = pltpu.VMEM((27 * C, C), f32)
+    line = pltpu.VMEM((PEERS, C), f32)
+    block, q1, keep, give = call(
         third_kernel,
-        [vmem, smem, smem] + [vmem] * 17,
-        [shape(*field), shape(PEERS // 2, 120, C), shape(PEERS // 2, 120, C)],
-        [table, pad, cols, wide, scratch, pltpu.VMEM((27 * C, C), f32)]
-        + [pltpu.VMEM((PEERS, C), f32)],
-        (feat, active, index, middle, gas, stats1, stats2, stats3)
-        + (gain1, bias1, gain2, bias2, conv_first, cols_a, grad_w2, sums2, centre2, *fields1),
+        [vmem, vmem, smem, smem] + [vmem] * 15,
+        [shape(*field, dtype=bf16), shape(*field)] + [shape(PEERS // 2, 120, C)] * 2,
+        [table, table, pad, cols, wide, two, scratch, weight, weight, line, line],
+        (feat, gout, active, index, middle, gas, stats1, stats2, stats3)
+        + (gain1, bias1, gain2, bias2, conv_first, conv_second, cols_a, *fields1),
     )
     other = lax.ppermute(give, "space", near_pairs[0])
     (share,) = call(

time: 172 us -> 167 us (0.971)
  waiting for transfers between devices: 12.8 us -> 8.36 us
    ppermute x4, waiting for transfers between devices: 8.82 us -> 4.41 us  [exchange(): near = [lax.ppermute(three, 'space', pairs) for pairs in near_pairs]]
  transfers between devices with their start and end apart: 9 -> 9, of which waited for: 3 -> 2; matrix products, arithmetic and copies ran while one was open for 0% -> 0% of each run, Pallas kernels for 0% -> 1%
where the time goes in v6:
time: 167 us
  blocking collectives  108 us (65%)
  starting transfers between devices  31.6 us (19%)
  Pallas kernels  17.5 us (10%)
  waiting for transfers between devices  8.36 us (5%)
    all_to_all x3, blocking collectives, spread(): return lax.all_to_all(stats, 'space', 0, 0, tiled=True)  52.2 us
    all_to_all x1, blocking collectives, per_device(): share = lax.all_to_all(share, 'space', 0, 0, axis_index_groups=chip_groups)  32.8 us
    all_to_all x1, blocking collectives, per_device(): rows = lax.all_to_all(rows, 'scene', 0, 0)  22.8 us
    ppermute x4, starting transfers between devices, exchange(): far = [lax.ppermute(fields, 'space', pairs) for pairs in far_pairs]  20.3 us
    pallas_call x7, Pallas kernels, call(): pl.pallas_call(kernel, in_specs=specs, out_specs=out_specs or [vmem] * le...  17.5 us
    ppermute x4, starting transfers between devices, exchange(): near = [lax.ppermute(three, 'space', pairs) for pairs in near_pairs]  9.35 us
    ppermute x4, waiting for transfers between devices, exchange(): near = [lax.ppermute(three, 'space', pairs) for pairs in near_pairs]  4.41 us
    ppermute x1, waiting for transfers between devices, per_device(): other = lax.ppermute(give, 'space', near_pairs[0])  3.94 us
  transfers between devices with their start and end apart: 9, of which 2 were waited for; matrix products, arithmetic and copies ran while one was open for 0% of the time, Pallas kernels for 1%

profile of v6, /device:TPU:64, one launch (start us, length us, event | category | flops | bytes accessed | tf_op | source)
XLA Modules:
  0.0 166.9 jit_solution(16054287093963799015)
XLA Ops:
  0.6 1.1 shard_map.147
  1.8 0.0 copy-start.4
  1.8 12.2 %collective-permute-start.1 = (bf16[2,4,64,128]{3,2,1,0:T(8,128)(2,1)S(1)}, bf16[2,4,64,128]{3,2,1,0:T(8,128)(2,1)S(1)}, u32[]{:S(2)}, u32[]{:S(2)}) collective-permute-start(bf16[2,4,64,128]{3,2,1,0:T(8,128)(2,1)S(1)} %get-tuple-element.23), channel_id=1, source_target_pairs={{4,8},{5,9},{6,10},{7,11},{12,16},{13,17},{14,18},{15,19},{20,24},... | collective-permute-start | bytes 393224 | tf_op jit(solution)/shard_map/ppermute | solution.py:575
  14.0 1.9 %collective-permute-start = (bf16[2,4,64,128]{3,2,1,0:T(8,128)(2,1)S(1)}, bf16[2,4,64,128]{3,2,1,0:T(8,128)(2,1)S(1)}, u32[]{:S(2)}, u32[]{:S(2)}) collective-permute-start(bf16[2,4,64,128]{3,2,1,0:T(8,128)(2,1)S(1)} %get-tuple-element.23), channel_id=1, source_target_pairs={{0,4},{1,5},{2,6},{3,7},{8,12},{9,13},{10,14},{11,15},{16,20},{17,... | collective-permute-start | bytes 393224 | tf_op jit(solution)/shard_map/ppermute | solution.py:575
  15.9 14.8 %all_to_all.45 = f32[64,1,128]{2,1,0:T(1,128)S(1)} all-to-all(f32[64,1,128]{2,1,0:T(1,128)S(1)} %bitcast.47), channel_id=1, replica_groups=mesh['scene'=8,'space'=64] {'space'}, dimensions={0} | all-to-all | bytes 65536 | tf_op jit(solution)/shard_map/all_to_all | solution.py:584
  30.8 0.0 collective-permute-done.1
  30.8 0.0 collective-permute-done
  30.8 2.8 %collective-permute-start.3 = (bf16[3,2,4,64,128]{4,3,2,1,0:T(8,128)(2,1)S(1)}, bf16[3,2,4,64,128]{4,3,2,1,0:T(8,128)(2,1)S(1)}, u32[]{:S(2)}, u32[]{:S(2)}) collective-permute-start(bf16[3,2,4,64,128]{4,3,2,1,0:T(8,128)(2,1)S(1)} %pad_maximum_fusion.rest_0_), channel_id=1, source_target_pairs={{1,2},{3,4},{5,6},{7,8},{9,10},{11,12},{13,14},{15,16},{17,18},{19... | collective-permute-start | bytes 1179656 | tf_op jit(solution)/shard_map/ppermute | solution.py:579
  33.6 1.9 %collective-permute-start.2 = (bf16[3,2,4,64,128]{4,3,2,1,0:T(8,128)(2,1)S(1)}, bf16[3,2,4,64,128]{4,3,2,1,0:T(8,128)(2,1)S(1)}, u32[]{:S(2)}, u32[]{:S(2)}) collective-permute-start(bf16[3,2,4,64,128]{4,3,2,1,0:T(8,128)(2,1)S(1)} %pad_maximum_fusion.rest_0_), channel_id=1, source_target_pairs={{0,1},{2,3},{4,5},{6,7},{8,9},{10,11},{12,13},{14,15},{16,17},{18,... | collective-permute-start | bytes 1179656 | tf_op jit(solution)/shard_map/ppermute | solution.py:579
  35.5 4.4 %collective-permute-done.3.rest_2_ = bf16[3,2,4,64,128]{4,3,2,1,0:T(8,128)(2,1)S(1)} collective-permute-done((bf16[3,2,4,64,128]{4,3,2,1,0:T(8,128)(2,1)S(1)}, bf16[3,2,4,64,128]{4,3,2,1,0:T(8,128)(2,1)S(1)}, u32[]{:S(2)}, u32[]{:S(2)}) %collective-permute-start.3) | collective-permute-done | bytes 393248 | tf_op jit(solution)/shard_map/ppermute | solution.py:579
  39.9 0.0 collective-permute-done.2.rest_1_
  39.9 0.0 copy-start.7
  39.9 0.0 copy-start.8
  39.9 0.0 copy-start.1
  39.9 0.0 copy-start.2
  40.0 0.0 copy-start.3
  40.0 0.0 copy-start.5
  40.0 0.0 copy-start.6
  40.0 5.4 %shard_map.148 = (f32[4,64,128]{2,1,0:T(8,128)S(1)}, f32[4,64,128]{2,1,0:T(8,128)S(1)}, bf16[9,4,6,16,128]{4,3,2,1,0:T(8,128)(2,1)S(1)}, bf16[2,4,64,128]{3,2,1,0:T(8,128)(2,1)S(1)}, s32[4,26]{1,0:T(4,128)S(1)}) custom-call(s32[1,4]{1,0:T(1,128)} %active.7, s32[4,26]{1,0:T(4,128)} %bitcast.62, s32[4,26]{1,0:T(4,128)} %bitcast.63, f32[1,128]{1,0:T(1,128)} %bitcast.48, ...), custom_call_target="tpu_custom_call" | custom-call | tf_op jit(solution)/shard_map/pallas_call | solution.py:551
  45.4 4.3 %collective-permute-start.5 = (bf16[2,4,64,128]{3,2,1,0:T(8,128)(2,1)S(1)}, bf16[2,4,64,128]{3,2,1,0:T(8,128)(2,1)S(1)}, u32[]{:S(2)}, u32[]{:S(2)}) collective-permute-start(bf16[2,4,64,128]{3,2,1,0:T(8,128)(2,1)S(1)} %get-tuple-element.31), channel_id=1, source_target_pairs={{4,8},{5,9},{6,10},{7,11},{12,16},{13,17},{14,18},{15,19},{20,24},... | collective-permute-start | bytes 393224 | tf_op jit(solution)/shard_map/ppermute | solution.py:575
  49.7 1.9 %collective-permute-start.4 = (bf16[2,4,64,128]{3,2,1,0:T(8,128)(2,1)S(1)}, bf16[2,4,64,128]{3,2,1,0:T(8,128)(2,1)S(1)}, u32[]{:S(2)}, u32[]{:S(2)}) collective-permute-start(bf16[2,4,64,128]{3,2,1,0:T(8,128)(2,1)S(1)} %get-tuple-element.31), channel_id=1, source_target_pairs={{0,4},{1,5},{2,6},{3,7},{8,12},{9,13},{10,14},{11,15},{16,20},{17,... | collective-permute-start | bytes 393224 | tf_op jit(solution)/shard_map/ppermute | solution.py:575
  51.6 0.0 copy-done.4
  51.6 0.7 shard_map.149
  52.3 21.2 %all_to_all.46 = f32[64,1,128]{2,1,0:T(1,128)S(1)} all-to-all(f32[64,1,128]{2,1,0:T(1,128)S(1)} %bitcast.43), channel_id=1, replica_groups=mesh['scene'=8,'space'=64] {'space'}, dimensions={0} | all-to-all | bytes 65536 | tf_op jit(solution)/shard_map/all_to_all | solution.py:584
  73.5 0.0 collective-permute-done.5
  73.5 0.0 collective-permute-done.4
  73.5 2.8 %collective-permute-start.7 = (bf16[3,2,4,64,128]{4,3,2,1,0:T(8,128)(2,1)S(1)}, bf16[3,2,4,64,128]{4,3,2,1,0:T(8,128)(2,1)S(1)}, u32[]{:S(2)}, u32[]{:S(2)}) collective-permute-start(bf16[3,2,4,64,128]{4,3,2,1,0:T(8,128)(2,1)S(1)} %pad_maximum_fusion.1.rest_0_), channel_id=1, source_target_pairs={{1,2},{3,4},{5,6},{7,8},{9,10},{11,12},{13,14},{15,16},{17,18},{19... | collective-permute-start | bytes 1179656 | tf_op jit(solution)/shard_map/ppermute | solution.py:579
  76.3 1.9 %collective-permute-start.6 = (bf16[3,2,4,64,128]{4,3,2,1,0:T(8,128)(2,1)S(1)}, bf16[3,2,4,64,128]{4,3,2,1,0:T(8,128)(2,1)S(1)}, u32[]{:S(2)}, u32[]{:S(2)}) collective-permute-start(bf16[3,2,4,64,128]{4,3,2,1,0:T(8,128)(2,1)S(1)} %pad_maximum_fusion.1.rest_0_), channel_id=1, source_target_pairs={{0,1},{2,3},{4,5},{6,7},{8,9},{10,11},{12,13},{14,15},{16,17},{18,... | collective-permute-start | bytes 1179656 | tf_op jit(solution)/shard_map/ppermute | solution.py:579
  78.2 0.0 copy-done.7
  78.2 0.0 copy-done.8
  78.3 0.9 shard_map.150
  79.2 16.2 %all_to_all.47 = f32[64,1,128]{2,1,0:T(1,128)S(1)} all-to-all(f32[64,1,128]{2,1,0:T(1,128)S(1)} %bitcast.44), channel_id=1, replica_groups=mesh['scene'=8,'space'=64] {'space'}, dimensions={0} | all-to-all | bytes 65536 | tf_op jit(solution)/shard_map/all_to_all | solution.py:584
  95.4 0.0 collective-permute-done.7.rest_2_
  95.4 0.0 collective-permute-done.6.rest_1_
  95.4 0.0 copy-done
  95.4 0.0 copy-done.1
  95.4 0.0 copy-done.2
  95.4 0.0 copy-done.3
  95.4 0.0 copy-done.5
  95.4 0.0 copy-done.6
  95.4 7.5 %shard_map.151 = (bf16[4,64,128]{2,1,0:T(8,128)(2,1)}, f32[4,64,128]{2,1,0:T(8,128)S(1)}, f32[32,120,128]{2,1,0:T(8,128)S(1)}, f32[32,120,128]{2,1,0:T(8,128)S(1)}) custom-call(bf16[4,64,128]{2,1,0:T(8,128)(2,1)S(1)} %bitcast.32, bf16[4,64,128]{2,1,0:T(8,128)(2,1)S(1)} %bitcast.35, s32[1,4]{1,0:T(1,128)S(1)} %copy-done.4, ...), custom_call_target="tpu_custom_call" | custom-call | tf_op jit(solution)/shard_map/pallas_call | solution.py:551
  102.9 1.9 %collective-permute-start.8 = (f32[32,120,128]{2,1,0:T(8,128)S(1)}, f32[32,120,128]{2,1,0:T(8,128)S(1)}, u32[]{:S(2)}, u32[]{:S(2)}) collective-permute-start(f32[32,120,128]{2,1,0:T(8,128)S(1)} %get-tuple-element.39), channel_id=1, source_target_pairs={{0,1},{2,3},{4,5},{6,7},{8,9},{10,11},{12,13},{14,15},{16,17},{18,... | collective-permute-start | bytes 5898248 | tf_op jit(solution)/shard_map/ppermute | solution.py:675
  104.8 3.9 %collective-permute-done.8.other = f32[32,120,128]{2,1,0:T(8,128)S(1)} collective-permute-done((f32[32,120,128]{2,1,0:T(8,128)S(1)}, f32[32,120,128]{2,1,0:T(8,128)S(1)}, u32[]{:S(2)}, u32[]{:S(2)}) %collective-permute-start.8) | collective-permute-done | bytes 1966112 | tf_op jit(solution)/shard_map/ppermute | solution.py:675
  108.8 0.4 shard_map.152
  109.1 32.8 %all_to_all.48.parts = bf16[32,128,128]{2,1,0:T(8,128)(2,1)S(1)} all-to-all(bf16[32,128,128]{2,1,0:T(8,128)(2,1)S(1)} %shard_map.152), channel_id=1, replica_groups={{0,2,4,6,8,10,12,14,16,18,20,22,24,26,28,30,32,34,36,38,40,42,44,46,48,..., dimensions={0} | all-to-all | bytes 2097152 | tf_op jit(solution)/shard_map/all_to_all | solution.py:683
  142.0 1.5 shard_map.153
  143.5 22.8 %all_to_all.49 = f32[8,112,128]{2,1,0:T(8,128)S(1)} all-to-all(f32[8,112,128]{2,1,0:T(8,128)S(1)} %get-tuple-element.41), channel_id=1, replica_groups=mesh['scene'=8,'space'=64] {'scene'}, dimensions={0} | all-to-all | bytes 917504 | tf_op jit(solution)/shard_map/all_to_all | solution.py:692
  166.3 0.6 fusion
  (4 shorter events, 0.1 us)
Async XLA Ops:
  1.8 49.9 %copy-start.4 = (s32[1,4]{1,0:T(1,128)S(1)}, s32[1,4]{1,0:T(1,128)}, u32[]{:S(2)}) copy-start(s32[1,4]{1,0:T(1,128)} %active.7) | copy-start | bytes 52
  1.8 29.0 %collective-permute-start.1 = (bf16[2,4,64,128]{3,2,1,0:T(8,128)(2,1)S(1)}, bf16[2,4,64,128]{3,2,1,0:T(8,128)(2,1)S(1)}, u32[]{:S(2)}, u32[]{:S(2)}) collective-permute-start(bf16[2,4,64,128]{3,2,1,0:T(8,128)(2,1)S(1)} %get-tuple-element.23), channel_id=1, source_target_pairs={{4,8},{5,9},{6,10},{7,11},{12,16},{13,17},{14,18},{15,19},{20,24},... | collective-permute-start | bytes 393224 | tf_op jit(solution)/shard_map/ppermute | solution.py:575
  14.0 16.8 %collective-permute-start = (bf16[2,4,64,128]{3,2,1,0:T(8,128)(2,1)S(1)}, bf16[2,4,64,128]{3,2,1,0:T(8,128)(2,1)S(1)}, u32[]{:S(2)}, u32[]{:S(2)}) collective-permute-start(bf16[2,4,64,128]{3,2,1,0:T(8,128)(2,1)S(1)} %get-tuple-element.23), channel_id=1, source_target_pairs={{0,4},{1,5},{2,6},{3,7},{8,12},{9,13},{10,14},{11,15},{16,20},{17,... | collective-permute-start | bytes 393224 | tf_op jit(solution)/shard_map/ppermute | solution.py:575
  30.8 9.1 %collective-permute-start.3 = (bf16[3,2,4,64,128]{4,3,2,1,0:T(8,128)(2,1)S(1)}, bf16[3,2,4,64,128]{4,3,2,1,0:T(8,128)(2,1)S(1)}, u32[]{:S(2)}, u32[]{:S(2)}) collective-permute-start(bf16[3,2,4,64,128]{4,3,2,1,0:T(8,128)(2,1)S(1)} %pad_maximum_fusion.rest_0_), channel_id=1, source_target_pairs={{1,2},{3,4},{5,6},{7,8},{9,10},{11,12},{13,14},{15,16},{17,18},{19... | collective-permute-start | bytes 1179656 | tf_op jit(solution)/shard_map/ppermute | solution.py:579
  33.6 6.3 %collective-permute-start.2 = (bf16[3,2,4,64,128]{4,3,2,1,0:T(8,128)(2,1)S(1)}, bf16[3,2,4,64,128]{4,3,2,1,0:T(8,128)(2,1)S(1)}, u32[]{:S(2)}, u32[]{:S(2)}) collective-permute-start(bf16[3,2,4,64,128]{4,3,2,1,0:T(8,128)(2,1)S(1)} %pad_maximum_fusion.rest_0_), channel_id=1, source_target_pairs={{0,1},{2,3},{4,5},{6,7},{8,9},{10,11},{12,13},{14,15},{16,17},{18,... | collective-permute-start | bytes 1179656 | tf_op jit(solution)/shard_map/ppermute | solution.py:579
  39.9 38.3 %copy-start.7 = (f32[128]{0:T(128)S(1)}, f32[128]{0:T(128)}, u32[]{:S(2)}) copy-start(f32[128]{0:T(128)} %param.21) | copy-start | bytes 1540
  39.9 38.3 %copy-start.8 = (f32[128]{0:T(128)S(1)}, f32[128]{0:T(128)}, u32[]{:S(2)}) copy-start(f32[128]{0:T(128)} %param.22) | copy-start | bytes 1540
  39.9 55.5 %copy-start = (bf16[27,128,128]{2,1,0:T(8,128)(2,1)S(1)}, bf16[27,128,128]{2,1,0:T(8,128)(2,1)}, u32[]{:S(2)}) copy-start(bf16[27,128,128]{2,1,0:T(8,128)(2,1)} %w1.1) | copy-start | bytes 2654212
  39.9 55.5 %copy-start.1 = (bf16[27,128,128]{2,1,0:T(8,128)(2,1)S(1)}, bf16[27,128,128]{2,1,0:T(8,128)(2,1)}, u32[]{:S(2)}) copy-start(bf16[27,128,128]{2,1,0:T(8,128)(2,1)} %w2.1) | copy-start | bytes 2654212
  39.9 55.5 %copy-start.2 = (bf16[1,4,64,128]{3,2,1,0:T(8,128)(2,1)S(1)}, bf16[1,4,64,128]{3,2,1,0:T(8,128)(2,1)}, u32[]{:S(2)}) copy-start(bf16[1,4,64,128]{3,2,1,0:T(8,128)(2,1)} %param.12) | copy-start | bytes 196612
  40.0 55.5 %copy-start.3 = (bf16[1,4,64,128]{3,2,1,0:T(8,128)(2,1)S(1)}, bf16[1,4,64,128]{3,2,1,0:T(8,128)(2,1)}, u32[]{:S(2)}) copy-start(bf16[1,4,64,128]{3,2,1,0:T(8,128)(2,1)} %param.23) | copy-start | bytes 196612
  40.0 55.5 %copy-start.5 = (f32[128]{0:T(128)S(1)}, f32[128]{0:T(128)}, u32[]{:S(2)}) copy-start(f32[128]{0:T(128)} %param.19) | copy-start | bytes 1540
  40.0 55.5 %copy-start.6 = (f32[128]{0:T(128)S(1)}, f32[128]{0:T(128)}, u32[]{:S(2)}) copy-start(f32[128]{0:T(128)} %param.20) | copy-start | bytes 1540
  45.4 28.1 %collective-permute-start.5 = (bf16[2,4,64,128]{3,2,1,0:T(8,128)(2,1)S(1)}, bf16[2,4,64,128]{3,2,1,0:T(8,128)(2,1)S(1)}, u32[]{:S(2)}, u32[]{:S(2)}) collective-permute-start(bf16[2,4,64,128]{3,2,1,0:T(8,128)(2,1)S(1)} %get-tuple-element.31), channel_id=1, source_target_pairs={{4,8},{5,9},{6,10},{7,11},{12,16},{13,17},{14,18},{15,19},{20,24},... | collective-permute-start | bytes 393224 | tf_op jit(solution)/shard_map/ppermute | solution.py:575
  49.7 23.8 %collective-permute-start.4 = (bf16[2,4,64,128]{3,2,1,0:T(8,128)(2,1)S(1)}, bf16[2,4,64,128]{3,2,1,0:T(8,128)(2,1)S(1)}, u32[]{:S(2)}, u32[]{:S(2)}) collective-permute-start(bf16[2,4,64,128]{3,2,1,0:T(8,128)(2,1)S(1)} %get-tuple-element.31), channel_id=1, source_target_pairs={{0,4},{1,5},{2,6},{3,7},{8,12},{9,13},{10,14},{11,15},{16,20},{17,... | collective-permute-start | bytes 393224 | tf_op jit(solution)/shard_map/ppermute | solution.py:575
  73.5 21.8 %collective-permute-start.7 = (bf16[3,2,4,64,128]{4,3,2,1,0:T(8,128)(2,1)S(1)}, bf16[3,2,4,64,128]{4,3,2,1,0:T(8,128)(2,1)S(1)}, u32[]{:S(2)}, u32[]{:S(2)}) collective-permute-start(bf16[3,2,4,64,128]{4,3,2,1,0:T(8,128)(2,1)S(1)} %pad_maximum_fusion.1.rest_0_), channel_id=1, source_target_pairs={{1,2},{3,4},{5,6},{7,8},{9,10},{11,12},{13,14},{15,16},{17,18},{19... | collective-permute-start | bytes 1179656 | tf_op jit(solution)/shard_map/ppermute | solution.py:579
  76.3 19.1 %collective-permute-start.6 = (bf16[3,2,4,64,128]{4,3,2,1,0:T(8,128)(2,1)S(1)}, bf16[3,2,4,64,128]{4,3,2,1,0:T(8,128)(2,1)S(1)}, u32[]{:S(2)}, u32[]{:S(2)}) collective-permute-start(bf16[3,2,4,64,128]{4,3,2,1,0:T(8,128)(2,1)S(1)} %pad_maximum_fusion.1.rest_0_), channel_id=1, source_target_pairs={{0,1},{2,3},{4,5},{6,7},{8,9},{10,11},{12,13},{14,15},{16,17},{18,... | collective-permute-start | bytes 1179656 | tf_op jit(solution)/shard_map/ppermute | solution.py:579
  102.9 5.9 %collective-permute-start.8 = (f32[32,120,128]{2,1,0:T(8,128)S(1)}, f32[32,120,128]{2,1,0:T(8,128)S(1)}, u32[]{:S(2)}, u32[]{:S(2)}) collective-permute-start(f32[32,120,128]{2,1,0:T(8,128)S(1)} %get-tuple-element.39), channel_id=1, source_target_pairs={{0,1},{2,3},{4,5},{6,7},{8,9},{10,11},{12,13},{14,15},{16,17},{18,... | collective-permute-start | bytes 5898248 | tf_op jit(solution)/shard_map/ppermute | solution.py:675

commit v7 on v6

--- a/solution.py
+++ b/solution.py
@@ -67,6 +67,14 @@
 
 def sigmoid(n):
     return 1.0 / (1.0 + jnp.exp(-n))
+
+
+def terms(row, count):
+    parts = []
+    for _ in range(count):
+        parts.append(row.astype(bf16).astype(f32))
+        row = row - parts[-1]
+    return parts
 
 
 def slot_weight(active_ref, s):
@@ -178,20 +186,19 @@
 
 
 def windows_of(pad, cols):
-    def one_layer(t, carry):
+    flat = pad.reshape(SLOTS * 6 * 6 * 8, C)
+    sub = lax.broadcasted_iota(jnp.int32, (8, C), 0)
+    for t in range(SLOTS * 6):
         s, a = t // 6, t % 6
-        sub = lax.broadcasted_iota(jnp.int32, (8, C), 0)
-        layer = [pad[s, a, b] for b in range(6)]
         for k2 in range(3):
-            low = [pltpu.roll(v, (8 - k2) % 8, 0) if k2 else v for v in layer]
-            high = [pltpu.roll(v, 4 - k2, 0) for v in layer]
-            pair = [jnp.where(sub < 4, low[b], high[b + 1]) for b in range(5)]
+            starts = [(6 * t + b) * 8 + k2 for b in range(5)]
+            pair = [
+                jnp.where(sub < 4, flat[first : first + 8], flat[first + 4 : first + 12])
+                for first in starts
+            ]
             for k1 in range(3):
                 tile = jnp.concatenate([pair[k1], pair[k1 + 2]], axis=0)
                 cols[3 * k1 + k2, s, a] = tile.astype(bf16)
-        return carry
-
-    lax.fori_loop(0, SLOTS * 6, one_layer, 0)
 
 
 def window(cols, k0, k1, k2):
@@ -452,19 +459,22 @@
         sum_q = sum_q + jnp.sum(q, axis=0, keepdims=True)
         sum_c = sum_c + jnp.sum(q * hat, axis=0, keepdims=True)
     packed = pack_stats([sum_q, sum_c])
+    sums = jnp.concatenate(terms(packed[0:1], 3), axis=0)
 
     def store(out, core):
+        kind = out.dtype
         for chip in range(PEERS // 2):
             p = 2 * chip + core
-            out[chip, 0:SHARE] = grad_w1[SHARE * p : SHARE * (p + 1)]
-            out[chip, SHARE : 2 * SHARE] = grad_w2[SHARE * p : SHARE * (p + 1)]
-            out[chip, SUM_ROW : SUM_ROW + 1] = packed[0:1]
-            out[chip, SUM_ROW + 1 : CENTRE_ROW] = jnp.zeros((3, C), f32)
-            out[chip, CENTRE_ROW : CENTRE_ROW + 1] = sums1[p : p + 1]
-            out[chip, CENTRE_ROW + 1 : CENTRE_ROW + 2] = centre1
-            out[chip, CENTRE_ROW + 2 : CENTRE_ROW + 3] = sums2[p : p + 1]
-            out[chip, CENTRE_ROW + 3 : CENTRE_ROW + 4] = centre2
-            out[chip, CENTRE_ROW + 4 : 120] = jnp.zeros((4, C), f32)
+            rows = [
+                grad_w1[SHARE * p : SHARE * (p + 1)],
+                grad_w2[SHARE * p : SHARE * (p + 1)],
+                sums,
+                jnp.zeros((1, C), f32),
+            ]
+            out[chip, 0:CENTRE_ROW] = jnp.concatenate(rows, axis=0).astype(kind)
+            rows = [*terms(sums1[p : p + 1], 2), centre1, *terms(sums2[p : p + 1], 2), centre2]
+            rows = jnp.concatenate([*rows, jnp.zeros((10, C), f32)], axis=0)
+            out[chip, CENTRE_ROW:ROWS] = rows.astype(kind)
 
     @pl.when(me % 2 == 0)
     def _():
@@ -478,26 +488,15 @@
 
 
 def pair_kernel(own, other, out):
-    def terms(row, count):
-        parts = []
-        for _ in range(count):
-            parts.append(row.astype(bf16).astype(f32))
-            row = row - parts[-1]
-        return parts
-
+    at = lax.broadcasted_iota(jnp.int32, (CENTRE_ROW, C), 0)
     for n in range(PEERS // 2):
-        total = own[n, 0:CENTRE_ROW] + other[n, 0:CENTRE_ROW]
-        at = lax.broadcasted_iota(jnp.int32, (CENTRE_ROW, C), 0)
-        for k, term in enumerate(terms(total[SUM_ROW : SUM_ROW + 1], 3)):
+        total = own[n, 0:CENTRE_ROW] + other[n, 0:CENTRE_ROW].astype(f32)
+        row = jnp.sum(total[SUM_ROW : SUM_ROW + 3], axis=0, keepdims=True)
+        for k, term in enumerate(terms(row, 3)):
             total = jnp.where(at == SUM_ROW + k, term, total)
         out[n, 0:CENTRE_ROW] = total.astype(bf16)
-        more = jnp.zeros((16, C), f32)
-        at = lax.broadcasted_iota(jnp.int32, (16, C), 0)
-        for core, ref in enumerate((own, other)):
-            rows = ref[n, CENTRE_ROW : CENTRE_ROW + 8]
-            lines = terms(rows[0:1], 2) + [rows[1:2]] + terms(rows[2:3], 2) + [rows[3:4]]
-            for k, line in enumerate(lines):
-                more = jnp.where(at == 6 * core + k, line, more)
+        more = other[n, CENTRE_ROW:ROWS].astype(f32)
+        more = own[n, CENTRE_ROW:ROWS] + pltpu.roll(more, 6, 0)
         out[n, CENTRE_ROW:ROWS] = more.astype(bf16)
 
 
@@ -667,7 +666,8 @@
     block, q1, keep, give = call(
         third_kernel,
         [vmem, vmem, smem, smem] + [vmem] * 15,
-        [shape(*field, dtype=bf16), shape(*field)] + [shape(PEERS // 2, 120, C)] * 2,
+        [shape(*field, dtype=bf16), shape(*field)]
+        + [shape(PEERS // 2, ROWS, C), shape(PEERS // 2, ROWS, C, dtype=bf16)],
         [table, table, pad, cols, wide, two, scratch, weight, weight, line, line],
         (feat, gout, active, index, middle, gas, stats1, stats2, stats3)
         + (gain1, bias1, gain2, bias2, conv_first, conv_second, cols_a, *fields1),

time: 167 us -> 165 us (0.988)
  no operation moved by 1% of the time
where the time goes in v7:
time: 165 us; the launch traced here: 164 us
  blocking collectives  108 us (65%)
  starting transfers between devices  31.6 us (19%)
  Pallas kernels  16.1 us (10%)
  waiting for transfers between devices  7.05 us (4%)
    all_to_all x3, blocking collectives, spread(): return lax.all_to_all(stats, 'space', 0, 0, tiled=True)  52.2 us
    all_to_all x1, blocking collectives, per_device(): share = lax.all_to_all(share, 'space', 0, 0, axis_index_groups=chip_groups)  32.8 us
    all_to_all x1, blocking collectives, per_device(): rows = lax.all_to_all(rows, 'scene', 0, 0)  22.9 us
    ppermute x4, starting transfers between devices, exchange(): far = [lax.ppermute(fields, 'space', pairs) for pairs in far_pairs]  20.3 us
    pallas_call x7, Pallas kernels, call(): pl.pallas_call(kernel, in_specs=specs, out_specs=out_specs or [vmem] * le...  16.1 us
    ppermute x4, starting transfers between devices, exchange(): near = [lax.ppermute(three, 'space', pairs) for pairs in near_pairs]  9.35 us
    ppermute x4, waiting for transfers between devices, exchange(): near = [lax.ppermute(three, 'space', pairs) for pairs in near_pairs]  4.41 us
  transfers between devices with their start and end apart: 9, of which 2 were waited for; matrix products, arithmetic and copies ran while one was open for 0% of the time, Pallas kernels for 1%

profile of v7, /device:TPU:64, one launch (start us, length us, event | category | flops | bytes accessed | tf_op | source)
XLA Modules:
  0.0 164.3 jit_solution(4023636000935510619)
XLA Ops:
  0.6 0.0 copy-start.4
  0.6 1.1 shard_map.147
  1.8 12.2 %collective-permute-start.1 = (bf16[2,4,64,128]{3,2,1,0:T(8,128)(2,1)S(1)}, bf16[2,4,64,128]{3,2,1,0:T(8,128)(2,1)S(1)}, u32[]{:S(2)}, u32[]{:S(2)}) collective-permute-start(bf16[2,4,64,128]{3,2,1,0:T(8,128)(2,1)S(1)} %get-tuple-element.23), channel_id=1, source_target_pairs={{4,8},{5,9},{6,10},{7,11},{12,16},{13,17},{14,18},{15,19},{20,24},... | collective-permute-start | bytes 393224 | tf_op jit(solution)/shard_map/ppermute | solution.py:574
  14.0 1.9 %collective-permute-start = (bf16[2,4,64,128]{3,2,1,0:T(8,128)(2,1)S(1)}, bf16[2,4,64,128]{3,2,1,0:T(8,128)(2,1)S(1)}, u32[]{:S(2)}, u32[]{:S(2)}) collective-permute-start(bf16[2,4,64,128]{3,2,1,0:T(8,128)(2,1)S(1)} %get-tuple-element.23), channel_id=1, source_target_pairs={{0,4},{1,5},{2,6},{3,7},{8,12},{9,13},{10,14},{11,15},{16,20},{17,... | collective-permute-start | bytes 393224 | tf_op jit(solution)/shard_map/ppermute | solution.py:574
  15.9 14.8 %all_to_all.45 = f32[64,1,128]{2,1,0:T(1,128)S(1)} all-to-all(f32[64,1,128]{2,1,0:T(1,128)S(1)} %bitcast.47), channel_id=1, replica_groups=mesh['scene'=8,'space'=64] {'space'}, dimensions={0} | all-to-all | bytes 65536 | tf_op jit(solution)/shard_map/all_to_all | solution.py:583
  30.8 0.0 collective-permute-done.1
  30.8 0.0 collective-permute-done
  30.8 0.0 copy-start.7
  30.8 0.0 copy-start.8
  30.8 2.8 %collective-permute-start.3 = (bf16[3,2,4,64,128]{4,3,2,1,0:T(8,128)(2,1)S(1)}, bf16[3,2,4,64,128]{4,3,2,1,0:T(8,128)(2,1)S(1)}, u32[]{:S(2)}, u32[]{:S(2)}) collective-permute-start(bf16[3,2,4,64,128]{4,3,2,1,0:T(8,128)(2,1)S(1)} %pad_maximum_fusion.rest_0_), channel_id=1, source_target_pairs={{1,2},{3,4},{5,6},{7,8},{9,10},{11,12},{13,14},{15,16},{17,18},{19... | collective-permute-start | bytes 1179656 | tf_op jit(solution)/shard_map/ppermute | solution.py:578
  33.6 1.9 %collective-permute-start.2 = (bf16[3,2,4,64,128]{4,3,2,1,0:T(8,128)(2,1)S(1)}, bf16[3,2,4,64,128]{4,3,2,1,0:T(8,128)(2,1)S(1)}, u32[]{:S(2)}, u32[]{:S(2)}) collective-permute-start(bf16[3,2,4,64,128]{4,3,2,1,0:T(8,128)(2,1)S(1)} %pad_maximum_fusion.rest_0_), channel_id=1, source_target_pairs={{0,1},{2,3},{4,5},{6,7},{8,9},{10,11},{12,13},{14,15},{16,17},{18,... | collective-permute-start | bytes 1179656 | tf_op jit(solution)/shard_map/ppermute | solution.py:578
  35.5 4.4 %collective-permute-done.3.rest_2_ = bf16[3,2,4,64,128]{4,3,2,1,0:T(8,128)(2,1)S(1)} collective-permute-done((bf16[3,2,4,64,128]{4,3,2,1,0:T(8,128)(2,1)S(1)}, bf16[3,2,4,64,128]{4,3,2,1,0:T(8,128)(2,1)S(1)}, u32[]{:S(2)}, u32[]{:S(2)}) %collective-permute-start.3) | collective-permute-done | bytes 393248 | tf_op jit(solution)/shard_map/ppermute | solution.py:578
  39.9 0.0 collective-permute-done.2.rest_1_
  39.9 0.0 copy-start
  40.0 0.0 copy-start.1
  40.0 0.0 copy-start.3
  40.0 0.0 copy-start.5
  40.0 0.0 copy-start.6
  40.0 4.7 %shard_map.148 = (f32[4,64,128]{2,1,0:T(8,128)S(1)}, f32[4,64,128]{2,1,0:T(8,128)S(1)}, bf16[9,4,6,16,128]{4,3,2,1,0:T(8,128)(2,1)S(1)}, bf16[2,4,64,128]{3,2,1,0:T(8,128)(2,1)S(1)}, s32[4,26]{1,0:T(4,128)S(1)}) custom-call(s32[1,4]{1,0:T(1,128)} %active.7, s32[4,26]{1,0:T(4,128)} %bitcast.62, s32[4,26]{1,0:T(4,128)} %bitcast.63, f32[1,128]{1,0:T(1,128)} %bitcast.48, ...), custom_call_target="tpu_custom_call" | custom-call | tf_op jit(solution)/shard_map/pallas_call | solution.py:550
  44.7 4.3 %collective-permute-start.5 = (bf16[2,4,64,128]{3,2,1,0:T(8,128)(2,1)S(1)}, bf16[2,4,64,128]{3,2,1,0:T(8,128)(2,1)S(1)}, u32[]{:S(2)}, u32[]{:S(2)}) collective-permute-start(bf16[2,4,64,128]{3,2,1,0:T(8,128)(2,1)S(1)} %get-tuple-element.31), channel_id=1, source_target_pairs={{4,8},{5,9},{6,10},{7,11},{12,16},{13,17},{14,18},{15,19},{20,24},... | collective-permute-start | bytes 393224 | tf_op jit(solution)/shard_map/ppermute | solution.py:574
  48.9 1.9 %collective-permute-start.4 = (bf16[2,4,64,128]{3,2,1,0:T(8,128)(2,1)S(1)}, bf16[2,4,64,128]{3,2,1,0:T(8,128)(2,1)S(1)}, u32[]{:S(2)}, u32[]{:S(2)}) collective-permute-start(bf16[2,4,64,128]{3,2,1,0:T(8,128)(2,1)S(1)} %get-tuple-element.31), channel_id=1, source_target_pairs={{0,4},{1,5},{2,6},{3,7},{8,12},{9,13},{10,14},{11,15},{16,20},{17,... | collective-permute-start | bytes 393224 | tf_op jit(solution)/shard_map/ppermute | solution.py:574
  50.9 0.0 copy-done.4
  50.9 0.7 shard_map.149
  51.6 21.2 %all_to_all.46 = f32[64,1,128]{2,1,0:T(1,128)S(1)} all-to-all(f32[64,1,128]{2,1,0:T(1,128)S(1)} %bitcast.43), channel_id=1, replica_groups=mesh['scene'=8,'space'=64] {'space'}, dimensions={0} | all-to-all | bytes 65536 | tf_op jit(solution)/shard_map/all_to_all | solution.py:583
  72.7 0.0 collective-permute-done.5
  72.7 0.0 collective-permute-done.4
  72.8 2.8 %collective-permute-start.7 = (bf16[3,2,4,64,128]{4,3,2,1,0:T(8,128)(2,1)S(1)}, bf16[3,2,4,64,128]{4,3,2,1,0:T(8,128)(2,1)S(1)}, u32[]{:S(2)}, u32[]{:S(2)}) collective-permute-start(bf16[3,2,4,64,128]{4,3,2,1,0:T(8,128)(2,1)S(1)} %pad_maximum_fusion.1.rest_0_), channel_id=1, source_target_pairs={{1,2},{3,4},{5,6},{7,8},{9,10},{11,12},{13,14},{15,16},{17,18},{19... | collective-permute-start | bytes 1179656 | tf_op jit(solution)/shard_map/ppermute | solution.py:578
  75.5 1.9 %collective-permute-start.6 = (bf16[3,2,4,64,128]{4,3,2,1,0:T(8,128)(2,1)S(1)}, bf16[3,2,4,64,128]{4,3,2,1,0:T(8,128)(2,1)S(1)}, u32[]{:S(2)}, u32[]{:S(2)}) collective-permute-start(bf16[3,2,4,64,128]{4,3,2,1,0:T(8,128)(2,1)S(1)} %pad_maximum_fusion.1.rest_0_), channel_id=1, source_target_pairs={{0,1},{2,3},{4,5},{6,7},{8,9},{10,11},{12,13},{14,15},{16,17},{18,... | collective-permute-start | bytes 1179656 | tf_op jit(solution)/shard_map/ppermute | solution.py:578
  77.5 0.0 copy-done.7
  77.5 0.0 copy-done.8
  77.5 0.9 shard_map.150
  78.4 16.2 %all_to_all.47 = f32[64,1,128]{2,1,0:T(1,128)S(1)} all-to-all(f32[64,1,128]{2,1,0:T(1,128)S(1)} %bitcast.44), channel_id=1, replica_groups=mesh['scene'=8,'space'=64] {'space'}, dimensions={0} | all-to-all | bytes 65536 | tf_op jit(solution)/shard_map/all_to_all | solution.py:583
  94.6 0.0 collective-permute-done.7.rest_2_
  94.6 0.0 collective-permute-done.6.rest_1_
  94.6 0.0 copy-done
  94.6 0.0 copy-done.1
  94.6 0.0 copy-done.2
  94.7 0.0 copy-done.3
  94.7 0.0 copy-done.5
  94.7 0.0 copy-done.6
  94.7 6.9 %shard_map.151 = (bf16[4,64,128]{2,1,0:T(8,128)(2,1)}, f32[4,64,128]{2,1,0:T(8,128)S(1)}, f32[32,128,128]{2,1,0:T(8,128)S(1)}, bf16[32,128,128]{2,1,0:T(8,128)(2,1)S(1)}) custom-call(bf16[4,64,128]{2,1,0:T(8,128)(2,1)S(1)} %bitcast.32, bf16[4,64,128]{2,1,0:T(8,128)(2,1)S(1)} %bitcast.35, s32[1,4]{1,0:T(1,128)S(1)} %copy-done.4, ...), custom_call_target="tpu_custom_call" | custom-call | tf_op jit(solution)/shard_map/pallas_call | solution.py:550
  101.5 1.9 %collective-permute-start.8 = (bf16[32,128,128]{2,1,0:T(8,128)(2,1)S(1)}, bf16[32,128,128]{2,1,0:T(8,128)(2,1)S(1)}, u32[]{:S(2)}, u32[]{:S(2)}) collective-permute-start(bf16[32,128,128]{2,1,0:T(8,128)(2,1)S(1)} %get-tuple-element.39), channel_id=1, source_target_pairs={{0,1},{2,3},{4,5},{6,7},{8,9},{10,11},{12,13},{14,15},{16,17},{18,... | collective-permute-start | bytes 3145736 | tf_op jit(solution)/shard_map/ppermute | solution.py:675
  103.5 2.6 %collective-permute-done.8.other = bf16[32,128,128]{2,1,0:T(8,128)(2,1)S(1)} collective-permute-done((bf16[32,128,128]{2,1,0:T(8,128)(2,1)S(1)}, bf16[32,128,128]{2,1,0:T(8,128)(2,1)S(1)}, u32[]{:S(2)}, u32[]{:S(2)}) %collective-permute-start.8) | collective-permute-done | bytes 1048608 | tf_op jit(solution)/shard_map/ppermute | solution.py:675
  106.1 0.3 shard_map.152
  106.4 32.8 %all_to_all.48.parts = bf16[32,128,128]{2,1,0:T(8,128)(2,1)S(1)} all-to-all(bf16[32,128,128]{2,1,0:T(8,128)(2,1)S(1)} %shard_map.152), channel_id=1, replica_groups={{0,2,4,6,8,10,12,14,16,18,20,22,24,26,28,30,32,34,36,38,40,42,44,46,48,..., dimensions={0} | all-to-all | bytes 2097152 | tf_op jit(solution)/shard_map/all_to_all | solution.py:683
  139.2 1.5 shard_map.153
  140.7 22.9 %all_to_all.49 = f32[8,112,128]{2,1,0:T(8,128)S(1)} all-to-all(f32[8,112,128]{2,1,0:T(8,128)S(1)} %get-tuple-element.41), channel_id=1, replica_groups=mesh['scene'=8,'space'=64] {'scene'}, dimensions={0} | all-to-all | bytes 917504 | tf_op jit(solution)/shard_map/all_to_all | solution.py:692
  163.7 0.6 fusion
  (4 shorter events, 0.1 us)
Async XLA Ops:
  0.6 50.2 %copy-start.4 = (s32[1,4]{1,0:T(1,128)S(1)}, s32[1,4]{1,0:T(1,128)}, u32[]{:S(2)}) copy-start(s32[1,4]{1,0:T(1,128)} %active.7) | copy-start | bytes 52
  1.8 29.0 %collective-permute-start.1 = (bf16[2,4,64,128]{3,2,1,0:T(8,128)(2,1)S(1)}, bf16[2,4,64,128]{3,2,1,0:T(8,128)(2,1)S(1)}, u32[]{:S(2)}, u32[]{:S(2)}) collective-permute-start(bf16[2,4,64,128]{3,2,1,0:T(8,128)(2,1)S(1)} %get-tuple-element.23), channel_id=1, source_target_pairs={{4,8},{5,9},{6,10},{7,11},{12,16},{13,17},{14,18},{15,19},{20,24},... | collective-permute-start | bytes 393224 | tf_op jit(solution)/shard_map/ppermute | solution.py:574
  14.0 16.8 %collective-permute-start = (bf16[2,4,64,128]{3,2,1,0:T(8,128)(2,1)S(1)}, bf16[2,4,64,128]{3,2,1,0:T(8,128)(2,1)S(1)}, u32[]{:S(2)}, u32[]{:S(2)}) collective-permute-start(bf16[2,4,64,128]{3,2,1,0:T(8,128)(2,1)S(1)} %get-tuple-element.23), channel_id=1, source_target_pairs={{0,4},{1,5},{2,6},{3,7},{8,12},{9,13},{10,14},{11,15},{16,20},{17,... | collective-permute-start | bytes 393224 | tf_op jit(solution)/shard_map/ppermute | solution.py:574
  30.8 46.7 %copy-start.7 = (f32[128]{0:T(128)S(1)}, f32[128]{0:T(128)}, u32[]{:S(2)}) copy-start(f32[128]{0:T(128)} %param.21) | copy-start | bytes 1540
  30.8 46.7 %copy-start.8 = (f32[128]{0:T(128)S(1)}, f32[128]{0:T(128)}, u32[]{:S(2)}) copy-start(f32[128]{0:T(128)} %param.22) | copy-start | bytes 1540
  30.8 9.1 %collective-permute-start.3 = (bf16[3,2,4,64,128]{4,3,2,1,0:T(8,128)(2,1)S(1)}, bf16[3,2,4,64,128]{4,3,2,1,0:T(8,128)(2,1)S(1)}, u32[]{:S(2)}, u32[]{:S(2)}) collective-permute-start(bf16[3,2,4,64,128]{4,3,2,1,0:T(8,128)(2,1)S(1)} %pad_maximum_fusion.rest_0_), channel_id=1, source_target_pairs={{1,2},{3,4},{5,6},{7,8},{9,10},{11,12},{13,14},{15,16},{17,18},{19... | collective-permute-start | bytes 1179656 | tf_op jit(solution)/shard_map/ppermute | solution.py:578
  33.6 6.3 %collective-permute-start.2 = (bf16[3,2,4,64,128]{4,3,2,1,0:T(8,128)(2,1)S(1)}, bf16[3,2,4,64,128]{4,3,2,1,0:T(8,128)(2,1)S(1)}, u32[]{:S(2)}, u32[]{:S(2)}) collective-permute-start(bf16[3,2,4,64,128]{4,3,2,1,0:T(8,128)(2,1)S(1)} %pad_maximum_fusion.rest_0_), channel_id=1, source_target_pairs={{0,1},{2,3},{4,5},{6,7},{8,9},{10,11},{12,13},{14,15},{16,17},{18,... | collective-permute-start | bytes 1179656 | tf_op jit(solution)/shard_map/ppermute | solution.py:578
  39.9 54.7 %copy-start = (bf16[27,128,128]{2,1,0:T(8,128)(2,1)S(1)}, bf16[27,128,128]{2,1,0:T(8,128)(2,1)}, u32[]{:S(2)}) copy-start(bf16[27,128,128]{2,1,0:T(8,128)(2,1)} %w1.1) | copy-start | bytes 2654212
  40.0 54.7 %copy-start.1 = (bf16[27,128,128]{2,1,0:T(8,128)(2,1)S(1)}, bf16[27,128,128]{2,1,0:T(8,128)(2,1)}, u32[]{:S(2)}) copy-start(bf16[27,128,128]{2,1,0:T(8,128)(2,1)} %w2.1) | copy-start | bytes 2654212
  40.0 54.7 %copy-start.2 = (bf16[1,4,64,128]{3,2,1,0:T(8,128)(2,1)S(1)}, bf16[1,4,64,128]{3,2,1,0:T(8,128)(2,1)}, u32[]{:S(2)}) copy-start(bf16[1,4,64,128]{3,2,1,0:T(8,128)(2,1)} %param.12) | copy-start | bytes 196612
  40.0 54.7 %copy-start.3 = (bf16[1,4,64,128]{3,2,1,0:T(8,128)(2,1)S(1)}, bf16[1,4,64,128]{3,2,1,0:T(8,128)(2,1)}, u32[]{:S(2)}) copy-start(bf16[1,4,64,128]{3,2,1,0:T(8,128)(2,1)} %param.23) | copy-start | bytes 196612
  40.0 54.7 %copy-start.5 = (f32[128]{0:T(128)S(1)}, f32[128]{0:T(128)}, u32[]{:S(2)}) copy-start(f32[128]{0:T(128)} %param.19) | copy-start | bytes 1540
  40.0 54.7 %copy-start.6 = (f32[128]{0:T(128)S(1)}, f32[128]{0:T(128)}, u32[]{:S(2)}) copy-start(f32[128]{0:T(128)} %param.20) | copy-start | bytes 1540
  44.7 28.1 %collective-permute-start.5 = (bf16[2,4,64,128]{3,2,1,0:T(8,128)(2,1)S(1)}, bf16[2,4,64,128]{3,2,1,0:T(8,128)(2,1)S(1)}, u32[]{:S(2)}, u32[]{:S(2)}) collective-permute-start(bf16[2,4,64,128]{3,2,1,0:T(8,128)(2,1)S(1)} %get-tuple-element.31), channel_id=1, source_target_pairs={{4,8},{5,9},{6,10},{7,11},{12,16},{13,17},{14,18},{15,19},{20,24},... | collective-permute-start | bytes 393224 | tf_op jit(solution)/shard_map/ppermute | solution.py:574
  48.9 23.8 %collective-permute-start.4 = (bf16[2,4,64,128]{3,2,1,0:T(8,128)(2,1)S(1)}, bf16[2,4,64,128]{3,2,1,0:T(8,128)(2,1)S(1)}, u32[]{:S(2)}, u32[]{:S(2)}) collective-permute-start(bf16[2,4,64,128]{3,2,1,0:T(8,128)(2,1)S(1)} %get-tuple-element.31), channel_id=1, source_target_pairs={{0,4},{1,5},{2,6},{3,7},{8,12},{9,13},{10,14},{11,15},{16,20},{17,... | collective-permute-start | bytes 393224 | tf_op jit(solution)/shard_map/ppermute | solution.py:574
  72.8 21.8 %collective-permute-start.7 = (bf16[3,2,4,64,128]{4,3,2,1,0:T(8,128)(2,1)S(1)}, bf16[3,2,4,64,128]{4,3,2,1,0:T(8,128)(2,1)S(1)}, u32[]{:S(2)}, u32[]{:S(2)}) collective-permute-start(bf16[3,2,4,64,128]{4,3,2,1,0:T(8,128)(2,1)S(1)} %pad_maximum_fusion.1.rest_0_), channel_id=1, source_target_pairs={{1,2},{3,4},{5,6},{7,8},{9,10},{11,12},{13,14},{15,16},{17,18},{19... | collective-permute-start | bytes 1179656 | tf_op jit(solution)/shard_map/ppermute | solution.py:578
  75.5 19.1 %collective-permute-start.6 = (bf16[3,2,4,64,128]{4,3,2,1,0:T(8,128)(2,1)S(1)}, bf16[3,2,4,64,128]{4,3,2,1,0:T(8,128)(2,1)S(1)}, u32[]{:S(2)}, u32[]{:S(2)}) collective-permute-start(bf16[3,2,4,64,128]{4,3,2,1,0:T(8,128)(2,1)S(1)} %pad_maximum_fusion.1.rest_0_), channel_id=1, source_target_pairs={{0,1},{2,3},{4,5},{6,7},{8,9},{10,11},{12,13},{14,15},{16,17},{18,... | collective-permute-start | bytes 1179656 | tf_op jit(solution)/shard_map/ppermute | solution.py:578
  101.5 4.5 %collective-permute-start.8 = (bf16[32,128,128]{2,1,0:T(8,128)(2,1)S(1)}, bf16[32,128,128]{2,1,0:T(8,128)(2,1)S(1)}, u32[]{:S(2)}, u32[]{:S(2)}) collective-permute-start(bf16[32,128,128]{2,1,0:T(8,128)(2,1)S(1)} %get-tuple-element.39), channel_id=1, source_target_pairs={{0,1},{2,3},{4,5},{6,7},{8,9},{10,11},{12,13},{14,15},{16,17},{18,... | collective-permute-start | bytes 3145736 | tf_op jit(solution)/shard_map/ppermute | solution.py:675

commit v8 on v7

--- a/solution.py
+++ b/solution.py
@@ -13,7 +13,7 @@
 PEERS = 64
 PLANE = 16
 SHARE = 54
-ROWS = 128
+ROWS = 120
 SUM_ROW = 108
 CENTRE_ROW = 112
 GROUP_COUNT = 64 * 4
@@ -460,6 +460,7 @@
         sum_c = sum_c + jnp.sum(q * hat, axis=0, keepdims=True)
     packed = pack_stats([sum_q, sum_c])
     sums = jnp.concatenate(terms(packed[0:1], 3), axis=0)
+    sums1[...], sums2[...] = terms(sums1[...] + pltpu.roll(sums2[...], C // 2, 1), 2)
 
     def store(out, core):
         kind = out.dtype
@@ -472,8 +473,8 @@
                 jnp.zeros((1, C), f32),
             ]
             out[chip, 0:CENTRE_ROW] = jnp.concatenate(rows, axis=0).astype(kind)
-            rows = [*terms(sums1[p : p + 1], 2), centre1, *terms(sums2[p : p + 1], 2), centre2]
-            rows = jnp.concatenate([*rows, jnp.zeros((10, C), f32)], axis=0)
+            rows = [sums1[p : p + 1], sums2[p : p + 1], centre1, centre2]
+            rows = jnp.concatenate([*rows, jnp.zeros((4, C), f32)], axis=0)
             out[chip, CENTRE_ROW:ROWS] = rows.astype(kind)
 
     @pl.when(me % 2 == 0)
@@ -496,7 +497,7 @@
             total = jnp.where(at == SUM_ROW + k, term, total)
         out[n, 0:CENTRE_ROW] = total.astype(bf16)
         more = other[n, CENTRE_ROW:ROWS].astype(f32)
-        more = own[n, CENTRE_ROW:ROWS] + pltpu.roll(more, 6, 0)
+        more = own[n, CENTRE_ROW:ROWS] + pltpu.roll(more, 4, 0)
         out[n, CENTRE_ROW:ROWS] = more.astype(bf16)
 
 
@@ -514,24 +515,25 @@
         back = slot_weight(active, s) * inv1 * (q1[s] - mean_q - hat * mean_c)
         top = jnp.where(active[0, s] > 0, gout[s].astype(f32), 0.0)
         grad_in[s] = (top + back).astype(bf16)
-    left = [[], []]
-    right = [[], []]
+    left, right = [], []
+    at = lax.broadcasted_iota(jnp.int32, (8, C), 0) % 4
     for n in range(PEERS // 2):
         more = parts[n, CENTRE_ROW:ROWS].astype(f32)
-        for core in range(2):
-            for weight in range(2):
-                first = 6 * core + 3 * weight
-                line = more[first + 2 : first + 3]
-                left[weight] += [more[first : first + 1], more[first + 1 : first + 2]]
-                right[weight] += [line, line]
+        left.append(more)
+        line = []
+        for weight in range(2):
+            near = jnp.where(at == 1, pltpu.roll(more, 7 - weight, 0), 0.0)
+            line.append(jnp.where(at == 0, pltpu.roll(more, 6 - weight, 0), near))
+        right.append(jnp.concatenate(line, axis=1))
+    outer = lax.dot_general(
+        jnp.concatenate(left, axis=0).astype(bf16),
+        jnp.concatenate(right, axis=0).astype(bf16),
+        (((0,), (0,)), ((), ())),
+        preferred_element_type=f32,
+    )
     for weight in range(2):
-        outer = lax.dot_general(
-            jnp.concatenate(left[weight], axis=0).astype(bf16),
-            jnp.concatenate(right[weight], axis=0).astype(bf16),
-            (((0,), (0,)), ((), ())),
-            preferred_element_type=f32,
-        )
-        whole = total[SHARE * weight : SHARE * (weight + 1)] + outer[0:SHARE]
+        back = outer[64 * weight : 64 * weight + SHARE, C * weight : C * (weight + 1)]
+        whole = total[SHARE * weight : SHARE * (weight + 1)] + back
         for n in range(8):
             rows[n, 56 * weight : 56 * weight + SHARE] = whole
             rows[n, 56 * weight + SHARE : 56 * weight + 56] = jnp.zeros((2, C), f32)

time: 165 us -> 163 us (0.988)
  no operation moved by 1% of the time
where the time goes in v8:
time: 163 us
  blocking collectives  107 us (66%)
  starting transfers between devices  31.6 us (19%)
  Pallas kernels  16 us (10%)
  waiting for transfers between devices  6.96 us (4%)
    all_to_all x3, blocking collectives, spread(): return lax.all_to_all(stats, 'space', 0, 0, tiled=True)  52.2 us
    all_to_all x1, blocking collectives, per_device(): share = lax.all_to_all(share, 'space', 0, 0, axis_index_groups=chip_groups)  31.5 us
    all_to_all x1, blocking collectives, per_device(): rows = lax.all_to_all(rows, 'scene', 0, 0)  22.9 us
    ppermute x4, starting transfers between devices, exchange(): far = [lax.ppermute(fields, 'space', pairs) for pairs in far_pairs]  20.3 us
    pallas_call x7, Pallas kernels, call(): pl.pallas_call(kernel, in_specs=specs, out_specs=out_specs or [vmem] * le...  16 us
    ppermute x4, starting transfers between devices, exchange(): near = [lax.ppermute(three, 'space', pairs) for pairs in near_pairs]  9.35 us
    ppermute x4, waiting for transfers between devices, exchange(): near = [lax.ppermute(three, 'space', pairs) for pairs in near_pairs]  4.41 us
  transfers between devices with their start and end apart: 9, of which 2 were waited for; matrix products, arithmetic and copies ran while one was open for 0% of the time, Pallas kernels for 1%

profile of v8, /device:TPU:64, one launch (start us, length us, event | category | flops | bytes accessed | tf_op | source)
XLA Modules:
  0.0 162.7 jit_solution(11658103769153048853)
XLA Ops:
  0.6 1.1 shard_map.147
  1.8 0.0 copy-start.4
  1.8 12.2 %collective-permute-start.1 = (bf16[2,4,64,128]{3,2,1,0:T(8,128)(2,1)S(1)}, bf16[2,4,64,128]{3,2,1,0:T(8,128)(2,1)S(1)}, u32[]{:S(2)}, u32[]{:S(2)}) collective-permute-start(bf16[2,4,64,128]{3,2,1,0:T(8,128)(2,1)S(1)} %get-tuple-element.23), channel_id=1, source_target_pairs={{4,8},{5,9},{6,10},{7,11},{12,16},{13,17},{14,18},{15,19},{20,24},... | collective-permute-start | bytes 393224 | tf_op jit(solution)/shard_map/ppermute | solution.py:576
  14.0 1.9 %collective-permute-start = (bf16[2,4,64,128]{3,2,1,0:T(8,128)(2,1)S(1)}, bf16[2,4,64,128]{3,2,1,0:T(8,128)(2,1)S(1)}, u32[]{:S(2)}, u32[]{:S(2)}) collective-permute-start(bf16[2,4,64,128]{3,2,1,0:T(8,128)(2,1)S(1)} %get-tuple-element.23), channel_id=1, source_target_pairs={{0,4},{1,5},{2,6},{3,7},{8,12},{9,13},{10,14},{11,15},{16,20},{17,... | collective-permute-start | bytes 393224 | tf_op jit(solution)/shard_map/ppermute | solution.py:576
  15.9 14.8 %all_to_all.45 = f32[64,1,128]{2,1,0:T(1,128)S(1)} all-to-all(f32[64,1,128]{2,1,0:T(1,128)S(1)} %bitcast.47), channel_id=1, replica_groups=mesh['scene'=8,'space'=64] {'space'}, dimensions={0} | all-to-all | bytes 65536 | tf_op jit(solution)/shard_map/all_to_all | solution.py:585
  30.8 0.0 collective-permute-done.1
  30.8 0.0 collective-permute-done
  30.8 2.8 %collective-permute-start.3 = (bf16[3,2,4,64,128]{4,3,2,1,0:T(8,128)(2,1)S(1)}, bf16[3,2,4,64,128]{4,3,2,1,0:T(8,128)(2,1)S(1)}, u32[]{:S(2)}, u32[]{:S(2)}) collective-permute-start(bf16[3,2,4,64,128]{4,3,2,1,0:T(8,128)(2,1)S(1)} %pad_maximum_fusion.rest_0_), channel_id=1, source_target_pairs={{1,2},{3,4},{5,6},{7,8},{9,10},{11,12},{13,14},{15,16},{17,18},{19... | collective-permute-start | bytes 1179656 | tf_op jit(solution)/shard_map/ppermute | solution.py:580
  33.6 1.9 %collective-permute-start.2 = (bf16[3,2,4,64,128]{4,3,2,1,0:T(8,128)(2,1)S(1)}, bf16[3,2,4,64,128]{4,3,2,1,0:T(8,128)(2,1)S(1)}, u32[]{:S(2)}, u32[]{:S(2)}) collective-permute-start(bf16[3,2,4,64,128]{4,3,2,1,0:T(8,128)(2,1)S(1)} %pad_maximum_fusion.rest_0_), channel_id=1, source_target_pairs={{0,1},{2,3},{4,5},{6,7},{8,9},{10,11},{12,13},{14,15},{16,17},{18,... | collective-permute-start | bytes 1179656 | tf_op jit(solution)/shard_map/ppermute | solution.py:580
  35.5 4.4 %collective-permute-done.3.rest_2_ = bf16[3,2,4,64,128]{4,3,2,1,0:T(8,128)(2,1)S(1)} collective-permute-done((bf16[3,2,4,64,128]{4,3,2,1,0:T(8,128)(2,1)S(1)}, bf16[3,2,4,64,128]{4,3,2,1,0:T(8,128)(2,1)S(1)}, u32[]{:S(2)}, u32[]{:S(2)}) %collective-permute-start.3) | collective-permute-done | bytes 393248 | tf_op jit(solution)/shard_map/ppermute | solution.py:580
  39.9 0.0 collective-permute-done.2.rest_1_
  39.9 0.0 copy-start.7
  39.9 0.0 copy-start
  39.9 0.0 copy-start.1
  39.9 0.0 copy-start.2
  40.0 0.0 copy-start.3
  40.0 0.0 copy-start.5
  40.0 0.0 copy-start.6
  40.0 4.7 %shard_map.148 = (f32[4,64,128]{2,1,0:T(8,128)S(1)}, f32[4,64,128]{2,1,0:T(8,128)S(1)}, bf16[9,4,6,16,128]{4,3,2,1,0:T(8,128)(2,1)S(1)}, bf16[2,4,64,128]{3,2,1,0:T(8,128)(2,1)S(1)}, s32[4,26]{1,0:T(4,128)S(1)}) custom-call(s32[1,4]{1,0:T(1,128)} %active.7, s32[4,26]{1,0:T(4,128)} %bitcast.62, s32[4,26]{1,0:T(4,128)} %bitcast.63, f32[1,128]{1,0:T(1,128)} %bitcast.48, ...), custom_call_target="tpu_custom_call" | custom-call | tf_op jit(solution)/shard_map/pallas_call | solution.py:552
  44.7 4.3 %collective-permute-start.5 = (bf16[2,4,64,128]{3,2,1,0:T(8,128)(2,1)S(1)}, bf16[2,4,64,128]{3,2,1,0:T(8,128)(2,1)S(1)}, u32[]{:S(2)}, u32[]{:S(2)}) collective-permute-start(bf16[2,4,64,128]{3,2,1,0:T(8,128)(2,1)S(1)} %get-tuple-element.31), channel_id=1, source_target_pairs={{4,8},{5,9},{6,10},{7,11},{12,16},{13,17},{14,18},{15,19},{20,24},... | collective-permute-start | bytes 393224 | tf_op jit(solution)/shard_map/ppermute | solution.py:576
  48.9 1.9 %collective-permute-start.4 = (bf16[2,4,64,128]{3,2,1,0:T(8,128)(2,1)S(1)}, bf16[2,4,64,128]{3,2,1,0:T(8,128)(2,1)S(1)}, u32[]{:S(2)}, u32[]{:S(2)}) collective-permute-start(bf16[2,4,64,128]{3,2,1,0:T(8,128)(2,1)S(1)} %get-tuple-element.31), channel_id=1, source_target_pairs={{0,4},{1,5},{2,6},{3,7},{8,12},{9,13},{10,14},{11,15},{16,20},{17,... | collective-permute-start | bytes 393224 | tf_op jit(solution)/shard_map/ppermute | solution.py:576
  50.9 0.0 copy-done.4
  50.9 0.7 shard_map.149
  51.6 21.2 %all_to_all.46 = f32[64,1,128]{2,1,0:T(1,128)S(1)} all-to-all(f32[64,1,128]{2,1,0:T(1,128)S(1)} %bitcast.43), channel_id=1, replica_groups=mesh['scene'=8,'space'=64] {'space'}, dimensions={0} | all-to-all | bytes 65536 | tf_op jit(solution)/shard_map/all_to_all | solution.py:585
  72.7 0.0 collective-permute-done.5
  72.7 0.0 collective-permute-done.4
  72.8 2.8 %collective-permute-start.7 = (bf16[3,2,4,64,128]{4,3,2,1,0:T(8,128)(2,1)S(1)}, bf16[3,2,4,64,128]{4,3,2,1,0:T(8,128)(2,1)S(1)}, u32[]{:S(2)}, u32[]{:S(2)}) collective-permute-start(bf16[3,2,4,64,128]{4,3,2,1,0:T(8,128)(2,1)S(1)} %pad_maximum_fusion.1.rest_0_), channel_id=1, source_target_pairs={{1,2},{3,4},{5,6},{7,8},{9,10},{11,12},{13,14},{15,16},{17,18},{19... | collective-permute-start | bytes 1179656 | tf_op jit(solution)/shard_map/ppermute | solution.py:580
  75.5 1.9 %collective-permute-start.6 = (bf16[3,2,4,64,128]{4,3,2,1,0:T(8,128)(2,1)S(1)}, bf16[3,2,4,64,128]{4,3,2,1,0:T(8,128)(2,1)S(1)}, u32[]{:S(2)}, u32[]{:S(2)}) collective-permute-start(bf16[3,2,4,64,128]{4,3,2,1,0:T(8,128)(2,1)S(1)} %pad_maximum_fusion.1.rest_0_), channel_id=1, source_target_pairs={{0,1},{2,3},{4,5},{6,7},{8,9},{10,11},{12,13},{14,15},{16,17},{18,... | collective-permute-start | bytes 1179656 | tf_op jit(solution)/shard_map/ppermute | solution.py:580
  77.5 0.0 copy-done.7
  77.5 0.0 copy-done.8
  77.5 0.9 shard_map.150
  78.4 16.2 %all_to_all.47 = f32[64,1,128]{2,1,0:T(1,128)S(1)} all-to-all(f32[64,1,128]{2,1,0:T(1,128)S(1)} %bitcast.44), channel_id=1, replica_groups=mesh['scene'=8,'space'=64] {'space'}, dimensions={0} | all-to-all | bytes 65536 | tf_op jit(solution)/shard_map/all_to_all | solution.py:585
  94.6 0.0 collective-permute-done.7.rest_2_
  94.6 0.0 collective-permute-done.6.rest_1_
  94.6 0.0 copy-done
  94.6 0.0 copy-done.1
  94.6 0.0 copy-done.2
  94.7 0.0 copy-done.3
  94.7 0.0 copy-done.5
  94.7 0.0 copy-done.6
  94.7 6.8 %shard_map.151 = (bf16[4,64,128]{2,1,0:T(8,128)(2,1)}, f32[4,64,128]{2,1,0:T(8,128)S(1)}, f32[32,120,128]{2,1,0:T(8,128)S(1)}, bf16[32,120,128]{2,1,0:T(8,128)(2,1)S(1)}) custom-call(bf16[4,64,128]{2,1,0:T(8,128)(2,1)S(1)} %bitcast.32, bf16[4,64,128]{2,1,0:T(8,128)(2,1)S(1)} %bitcast.35, s32[1,4]{1,0:T(1,128)S(1)} %copy-done.4, ...), custom_call_target="tpu_custom_call" | custom-call | tf_op jit(solution)/shard_map/pallas_call | solution.py:552
  101.5 1.9 %collective-permute-start.8 = (bf16[32,120,128]{2,1,0:T(8,128)(2,1)S(1)}, bf16[32,120,128]{2,1,0:T(8,128)(2,1)S(1)}, u32[]{:S(2)}, u32[]{:S(2)}) collective-permute-start(bf16[32,120,128]{2,1,0:T(8,128)(2,1)S(1)} %get-tuple-element.39), channel_id=1, source_target_pairs={{0,1},{2,3},{4,5},{6,7},{8,9},{10,11},{12,13},{14,15},{16,17},{18,... | collective-permute-start | bytes 2949128 | tf_op jit(solution)/shard_map/ppermute | solution.py:677
  103.4 2.5 %collective-permute-done.8.other = bf16[32,120,128]{2,1,0:T(8,128)(2,1)S(1)} collective-permute-done((bf16[32,120,128]{2,1,0:T(8,128)(2,1)S(1)}, bf16[32,120,128]{2,1,0:T(8,128)(2,1)S(1)}, u32[]{:S(2)}, u32[]{:S(2)}) %collective-permute-start.8) | collective-permute-done | bytes 983072 | tf_op jit(solution)/shard_map/ppermute | solution.py:677
  105.9 0.3 shard_map.152
  106.2 31.5 %all_to_all.48.parts = bf16[32,120,128]{2,1,0:T(8,128)(2,1)S(1)} all-to-all(bf16[32,120,128]{2,1,0:T(8,128)(2,1)S(1)} %shard_map.152), channel_id=1, replica_groups={{0,2,4,6,8,10,12,14,16,18,20,22,24,26,28,30,32,34,36,38,40,42,44,46,48,..., dimensions={0} | all-to-all | bytes 1966080 | tf_op jit(solution)/shard_map/all_to_all | solution.py:685
  137.7 1.5 shard_map.153
  139.1 22.9 %all_to_all.49 = f32[8,112,128]{2,1,0:T(8,128)S(1)} all-to-all(f32[8,112,128]{2,1,0:T(8,128)S(1)} %get-tuple-element.41), channel_id=1, replica_groups=mesh['scene'=8,'space'=64] {'scene'}, dimensions={0} | all-to-all | bytes 917504 | tf_op jit(solution)/shard_map/all_to_all | solution.py:694
  162.1 0.6 fusion
  (4 shorter events, 0.1 us)
Async XLA Ops:
  1.8 49.1 %copy-start.4 = (s32[1,4]{1,0:T(1,128)S(1)}, s32[1,4]{1,0:T(1,128)}, u32[]{:S(2)}) copy-start(s32[1,4]{1,0:T(1,128)} %active.7) | copy-start | bytes 52
  1.8 29.0 %collective-permute-start.1 = (bf16[2,4,64,128]{3,2,1,0:T(8,128)(2,1)S(1)}, bf16[2,4,64,128]{3,2,1,0:T(8,128)(2,1)S(1)}, u32[]{:S(2)}, u32[]{:S(2)}) collective-permute-start(bf16[2,4,64,128]{3,2,1,0:T(8,128)(2,1)S(1)} %get-tuple-element.23), channel_id=1, source_target_pairs={{4,8},{5,9},{6,10},{7,11},{12,16},{13,17},{14,18},{15,19},{20,24},... | collective-permute-start | bytes 393224 | tf_op jit(solution)/shard_map/ppermute | solution.py:576
  14.0 16.8 %collective-permute-start = (bf16[2,4,64,128]{3,2,1,0:T(8,128)(2,1)S(1)}, bf16[2,4,64,128]{3,2,1,0:T(8,128)(2,1)S(1)}, u32[]{:S(2)}, u32[]{:S(2)}) collective-permute-start(bf16[2,4,64,128]{3,2,1,0:T(8,128)(2,1)S(1)} %get-tuple-element.23), channel_id=1, source_target_pairs={{0,4},{1,5},{2,6},{3,7},{8,12},{9,13},{10,14},{11,15},{16,20},{17,... | collective-permute-start | bytes 393224 | tf_op jit(solution)/shard_map/ppermute | solution.py:576
  30.8 9.1 %collective-permute-start.3 = (bf16[3,2,4,64,128]{4,3,2,1,0:T(8,128)(2,1)S(1)}, bf16[3,2,4,64,128]{4,3,2,1,0:T(8,128)(2,1)S(1)}, u32[]{:S(2)}, u32[]{:S(2)}) collective-permute-start(bf16[3,2,4,64,128]{4,3,2,1,0:T(8,128)(2,1)S(1)} %pad_maximum_fusion.rest_0_), channel_id=1, source_target_pairs={{1,2},{3,4},{5,6},{7,8},{9,10},{11,12},{13,14},{15,16},{17,18},{19... | collective-permute-start | bytes 1179656 | tf_op jit(solution)/shard_map/ppermute | solution.py:580
  33.6 6.3 %collective-permute-start.2 = (bf16[3,2,4,64,128]{4,3,2,1,0:T(8,128)(2,1)S(1)}, bf16[3,2,4,64,128]{4,3,2,1,0:T(8,128)(2,1)S(1)}, u32[]{:S(2)}, u32[]{:S(2)}) collective-permute-start(bf16[3,2,4,64,128]{4,3,2,1,0:T(8,128)(2,1)S(1)} %pad_maximum_fusion.rest_0_), channel_id=1, source_target_pairs={{0,1},{2,3},{4,5},{6,7},{8,9},{10,11},{12,13},{14,15},{16,17},{18,... | collective-permute-start | bytes 1179656 | tf_op jit(solution)/shard_map/ppermute | solution.py:580
  39.9 37.6 %copy-start.7 = (f32[128]{0:T(128)S(1)}, f32[128]{0:T(128)}, u32[]{:S(2)}) copy-start(f32[128]{0:T(128)} %param.21) | copy-start | bytes 1540
  39.9 37.6 %copy-start.8 = (f32[128]{0:T(128)S(1)}, f32[128]{0:T(128)}, u32[]{:S(2)}) copy-start(f32[128]{0:T(128)} %param.22) | copy-start | bytes 1540
  39.9 54.7 %copy-start = (bf16[27,128,128]{2,1,0:T(8,128)(2,1)S(1)}, bf16[27,128,128]{2,1,0:T(8,128)(2,1)}, u32[]{:S(2)}) copy-start(bf16[27,128,128]{2,1,0:T(8,128)(2,1)} %w1.1) | copy-start | bytes 2654212
  39.9 54.7 %copy-start.1 = (bf16[27,128,128]{2,1,0:T(8,128)(2,1)S(1)}, bf16[27,128,128]{2,1,0:T(8,128)(2,1)}, u32[]{:S(2)}) copy-start(bf16[27,128,128]{2,1,0:T(8,128)(2,1)} %w2.1) | copy-start | bytes 2654212
  39.9 54.7 %copy-start.2 = (bf16[1,4,64,128]{3,2,1,0:T(8,128)(2,1)S(1)}, bf16[1,4,64,128]{3,2,1,0:T(8,128)(2,1)}, u32[]{:S(2)}) copy-start(bf16[1,4,64,128]{3,2,1,0:T(8,128)(2,1)} %param.12) | copy-start | bytes 196612
  40.0 54.7 %copy-start.3 = (bf16[1,4,64,128]{3,2,1,0:T(8,128)(2,1)S(1)}, bf16[1,4,64,128]{3,2,1,0:T(8,128)(2,1)}, u32[]{:S(2)}) copy-start(bf16[1,4,64,128]{3,2,1,0:T(8,128)(2,1)} %param.23) | copy-start | bytes 196612
  40.0 54.7 %copy-start.5 = (f32[128]{0:T(128)S(1)}, f32[128]{0:T(128)}, u32[]{:S(2)}) copy-start(f32[128]{0:T(128)} %param.19) | copy-start | bytes 1540
  40.0 54.7 %copy-start.6 = (f32[128]{0:T(128)S(1)}, f32[128]{0:T(128)}, u32[]{:S(2)}) copy-start(f32[128]{0:T(128)} %param.20) | copy-start | bytes 1540
  44.7 28.1 %collective-permute-start.5 = (bf16[2,4,64,128]{3,2,1,0:T(8,128)(2,1)S(1)}, bf16[2,4,64,128]{3,2,1,0:T(8,128)(2,1)S(1)}, u32[]{:S(2)}, u32[]{:S(2)}) collective-permute-start(bf16[2,4,64,128]{3,2,1,0:T(8,128)(2,1)S(1)} %get-tuple-element.31), channel_id=1, source_target_pairs={{4,8},{5,9},{6,10},{7,11},{12,16},{13,17},{14,18},{15,19},{20,24},... | collective-permute-start | bytes 393224 | tf_op jit(solution)/shard_map/ppermute | solution.py:576
  48.9 23.8 %collective-permute-start.4 = (bf16[2,4,64,128]{3,2,1,0:T(8,128)(2,1)S(1)}, bf16[2,4,64,128]{3,2,1,0:T(8,128)(2,1)S(1)}, u32[]{:S(2)}, u32[]{:S(2)}) collective-permute-start(bf16[2,4,64,128]{3,2,1,0:T(8,128)(2,1)S(1)} %get-tuple-element.31), channel_id=1, source_target_pairs={{0,4},{1,5},{2,6},{3,7},{8,12},{9,13},{10,14},{11,15},{16,20},{17,... | collective-permute-start | bytes 393224 | tf_op jit(solution)/shard_map/ppermute | solution.py:576
  72.8 21.8 %collective-permute-start.7 = (bf16[3,2,4,64,128]{4,3,2,1,0:T(8,128)(2,1)S(1)}, bf16[3,2,4,64,128]{4,3,2,1,0:T(8,128)(2,1)S(1)}, u32[]{:S(2)}, u32[]{:S(2)}) collective-permute-start(bf16[3,2,4,64,128]{4,3,2,1,0:T(8,128)(2,1)S(1)} %pad_maximum_fusion.1.rest_0_), channel_id=1, source_target_pairs={{1,2},{3,4},{5,6},{7,8},{9,10},{11,12},{13,14},{15,16},{17,18},{19... | collective-permute-start | bytes 1179656 | tf_op jit(solution)/shard_map/ppermute | solution.py:580
  75.5 19.1 %collective-permute-start.6 = (bf16[3,2,4,64,128]{4,3,2,1,0:T(8,128)(2,1)S(1)}, bf16[3,2,4,64,128]{4,3,2,1,0:T(8,128)(2,1)S(1)}, u32[]{:S(2)}, u32[]{:S(2)}) collective-permute-start(bf16[3,2,4,64,128]{4,3,2,1,0:T(8,128)(2,1)S(1)} %pad_maximum_fusion.1.rest_0_), channel_id=1, source_target_pairs={{0,1},{2,3},{4,5},{6,7},{8,9},{10,11},{12,13},{14,15},{16,17},{18,... | collective-permute-start | bytes 1179656 | tf_op jit(solution)/shard_map/ppermute | solution.py:580
  101.5 4.4 %collective-permute-start.8 = (bf16[32,120,128]{2,1,0:T(8,128)(2,1)S(1)}, bf16[32,120,128]{2,1,0:T(8,128)(2,1)S(1)}, u32[]{:S(2)}, u32[]{:S(2)}) collective-permute-start(bf16[32,120,128]{2,1,0:T(8,128)(2,1)S(1)} %get-tuple-element.39), channel_id=1, source_target_pairs={{0,1},{2,3},{4,5},{6,7},{8,9},{10,11},{12,13},{14,15},{16,17},{18,... | collective-permute-start | bytes 2949128 | tf_op jit(solution)/shard_map/ppermute | solution.py:677
